TPU v7x, 32 devices: a whole 2x2x4 slice. The times are simulated.
32 devices in a mesh: fs: 4 (over y, core), nodes: 8 (over z, x).
Axes of the slice: x: 2, y: 2, z: 4, core: 2. Of those that a mesh axis runs over, the one named last changes fastest.
Arguments:
- edge_latent: bfloat16 [16, 12288, 256], P('fs', 'nodes'), may hold values from -6 to 6
- node_latent: bfloat16 [16, 2048, 256], P('fs', 'nodes'), may hold values from -6 to 6
- edge_cot: bfloat16 [16, 12288, 256], P('fs', 'nodes'), may hold values from -6 to 6
- node_cot: bfloat16 [16, 2048, 256], P('fs', 'nodes'), may hold values from -6 to 6
- five_flag: int32 [2048], P('nodes'), may hold values 0 or 1
- senders: int32 [12288], P('nodes'), may hold values from 0 to 287, as said below
- send_rows: int32 [16, 16], P('nodes'), may hold values from 0 to 255, as said below
- kernels: float32 [1792, 256], P('fs')
- kernel_first: float32 [1792, 256], P('fs')
- kernel_second: float32 [1792, 256], P('fs')
- vectors: float32 [6, 256], replicated
- vector_first: float32 [6, 256], replicated
- vector_second: float32 [6, 256], replicated
- statistics: float32 [4, 256, 256], replicated, as said below
- bases: float32 [4, 256, 256], replicated
Outputs:
- edge_output: bfloat16 [16, 12288, 256], P('fs', 'nodes')
- node_output: bfloat16 [16, 2048, 256], P('fs', 'nodes')
- edge_grad: bfloat16 [16, 12288, 256], P('fs', 'nodes')
- node_grad: bfloat16 [16, 2048, 256], P('fs', 'nodes')
- kernel_new: float32 [1792, 256], P('fs')
- kernel_first_new: float32 [1792, 256], P('fs')
- kernel_second_new: float32 [1792, 256], P('fs')
- vector_new: float32 [6, 256], replicated
- vector_first_new: float32 [6, 256], replicated
- vector_second_new: float32 [6, 256], replicated
- statistics_new: float32 [4, 256, 256], replicated
- bases_new: float32 [4, 256, 256], replicated
- weights_half: bfloat16 [1792, 256], replicated
Inputs may be any that keep to these rules, and one draw needn't show every extreme that they name: `senders`: entries below 16 occur only on devices with a lower neighbour, entries from 272 on only on devices with an upper neighbour. `send_rows`: each row lists distinct nodes of its device; row 2 * d goes to device d - 1, row 2 * d + 1 to device d + 1. `statistics`: each matrix is symmetric.
All inputs are finite; a program needn't handle non-finite values. No bound on the sum of `five_flag` on one device may be relied on, other than what follows from the above.
Results may differ from a plain program's by a relative error of at most 0.0075.
Values may be sent and summed in bfloat16 or wider, within the bound.
A program may use at most 192 MiB of HBM per device.

v0:
```python
from functools import partial

import jax
import jax.numpy as jnp
from jax import lax
from jax.sharding import PartitionSpec as P

STEP = 5


NORM_EPS = 1e-05
BETA_ONE = 0.5
BETA_TWO = 0.5
RATE_MATRIX = 0.05
RATE_VECTOR = 0.2
DECAY_RATE = 0.01
ADAM_EPS = 1e-08
HIGH = lax.Precision.HIGHEST


def with_halo(block, sides, width):
    for axis, dim in sides:
        count = lax.axis_size(axis)
        forward = [(i, i + 1) for i in range(count - 1)]
        backward = [(target, source) for source, target in forward]
        low = lax.ppermute(
            lax.slice_in_dim(block, block.shape[dim] - width, None, axis=dim), axis, forward
        )
        high = lax.ppermute(lax.slice_in_dim(block, 0, width, axis=dim), axis, backward)
        block = jnp.concatenate([low, block, high], axis=dim)
    return block


def swish_slope(values):
    logistic = jax.nn.sigmoid(values)
    return logistic * (1.0 + values * (1.0 - logistic))


def norm_forward(values, gain, shift):
    centre = values - jnp.mean(values, -1, keepdims=True)
    scale_inv = lax.rsqrt(jnp.mean(centre * centre, -1, keepdims=True) + NORM_EPS)
    normed = centre * scale_inv
    return (normed * gain + shift, normed, scale_inv)


def norm_backward(upstream, normed, scale_inv, gain):
    scaled = upstream * gain
    return scale_inv * (
        scaled
        - jnp.mean(scaled, -1, keepdims=True)
        - normed * jnp.mean(scaled * normed, -1, keepdims=True)
    )


def rows_product(left, right):
    return lax.dot_general(
        left, right, (((0,), (0,)), ((), ())), preferred_element_type=jnp.float32
    )


def cols_product(left, right):
    return lax.dot_general(
        left, right, (((1,), (1,)), ((), ())), preferred_element_type=jnp.float32
    )


def on_device(
    edge_latent,
    node_latent,
    edge_cot,
    node_cot,
    five_flag,
    senders,
    send_rows,
    kernels,
    kernel_first,
    kernel_second,
    vectors,
    vector_first,
    vector_second,
    statistics,
    bases,
):
    sample_count = node_latent.shape[0]
    node_count = node_latent.shape[1]
    features = node_latent.shape[2]
    slot_count = senders.shape[0] // node_count
    halo_width = send_rows.shape[1]
    shard_rows = kernels.shape[0]
    local_half = kernels.astype(jnp.bfloat16)
    bias_edge, gain_edge, shift_edge = (vectors[0], vectors[1], vectors[2])
    bias_node, gain_node, shift_node = (vectors[3], vectors[4], vectors[5])
    slot_ids = lax.broadcasted_iota(jnp.int32, (node_count, slot_count), 1)
    live = (
        (slot_ids < slot_count - five_flag[:, None])
        .astype(jnp.float32)
        .reshape(node_count * slot_count, 1)
    )
    grad_first_edge = jnp.zeros((3 * features, features), jnp.float32)
    grad_second_edge = jnp.zeros((features, features), jnp.float32)
    grad_first_node = jnp.zeros((2 * features, features), jnp.float32)
    grad_second_node = jnp.zeros((features, features), jnp.float32)
    vector_rows = [jnp.zeros((features,), jnp.float32) for index_row in range(6)]
    edge_outs, node_outs, edge_grads, node_grads = ([], [], [], [])
    for sample in range(sample_count):
        stacked = lax.all_gather(local_half, "fs", axis=0, tiled=True)
        first_edge = stacked[: 3 * features]
        second_edge = stacked[3 * features : 4 * features]
        first_node = stacked[4 * features : 6 * features]
        second_node = stacked[6 * features :]
        node_now = node_latent[sample]
        edge_now = edge_latent[sample]
        packed = jnp.concatenate([node_now[send_rows[0]], node_now[send_rows[1]]], 0)
        border = with_halo(packed, (("nodes", 0),), halo_width)
        table = jnp.concatenate([border[:halo_width], node_now, border[3 * halo_width :]], 0)
        joined = jnp.concatenate(
            [edge_now, table[senders], jnp.repeat(node_now, slot_count, axis=0)], 1
        )
        pre_edge = jnp.dot(joined, first_edge, preferred_element_type=jnp.float32) + bias_edge
        act_edge = jax.nn.silu(pre_edge).astype(jnp.bfloat16)
        out_edge = jnp.dot(act_edge, second_edge, preferred_element_type=jnp.float32)
        edge_value, normed_edge, inv_edge = norm_forward(out_edge, gain_edge, shift_edge)
        update = edge_value * live
        edge_outs.append((edge_now.astype(jnp.float32) + update).astype(jnp.bfloat16))
        gathered = jnp.sum(update.reshape(node_count, slot_count, features), 1).astype(jnp.bfloat16)
        joined_node = jnp.concatenate([node_now, gathered], 1)
        pre_node = jnp.dot(joined_node, first_node, preferred_element_type=jnp.float32) + bias_node
        act_node = jax.nn.silu(pre_node).astype(jnp.bfloat16)
        out_node = jnp.dot(act_node, second_node, preferred_element_type=jnp.float32)
        node_value, normed_node, inv_node = norm_forward(out_node, gain_node, shift_node)
        node_outs.append((node_now.astype(jnp.float32) + node_value).astype(jnp.bfloat16))
        node_back = node_cot[sample].astype(jnp.float32)
        edge_back = edge_cot[sample].astype(jnp.float32)
        d_out_node = norm_backward(node_back, normed_node, inv_node, gain_node).astype(jnp.bfloat16)
        grad_second_node = grad_second_node + rows_product(act_node, d_out_node)
        d_pre_node = (cols_product(d_out_node, second_node) * swish_slope(pre_node)).astype(
            jnp.bfloat16
        )
        grad_first_node = grad_first_node + rows_product(joined_node, d_pre_node)
        vector_rows[3] = vector_rows[3] + jnp.sum(d_pre_node.astype(jnp.float32), 0)
        vector_rows[4] = vector_rows[4] + jnp.sum(node_back * normed_node, 0)
        vector_rows[5] = vector_rows[5] + jnp.sum(node_back, 0)
        d_joined_node = cols_product(d_pre_node, first_node)
        d_update = (edge_back + jnp.repeat(d_joined_node[:, features:], slot_count, axis=0)) * live
        vector_rows[1] = vector_rows[1] + jnp.sum(d_update * normed_edge, 0)
        vector_rows[2] = vector_rows[2] + jnp.sum(d_update, 0)
        d_out_edge = norm_backward(d_update, normed_edge, inv_edge, gain_edge).astype(jnp.bfloat16)
        grad_second_edge = grad_second_edge + rows_product(act_edge, d_out_edge)
        d_pre_edge = (cols_product(d_out_edge, second_edge) * swish_slope(pre_edge)).astype(
            jnp.bfloat16
        )
        grad_first_edge = grad_first_edge + rows_product(joined, d_pre_edge)
        vector_rows[0] = vector_rows[0] + jnp.sum(d_pre_edge.astype(jnp.float32), 0)
        d_joined = cols_product(d_pre_edge, first_edge)
        edge_grads.append((edge_back + d_joined[:, :features]).astype(jnp.bfloat16))
        node_total = node_back + d_joined_node[:, :features]
        node_total = node_total + jnp.sum(
            d_joined[:, 2 * features :].reshape(node_count, slot_count, features), 1
        )
        table_grad = (
            jnp.zeros((node_count + 2 * halo_width, features), jnp.float32)
            .at[senders]
            .add(d_joined[:, features : 2 * features])
        )
        node_total = node_total + table_grad[halo_width : halo_width + node_count]
        border_grad = jnp.concatenate(
            [table_grad[:halo_width], table_grad[halo_width + node_count :]], 0
        )
        returned = with_halo(border_grad.astype(jnp.bfloat16), (("nodes", 0),), halo_width).astype(
            border_grad.dtype
        )
        node_total = node_total.at[send_rows[0]].add(returned[:halo_width])
        node_total = node_total.at[send_rows[1]].add(returned[3 * halo_width :])
        node_grads.append(node_total.astype(jnp.bfloat16))
    grad_stack = jnp.concatenate(
        [grad_first_edge, grad_second_edge, grad_first_node, grad_second_node], 0
    )
    vector_part = jnp.stack(vector_rows)
    shard_grad = lax.psum_scatter(
        grad_stack.astype(jnp.bfloat16), "fs", scatter_dimension=0, tiled=True
    ).astype(jnp.float32)
    shard_grad, vector_part = lax.psum((shard_grad, vector_part), "nodes")
    rows_global = lax.axis_index("fs") * shard_rows + jnp.arange(shard_rows, dtype=jnp.int32)
    block_ids = (
        (rows_global >= 3 * features).astype(jnp.int32)
        + (rows_global >= 4 * features).astype(jnp.int32)
        + (rows_global >= 6 * features).astype(jnp.int32)
    )
    select = (block_ids[None, :] == jnp.arange(4, dtype=jnp.int32)[:, None]).astype(jnp.float32)
    masked = select[:, :, None] * shard_grad[None]
    stat_part = jnp.einsum("krd,re->kde", masked, shard_grad, precision=HIGH)
    stat_total, grad_vectors = (
        lax.psum(stat_part.astype(jnp.bfloat16), "fs").astype(jnp.float32),
        lax.psum(vector_part.astype(jnp.bfloat16), "fs").astype(jnp.float32),
    )
    correct = 1.0 - BETA_ONE**STEP
    correct_two = 1.0 - BETA_TWO**STEP
    rotated_all = jnp.einsum("rd,kde->kre", shard_grad, bases, precision=HIGH)
    rotated = jnp.sum(select[:, :, None] * rotated_all, 0)
    first_new = BETA_ONE * kernel_first + (1.0 - BETA_ONE) * rotated
    second_new = BETA_TWO * kernel_second + (1.0 - BETA_TWO) * rotated * rotated
    scaled_step = first_new / correct / (jnp.sqrt(second_new / correct_two) + ADAM_EPS)
    turned_all = jnp.einsum("re,kde->krd", scaled_step, bases, precision=HIGH)
    turned = jnp.sum(select[:, :, None] * turned_all, 0)
    kernel_new = kernels - RATE_MATRIX * (turned + DECAY_RATE * kernels)
    weights_half = lax.all_gather(kernel_new.astype(jnp.bfloat16), "fs", axis=0, tiled=True)
    vector_first_new = BETA_ONE * vector_first + (1.0 - BETA_ONE) * grad_vectors
    vector_second_new = BETA_TWO * vector_second + (1.0 - BETA_TWO) * grad_vectors * grad_vectors
    vector_new = vectors - RATE_VECTOR * (vector_first_new / correct) / (
        jnp.sqrt(vector_second_new / correct_two) + ADAM_EPS
    )
    stat_new = BETA_TWO * statistics + (1.0 - BETA_TWO) * stat_total
    projected = jnp.einsum("kij,kjl->kil", stat_new, bases, precision=HIGH)
    gram = jnp.einsum("kij,kil->kjl", projected, projected, precision=HIGH)
    factor = jnp.linalg.cholesky(gram)
    solved = jax.vmap(partial(jax.scipy.linalg.solve_triangular, lower=True))(
        factor, jnp.swapaxes(projected, 1, 2)
    )
    basis_new = jnp.swapaxes(solved, 1, 2)
    return (
        jnp.stack(edge_outs),
        jnp.stack(node_outs),
        jnp.stack(edge_grads),
        jnp.stack(node_grads),
        kernel_new,
        first_new,
        second_new,
        vector_new,
        vector_first_new,
        vector_second_new,
        stat_new,
        basis_new,
        weights_half,
    )


def solution(mesh):
    in_specs = (
        P("fs", "nodes", None),
        P("fs", "nodes", None),
        P("fs", "nodes", None),
        P("fs", "nodes", None),
        P("nodes"),
        P("nodes"),
        P("nodes", None),
        P("fs", None),
        P("fs", None),
        P("fs", None),
        P(),
        P(),
        P(),
        P(),
        P(),
    )
    out_specs = (
        P("fs", "nodes", None),
        P("fs", "nodes", None),
        P("fs", "nodes", None),
        P("fs", "nodes", None),
        P("fs", None),
        P("fs", None),
        P("fs", None),
        P(),
        P(),
        P(),
        P(),
        P(),
        P(),
    )
    return jax.shard_map(
        on_device, mesh=mesh, in_specs=in_specs, out_specs=out_specs, check_vma=False
    )
```

profile of v0, /device:TPU:0, one launch (start us, length us, event | category | flops | bytes accessed | tf_op | source)
XLA Modules:
  0.0 736.8 jit_solution(2118433959619693914)
XLA Ops:
  14.0 6.1 collective-permute-start
  24.0 5.4 collective-permute-start.2
  37.1 9.6 %all_gather.4 = bf16[1792,256]{1,0:T(8,128)(2,1)S(1)} all-gather(bf16[448,256]{1,0:T(8,128)(2,1)S(1)} %convert_element_type.331), channel_id=1, replica_groups=mesh['fs'=4,'nodes'=8] {'fs'}, dimensions={0}, use_global_device_ids=true | all-gather | bytes 1146880 | tf_op jit(solution)/shard_map/all_gather | solution.py:106
  46.7 3.6 slice_bitcast_fusion.3
  66.5 5.2 collective-permute-start.4
  72.8 5.0 collective-permute-start.6
  80.5 5.4 gather_fusion.11
  85.9 5.3 gather_fusion.5
  91.3 5.3 gather_fusion.8
  96.6 5.4 gather_fusion.2
  120.1 5.3 fusion.55
  125.4 2.8 reshape.677
  128.3 2.9 reduce_sum.602
  138.3 2.9 reduce_sum.611
  148.4 2.9 reduce_sum.608
  158.4 2.9 reduce_sum.605
  185.4 2.6 broadcast_in_dim.36
  207.1 2.6 reshape.684
  209.7 2.6 broadcast_in_dim.40
  212.4 5.9 fusion.48
  221.4 3.6 multiply_convert_fusion.2
  227.3 3.0 fusion.143
  230.3 10.0 %scatter_custom_fusion.9 = f32[288,256]{1,0:T(8,128)} fusion(s32[1536]{0:T(1024)} %copy-done.158, f32[1536,768]{1,0:T(8,128)} %fusion.143, f32[]{:T(128)} %constant.164.clone.1), kind=kCustom, calls=%fused_computation.78 | custom fusion | flops 393216 | bytes 1868288 | tf_op jit(solution)/shard_map/scatter-add | solution.py:163
  241.9 3.0 convert_reduce_fusion.2
  245.8 3.0 fusion.147
  248.8 10.0 %scatter_custom_fusion.3 = f32[288,256]{1,0:T(8,128)} fusion(s32[1536]{0:T(1024)} %copy-done.158, f32[1536,768]{1,0:T(8,128)} %fusion.147, f32[]{:T(128)} %constant.164.clone.1), kind=kCustom, calls=%fused_computation.82 | custom fusion | flops 393216 | bytes 1868288 | tf_op jit(solution)/shard_map/scatter-add | solution.py:163
  262.1 9.0 %fusion.269 = (f32[1536,256]{1,0:T(8,128)}, bf16[1,1536,256]{2,1,0:T(8,128)(2,1)}, f32[256]{0:T(256)}, f32[1536]{0:T(1024)S(1)}, f32[1536]{0:T(1024)S(1)}, /*index=5*/f32[256]{0:T(256)}) fusion(f32[1536,768]{1,0:T(8,128)} %fusion.147, bf16[4,1536,256]{2,1,0:T(8,128)(2,1)} %param.17, f32[1536]{0:T(1024)} %copy-done.139, ...), kind=kLoop, calls=%fused_computation.521 | loop fusion | flops 9040384 | bytes 14201856 | tf_op jit(solution)/shard_map/slice | solution.py:158
  271.2 4.0 fusion.271
  276.5 3.0 fusion.145
  279.5 9.4 %scatter_custom_fusion.6 = f32[288,256]{1,0:T(8,128)S(1)} fusion(s32[1536]{0:T(1024)} %copy-done.158, f32[1536,768]{1,0:T(8,128)} %fusion.145, f32[]{:T(128)} %constant.164.clone.1), kind=kCustom, calls=%fused_computation.80 | custom fusion | flops 393216 | bytes 1868288 | tf_op jit(solution)/shard_map/scatter-add | solution.py:163
  289.0 3.9 fusion.270
  298.0 3.0 fusion.149
  301.0 9.8 %scatter_custom_fusion = f32[288,256]{1,0:T(8,128)S(1)} fusion(s32[1536]{0:T(1024)} %copy-done.158, f32[1536,768]{1,0:T(8,128)} %fusion.149, f32[]{:T(128)} %constant.164.clone.1), kind=kCustom, calls=%fused_computation.84 | custom fusion | flops 393216 | bytes 1868288 | tf_op jit(solution)/shard_map/scatter-add | solution.py:163
  310.9 3.9 fusion.268
  323.5 4.5 collective-permute-start.14
  342.7 5.3 collective-permute-start.10
  359.1 5.4 collective-permute-start.12
  386.6 4.9 collective-permute-start.8
  403.3 45.5 %all-reduce.6 = (f32[448,256]{1,0:T(8,128)S(1)}, bf16[6,256]{1,0:T(8,128)(2,1)S(1)}) all-reduce(bf16[448,256]{1,0:T(8,128)(2,1)} %reduce-scatter.2.cloned.1.call-done, f32[6,256]{1,0:T(8,128)S(1)} %stack.89), channel_id=1, replica_groups=mesh['fs'=4,'nodes'=8] {'nodes'}, use_global_device_ids=true, to_apply=%region_53.54 | all-reduce | flops 116224 | bytes 697344 | tf_op jit(solution)/shard_map/psum | solution.py:182
  448.8 4.5 fusion.36
  458.2 11.2 %all_gather.10 = bf16[1792,256]{1,0:T(8,128)(2,1)} all-gather(bf16[448,256]{1,0:T(8,128)(2,1)S(1)} %get-tuple-element.123), channel_id=1, replica_groups=mesh['fs'=4,'nodes'=8] {'fs'}, dimensions={0}, use_global_device_ids=true | all-gather | bytes 1146880 | tf_op jit(solution)/shard_map/all_gather | solution.py:206
  469.4 7.3 psum.30
  477.3 8.7 %all-reduce.5.cloned.1.call-done = bf16[4,256,256]{2,1,0:T(8,128)(2,1)} async-done(((bf16[4,256,256]{2,1,0:T(8,128)(2,1)}), bf16[4,256,256]{2,1,0:T(8,128)(2,1)}) %all-reduce.5.cloned.1.call-update) | async-done | bytes 524304 | tf_op jit(solution)/shard_map/psum | solution.py:193
  493.9 47.1 %custom-call.17 = f32[4,128,128]{2,1,0:T(8,128)S(1)} custom-call(f32[4,128,128]{2,1,0:T(8,128)S(1)} %cholesky.122), custom_call_target="Cholesky" | custom-call | tf_op jit(solution)/shard_map/jit(cholesky)/cholesky | solution.py:215
  541.8 40.8 %custom-call.18 = f32[4,1,128,128]{2,3,1,0:T(8,128)} custom-call(f32[4,1,128,128]{3,2,1,0:T(8,128)} %select_bitcast_fusion), custom_call_target="InvertDiagBlocksLowerTriangular" | custom-call | tf_op jit(solution)/shard_map/jit(cholesky)/cholesky | solution.py:215
  586.4 48.4 %custom-call.19 = f32[4,128,128]{2,1,0:T(8,128)} custom-call(f32[4,128,128]{2,1,0:T(8,128)} %convolution_subtract_fusion.1), custom_call_target="Cholesky" | custom-call | tf_op jit(solution)/shard_map/jit(cholesky)/cholesky | solution.py:215
  638.2 5.5 while.1
  643.7 80.3 %custom-call.20 = f32[4,2,128,128]{2,3,1,0:T(8,128)} custom-call(f32[4,2,128,128]{3,2,1,0:T(8,128)} %bitcast.405), custom_call_target="InvertDiagBlocksLowerTriangular" | custom-call | tf_op jit(solution)/shard_map/vmap(jit(_solve_triangular))/triangular_solve | solution.py:216
  (747 shorter events, 237.1 us)
Async XLA Ops:
  7.2 446.2 %copy-start = (f32[4,256,256]{2,1,0:T(8,128)S(1)}, f32[4,256,256]{2,1,0:T(8,128)}, u32[]{:S(2)}) copy-start(f32[4,256,256]{2,1,0:T(8,128)} %param.29) | copy-start | bytes 3145732
  7.2 26.8 %copy-start.200 = (s32[256]{0:T(256)S(1)}, s32[256]{0:T(256)}, u32[]{:S(2)}) copy-start(s32[256]{0:T(256)} %param.19) | copy-start | bytes 3076
  7.2 27.4 %copy-start.159 = (f32[6,256]{1,0:T(8,128)S(1)}, f32[6,256]{1,0:T(8,128)}, u32[]{:S(2)}) copy-start(f32[6,256]{1,0:T(8,128)} %param.25) | copy-start | bytes 18436
  7.2 28.0 %copy-start.172 = (s32[1536]{0:T(1024)S(1)}, s32[1536]{0:T(1024)}, u32[]{:S(2)}) copy-start(s32[1536]{0:T(1024)} %param.20) | copy-start | bytes 18436
  7.2 29.3 %copy-start.60 = (f32[448,256]{1,0:T(8,128)S(1)}, f32[448,256]{1,0:T(8,128)}, u32[]{:S(2)}) copy-start(f32[448,256]{1,0:T(8,128)} %param.22) | copy-start | bytes 1376260
  7.2 396.0 %reduce-scatter.2.cloned.1.call-start = ((), (), s32[]{:S(2)}) async-start(), calls=%async_computation.1 | async-start | bytes 1146880 | tf_op jit(solution)/shard_map/reduce_scatter | solution.py:179
  8.1 28.5 %copy-start.114 = (bf16[4,256,256]{2,1,0:T(8,128)(2,1)S(1)}, bf16[4,256,256]{2,1,0:T(8,128)(2,1)}, u32[]{:S(2)}) copy-start(bf16[4,256,256]{2,1,0:T(8,128)(2,1)} %param.18) | copy-start | bytes 1572868
  10.0 26.8 %copy-start.62 = (bf16[256,256]{1,0:T(8,128)(2,1)}, bf16[256,256]{1,0:T(8,128)(2,1)S(1)}, u32[]{:S(2)}) copy-start(bf16[256,256]{1,0:T(8,128)(2,1)S(1)} %get-tuple-element.179) | copy-start | bytes 393220
  10.0 26.8 %copy-start.63 = (bf16[256,256]{1,0:T(8,128)(2,1)}, bf16[256,256]{1,0:T(8,128)(2,1)S(1)}, u32[]{:S(2)}) copy-start(bf16[256,256]{1,0:T(8,128)(2,1)S(1)} %get-tuple-element.180) | copy-start | bytes 393220
  10.0 41.7 %copy-start.64 = (bf16[256,256]{1,0:T(8,128)(2,1)}, bf16[256,256]{1,0:T(8,128)(2,1)S(1)}, u32[]{:S(2)}) copy-start(bf16[256,256]{1,0:T(8,128)(2,1)S(1)} %get-tuple-element.181) | copy-start | bytes 393220
  10.0 42.9 %copy-start.65 = (bf16[256,256]{1,0:T(8,128)(2,1)}, bf16[256,256]{1,0:T(8,128)(2,1)S(1)}, u32[]{:S(2)}) copy-start(bf16[256,256]{1,0:T(8,128)(2,1)S(1)} %get-tuple-element.182) | copy-start | bytes 393220
  11.4 53.8 %collective-permute-start.1 = (bf16[16,256]{0,1:T(8,128)(2,1)}, bf16[16,256]{0,1:T(8,128)(2,1)}, u32[]{:S(2)}, u32[]{:S(2)}) collective-permute-start(bf16[16,256]{0,1:T(8,128)(2,1)} %copy.203), channel_id=1, source_target_pairs={{1,0},{2,1},{3,2},{4,3},{5,4},{6,5},{7,6},{9,8},{10,9},{11,10},{12... | collective-permute-start | bytes 24584 | tf_op jit(solution)/shard_map/ppermute | solution.py:29
  14.0 52.5 %collective-permute-start = (bf16[16,256]{0,1:T(8,128)(2,1)}, bf16[16,256]{0,1:T(8,128)(2,1)}, u32[]{:S(2)}, u32[]{:S(2)}) collective-permute-start(bf16[16,256]{0,1:T(8,128)(2,1)} %copy.201), channel_id=1, source_target_pairs={{0,1},{1,2},{2,3},{3,4},{4,5},{5,6},{6,7},{8,9},{9,10},{10,11},{11... | collective-permute-start | bytes 24584 | tf_op jit(solution)/shard_map/ppermute | solution.py:26
  21.4 57.4 %collective-permute-start.3 = (bf16[16,256]{0,1:T(8,128)(2,1)}, bf16[16,256]{0,1:T(8,128)(2,1)}, u32[]{:S(2)}, u32[]{:S(2)}) collective-permute-start(bf16[16,256]{0,1:T(8,128)(2,1)} %copy.210), channel_id=1, source_target_pairs={{1,0},{2,1},{3,2},{4,3},{5,4},{6,5},{7,6},{9,8},{10,9},{11,10},{12... | collective-permute-start | bytes 24584 | tf_op jit(solution)/shard_map/ppermute | solution.py:29
  24.0 54.8 %collective-permute-start.2 = (bf16[16,256]{0,1:T(8,128)(2,1)}, bf16[16,256]{0,1:T(8,128)(2,1)}, u32[]{:S(2)}, u32[]{:S(2)}) collective-permute-start(bf16[16,256]{0,1:T(8,128)(2,1)} %copy.208), channel_id=1, source_target_pairs={{0,1},{1,2},{2,3},{3,4},{4,5},{5,6},{6,7},{8,9},{9,10},{10,11},{11... | collective-permute-start | bytes 24584 | tf_op jit(solution)/shard_map/ppermute | solution.py:26
  30.8 42.0 %collective-permute-start.5 = (bf16[16,256]{0,1:T(8,128)(2,1)}, bf16[16,256]{0,1:T(8,128)(2,1)}, u32[]{:S(2)}, u32[]{:S(2)}) collective-permute-start(bf16[16,256]{0,1:T(8,128)(2,1)} %copy.217), channel_id=1, source_target_pairs={{1,0},{2,1},{3,2},{4,3},{5,4},{6,5},{7,6},{9,8},{10,9},{11,10},{12... | collective-permute-start | bytes 24584 | tf_op jit(solution)/shard_map/ppermute | solution.py:29
  36.7 13.7 %copy-start.20 = (bf16[1,256,256]{1,2,0:T(8,128)(2,1)}, bf16[1,256,256]{1,2,0:T(8,128)(2,1)S(1)}, u32[]{:S(2)}) copy-start(bf16[1,256,256]{1,2,0:T(8,128)(2,1)S(1)} %copy.278) | copy-start | bytes 393220
  36.9 13.4 %copy-start.23 = (bf16[1,256,256]{1,2,0:T(8,128)(2,1)}, bf16[1,256,256]{1,2,0:T(8,128)(2,1)S(1)}, u32[]{:S(2)}) copy-start(bf16[1,256,256]{1,2,0:T(8,128)(2,1)S(1)} %copy.277) | copy-start | bytes 393220
  37.0 13.3 %copy-start.17 = (bf16[1,256,256]{1,2,0:T(8,128)(2,1)}, bf16[1,256,256]{1,2,0:T(8,128)(2,1)S(1)}, u32[]{:S(2)}) copy-start(bf16[1,256,256]{1,2,0:T(8,128)(2,1)S(1)} %copy.276) | copy-start | bytes 393220
  37.1 13.4 %copy-start.26 = (bf16[1,256,256]{1,2,0:T(8,128)(2,1)}, bf16[1,256,256]{1,2,0:T(8,128)(2,1)S(1)}, u32[]{:S(2)}) copy-start(bf16[1,256,256]{1,2,0:T(8,128)(2,1)S(1)} %copy.279) | copy-start | bytes 393220
  53.8 18.0 %copy-start.52 = (bf16[1,256,256]{1,2,0:T(8,128)(2,1)}, bf16[1,256,256]{1,2,0:T(8,128)(2,1)S(1)}, u32[]{:S(2)}) copy-start(bf16[1,256,256]{1,2,0:T(8,128)(2,1)S(1)} %copy.272) | copy-start | bytes 393220
  56.1 21.7 %copy-start.55 = (bf16[1,256,256]{1,2,0:T(8,128)(2,1)}, bf16[1,256,256]{1,2,0:T(8,128)(2,1)S(1)}, u32[]{:S(2)}) copy-start(bf16[1,256,256]{1,2,0:T(8,128)(2,1)S(1)} %copy.274) | copy-start | bytes 393220
  56.2 22.6 %copy-start.57 = (bf16[1,256,256]{1,2,0:T(8,128)(2,1)}, bf16[1,256,256]{1,2,0:T(8,128)(2,1)S(1)}, u32[]{:S(2)}) copy-start(bf16[1,256,256]{1,2,0:T(8,128)(2,1)S(1)} %copy.273) | copy-start | bytes 393220
  56.3 23.9 %copy-start.50 = (bf16[1,256,256]{1,2,0:T(8,128)(2,1)}, bf16[1,256,256]{1,2,0:T(8,128)(2,1)S(1)}, u32[]{:S(2)}) copy-start(bf16[1,256,256]{1,2,0:T(8,128)(2,1)S(1)} %copy.275) | copy-start | bytes 393220
  65.2 15.0 %collective-permute-start.7 = (bf16[16,256]{0,1:T(8,128)(2,1)}, bf16[16,256]{0,1:T(8,128)(2,1)S(1)}, u32[]{:S(2)}, u32[]{:S(2)}) collective-permute-start(bf16[16,256]{0,1:T(8,128)(2,1)} %copy.224), channel_id=1, source_target_pairs={{1,0},{2,1},{3,2},{4,3},{5,4},{6,5},{7,6},{9,8},{10,9},{11,10},{12... | collective-permute-start | bytes 24584 | tf_op jit(solution)/shard_map/ppermute | solution.py:29
  66.5 11.3 %collective-permute-start.4 = (bf16[16,256]{0,1:T(8,128)(2,1)}, bf16[16,256]{0,1:T(8,128)(2,1)S(1)}, u32[]{:S(2)}, u32[]{:S(2)}) collective-permute-start(bf16[16,256]{0,1:T(8,128)(2,1)} %copy.215), channel_id=1, source_target_pairs={{0,1},{1,2},{2,3},{3,4},{4,5},{5,6},{6,7},{8,9},{9,10},{10,11},{11... | collective-permute-start | bytes 24584 | tf_op jit(solution)/shard_map/ppermute | solution.py:26
  72.8 7.4 %collective-permute-start.6 = (bf16[16,256]{0,1:T(8,128)(2,1)}, bf16[16,256]{0,1:T(8,128)(2,1)S(1)}, u32[]{:S(2)}, u32[]{:S(2)}) collective-permute-start(bf16[16,256]{0,1:T(8,128)(2,1)} %copy.222), channel_id=1, source_target_pairs={{0,1},{1,2},{2,3},{3,4},{4,5},{5,6},{6,7},{8,9},{9,10},{10,11},{11... | collective-permute-start | bytes 24584 | tf_op jit(solution)/shard_map/ppermute | solution.py:26
  106.0 13.0 %copy-start.3 = (f32[1536,256]{1,0:T(8,128)}, f32[1536,256]{1,0:T(8,128)S(1)}, u32[]{:S(2)}) copy-start(f32[1536,256]{1,0:T(8,128)S(1)} %get-tuple-element.233) | copy-start | bytes 4718596
  106.5 12.5 %copy-start.137 = (f32[1536]{0:T(1024)}, f32[1536]{0:T(1024)S(1)}, u32[]{:S(2)}) copy-start(f32[1536]{0:T(1024)S(1)} %add_rsqrt_fusion.1) | copy-start | bytes 18436
  319.4 10.2 %copy-start.202 = (f32[256,256]{1,0:T(8,128)S(1)}, f32[256,256]{1,0:T(8,128)}, u32[]{:S(2)}) copy-start(f32[256,256]{1,0:T(8,128)} %fusion.291) | copy-start | bytes 786436
  323.5 61.7 %collective-permute-start.14 = (bf16[16,256]{1,0:T(8,128)(2,1)S(1)}, bf16[16,256]{1,0:T(8,128)(2,1)}, u32[]{:S(2)}, u32[]{:S(2)}) collective-permute-start(bf16[16,256]{1,0:T(8,128)(2,1)S(1)} %get-tuple-element.203), channel_id=1, source_target_pairs={{0,1},{1,2},{2,3},{3,4},{4,5},{5,6},{6,7},{8,9},{9,10},{10,11},{11... | collective-permute-start | bytes 24584 | tf_op jit(solution)/shard_map/ppermute | solution.py:26
  328.0 58.6 %collective-permute-start.15 = (bf16[16,256]{1,0:T(8,128)(2,1)S(1)}, bf16[16,256]{1,0:T(8,128)(2,1)}, u32[]{:S(2)}, u32[]{:S(2)}) collective-permute-start(bf16[16,256]{1,0:T(8,128)(2,1)S(1)} %get-tuple-element.204), channel_id=1, source_target_pairs={{1,0},{2,1},{3,2},{4,3},{5,4},{6,5},{7,6},{9,8},{10,9},{11,10},{12... | collective-permute-start | bytes 24584 | tf_op jit(solution)/shard_map/ppermute | solution.py:29
  340.4 145.6 %all-reduce.5.cloned.1.call-start = ((), (), s32[]{:S(2)}) async-start(), calls=%async_computation.2 | async-start | bytes 1048576 | tf_op jit(solution)/shard_map/psum | solution.py:193
  342.7 48.8 %collective-permute-start.10 = (bf16[16,256]{1,0:T(8,128)(2,1)}, bf16[16,256]{1,0:T(8,128)(2,1)}, u32[]{:S(2)}, u32[]{:S(2)}) collective-permute-start(bf16[16,256]{1,0:T(8,128)(2,1)} %get-tuple-element.199), channel_id=1, source_target_pairs={{0,1},{1,2},{2,3},{3,4},{4,5},{5,6},{6,7},{8,9},{9,10},{10,11},{11... | collective-permute-start | bytes 24584 | tf_op jit(solution)/shard_map/ppermute | solution.py:26
  347.9 48.5 %collective-permute-start.11 = (bf16[16,256]{1,0:T(8,128)(2,1)}, bf16[16,256]{1,0:T(8,128)(2,1)}, u32[]{:S(2)}, u32[]{:S(2)}) collective-permute-start(bf16[16,256]{1,0:T(8,128)(2,1)} %get-tuple-element.200), channel_id=1, source_target_pairs={{1,0},{2,1},{3,2},{4,3},{5,4},{6,5},{7,6},{9,8},{10,9},{11,10},{12... | collective-permute-start | bytes 24584 | tf_op jit(solution)/shard_map/ppermute | solution.py:29
  359.1 39.4 %collective-permute-start.12 = (bf16[16,256]{1,0:T(8,128)(2,1)}, bf16[16,256]{1,0:T(8,128)(2,1)}, u32[]{:S(2)}, u32[]{:S(2)}) collective-permute-start(bf16[16,256]{1,0:T(8,128)(2,1)} %get-tuple-element.201), channel_id=1, source_target_pairs={{0,1},{1,2},{2,3},{3,4},{4,5},{5,6},{6,7},{8,9},{9,10},{10,11},{11... | collective-permute-start | bytes 24584 | tf_op jit(solution)/shard_map/ppermute | solution.py:26
  385.2 13.3 %collective-permute-start.13 = (bf16[16,256]{1,0:T(8,128)(2,1)S(1)}, bf16[16,256]{1,0:T(8,128)(2,1)S(1)}, u32[]{:S(2)}, u32[]{:S(2)}) collective-permute-start(bf16[16,256]{1,0:T(8,128)(2,1)S(1)} %copy-done.151), channel_id=1, source_target_pairs={{1,0},{2,1},{3,2},{4,3},{5,4},{6,5},{7,6},{9,8},{10,9},{11,10},{12... | collective-permute-start | bytes 24584 | tf_op jit(solution)/shard_map/ppermute | solution.py:29
  386.6 13.8 %collective-permute-start.8 = (bf16[16,256]{1,0:T(8,128)(2,1)S(1)}, bf16[16,256]{1,0:T(8,128)(2,1)S(1)}, u32[]{:S(2)}, u32[]{:S(2)}) collective-permute-start(bf16[16,256]{1,0:T(8,128)(2,1)S(1)} %copy-done.149), channel_id=1, source_target_pairs={{0,1},{1,2},{2,3},{3,4},{4,5},{5,6},{6,7},{8,9},{9,10},{10,11},{11... | collective-permute-start | bytes 24584 | tf_op jit(solution)/shard_map/ppermute | solution.py:26
  391.5 8.9 %collective-permute-start.9 = (bf16[16,256]{1,0:T(8,128)(2,1)S(1)}, bf16[16,256]{1,0:T(8,128)(2,1)S(1)}, u32[]{:S(2)}, u32[]{:S(2)}) collective-permute-start(bf16[16,256]{1,0:T(8,128)(2,1)S(1)} %copy-done.150), channel_id=1, source_target_pairs={{1,0},{2,1},{3,2},{4,3},{5,4},{6,5},{7,6},{9,8},{10,9},{11,10},{12... | collective-permute-start | bytes 24584 | tf_op jit(solution)/shard_map/ppermute | solution.py:29
  401.4 47.5 %copy-start.157 = (f32[4,448]{1,0:T(4,128)S(1)}, f32[4,448]{1,0:T(4,128)}, u32[]{:S(2)}) copy-start(f32[4,448]{1,0:T(4,128)} %fusion.240) | copy-start | bytes 21508
  457.3 19.4 %copy-start.160 = (f32[6,256]{1,0:T(8,128)S(1)}, f32[6,256]{1,0:T(8,128)}, u32[]{:S(2)}) copy-start(f32[6,256]{1,0:T(8,128)} %param.25) | copy-start | bytes 18436
  457.3 19.4 %copy-start.173 = (f32[6,256]{1,0:T(8,128)S(1)}, f32[6,256]{1,0:T(8,128)}, u32[]{:S(2)}) copy-start(f32[6,256]{1,0:T(8,128)} %param.26) | copy-start | bytes 18436
  457.3 19.4 %copy-start.174 = (f32[6,256]{1,0:T(8,128)S(1)}, f32[6,256]{1,0:T(8,128)}, u32[]{:S(2)}) copy-start(f32[6,256]{1,0:T(8,128)} %param.27) | copy-start | bytes 18436
  457.3 28.7 %copy-start.66 = (f32[4,256,256]{2,1,0:T(8,128)S(1)}, f32[4,256,256]{2,1,0:T(8,128)}, u32[]{:S(2)}) copy-start(f32[4,256,256]{2,1,0:T(8,128)} %param.28) | copy-start | bytes 3145732
  493.9 47.2 %copy-start.153 = (pred[128,128]{1,0:T(8,128)(4,1)S(1)}, pred[128,128]{1,0:T(8,128)(4,1)}, u32[]{:S(2)}) copy-start(pred[128,128]{1,0:T(8,128)(4,1)} %iota_compare_fusion.2) | copy-start | bytes 49156
  541.1 93.6 %copy-start.152 = (pred[128,128]{1,0:T(8,128)(4,1)S(1)}, pred[128,128]{1,0:T(8,128)(4,1)}, u32[]{:S(2)}) copy-start(pred[128,128]{1,0:T(8,128)(4,1)} %iota_compare_fusion.3) | copy-start | bytes 49156
  541.8 94.9 %copy-start.130 = (pred[256,256]{1,0:T(8,128)(4,1)S(1)}, pred[256,256]{1,0:T(8,128)(4,1)}, u32[]{:S(2)}) copy-start(pred[256,256]{1,0:T(8,128)(4,1)} %iota_compare_fusion) | copy-start | bytes 196612
  586.4 51.8 %copy-start.201 = (s32[2]{0:T(128)S(1)}, s32[2]{0:T(128)}, u32[]{:S(2)}) copy-start(s32[2]{0:T(128)} %iota_multiply_fusion) | copy-start | bytes 28
  (198 other events, 638.6 us)
Sparse Core Ops, SparseCore 0:
  340.6 26.0 reduce-scatter.1
  455.2 30.7 all-reduce.4
where the time goes:
time: 744 us; the launch traced here: 737 us
  other arithmetic  361 us (49%)
  local copies, waits for them, and re-layouts  154 us (21%)
  blocking collectives  73.6 us (10%)
  matrix products  70 us (9%)
  starting transfers between devices  52.5 us (7%)
  between operations  17.4 us (2%)
  waiting for transfers between devices  8.8 us (1%)
    another operation x10, other arithmetic, on_device(): factor = jnp.linalg.cholesky(gram)  139 us
    another operation x4, other arithmetic, on_device(): jax.vmap(partial(jax.scipy.linalg.solve_triangular, lower=True))  82.9 us
    psum x1, blocking collectives, on_device(): shard_grad, vector_part = lax.psum((shard_grad, vector_part), 'nodes')  45.5 us
    ppermute x8, starting transfers between devices, with_halo(): lax.ppermute(lax.slice_in_dim(block, block.shape[dim] - width, None, axis...  41.8 us
    scatter-add x4, other arithmetic, on_device(): table_grad = jnp.zeros((node_count + 2 * halo_width, features), jnp.float...  39.3 us
    unnamed x467, local copies, waits for them, and re-layouts  34.9 us
    dot_general x16, matrix products, cols_product(): lax.dot_general(left, right, (((1,), (1,)), ((), ())), preferred_element_...  25.1 us
    gather x4, local copies, waits for them, and re-layouts, on_device(): table[senders]  21.4 us
  transfers between devices with their start and end apart: 18, of which 1 were waited for; matrix products, arithmetic and copies ran while one was open for 11% of the time, Pallas kernels for 0%

commit v1 on v0

v1 whole, which is shorter than its diff:
```python
from functools import partial

import jax
import jax.numpy as jnp
from jax import lax
from jax.experimental import pallas as pl
from jax.experimental.pallas import tpu as pltpu
from jax.sharding import PartitionSpec as P

STEP = 5

NORM_EPS = 1e-05
BETA_ONE = 0.5
BETA_TWO = 0.5
RATE_MATRIX = 0.05
RATE_VECTOR = 0.2
DECAY_RATE = 0.01
ADAM_EPS = 1e-08
HIGH = lax.Precision.HIGHEST
F32 = jnp.float32
BF16 = jnp.bfloat16
LANES = 128
VMEM_LIMIT = 56 * 1024 * 1024


def dot_nn(left, right):
    return lax.dot_general(left, right, (((1,), (0,)), ((), ())), preferred_element_type=F32)


def dot_nt(left, right):
    return lax.dot_general(left, right, (((1,), (1,)), ((), ())), preferred_element_type=F32)


def dot_tn(left, right):
    return lax.dot_general(left, right, (((0,), (0,)), ((), ())), preferred_element_type=F32)


def split(value):
    high = value.astype(BF16)
    return high, (value - high.astype(F32)).astype(BF16)


def iota(shape, dim):
    return lax.broadcasted_iota(jnp.int32, shape, dim)


def ones_where(mask):
    return jnp.where(mask, 1.0, 0.0).astype(BF16)


def fold_rows(value):
    rows, width = value.shape
    return jnp.sum(value.reshape(rows // 8, 8, width), 0)


def aligned(index, step):
    return pl.ds(pl.multiple_of(index * step, step), step)


class Sizes:
    def __init__(self, samples, nodes, slots, halo, width):
        self.samples, self.nodes, self.slots = samples, nodes, slots
        self.halo, self.width = halo, width
        self.edges = nodes * slots
        self.fwd_nodes, self.bwd_nodes = 64, 128
        self.fwd_rows = self.fwd_nodes * slots
        self.bwd_rows = self.bwd_nodes * slots
        self.fwd_chunks = nodes // self.fwd_nodes
        self.bwd_chunks = nodes // self.bwd_nodes


def main_scratch(z):
    rows, width = z.samples * z.edges, z.width
    per_node = z.samples * z.nodes
    per_halo = z.samples * 2 * z.halo
    return dict(
        edge_v=pltpu.VMEM((rows, width), BF16),
        cot_v=pltpu.VMEM((rows, width), BF16),
        eout_v=pltpu.VMEM((rows, width), BF16),
        egrad_v=pltpu.VMEM((rows, width), BF16),
        act_v=pltpu.VMEM((rows, width), BF16),
        slope_v=pltpu.VMEM((rows, width), F32),
        norm_v=pltpu.VMEM((rows, width), BF16),
        inv_v=pltpu.VMEM((rows, LANES), F32),
        own_v=pltpu.VMEM((z.edges, z.nodes), BF16),
        own_t=pltpu.VMEM((z.nodes, z.edges), BF16),
        halo_t=pltpu.VMEM((2 * z.halo, z.edges), BF16),
        sel_v=pltpu.VMEM((z.edges, 2 * LANES), BF16),
        rep_v=pltpu.VMEM((z.bwd_rows, 2 * LANES), BF16),
        rep_t=pltpu.VMEM((LANES, z.bwd_rows), BF16),
        live_v=pltpu.VMEM((z.edges, LANES), F32),
        half_v=pltpu.VMEM((7 * width, width), BF16),
        pown_v=pltpu.VMEM((z.samples * 2 * z.nodes, width), BF16),
        psel_v=pltpu.VMEM((z.samples * z.fwd_chunks * 2 * LANES, width), BF16),
        gath_v=pltpu.VMEM((per_node, width), BF16),
        drep_v=pltpu.VMEM((z.samples * z.bwd_chunks * 2 * LANES, width), BF16),
        recv_v=pltpu.VMEM((per_node, width), F32),
        aown_v=pltpu.VMEM((per_node, width), F32),
        ahalo_v=pltpu.VMEM((per_halo, width), F32),
        table_v=pltpu.VMEM((per_halo, width), BF16),
        gmat_v=pltpu.VMEM((7 * width, width), F32),
        vsum_v=pltpu.VMEM((6 * 8, width), F32),
        edge_sem=pltpu.SemaphoreType.DMA((z.samples,)),
        cot_sem=pltpu.SemaphoreType.DMA((z.samples,)),
        eout_sem=pltpu.SemaphoreType.DMA((z.samples,)),
        egrad_sem=pltpu.SemaphoreType.DMA((z.samples,)),
    )


def build_selectors(z, m, five_ref, send_ref):
    halo, nodes, slots = z.halo, z.nodes, z.slots
    lane = iota((LANES, LANES), 1)
    row = iota((LANES, LANES), 0)
    for g in range(z.edges // LANES):
        rows = slice(g * LANES, (g + 1) * LANES)
        line = jnp.broadcast_to(send_ref[:, rows].astype(F32), (LANES, LANES))
        column = line.T.astype(jnp.int32)
        for h in range(nodes // LANES):
            m.own_v[rows, h * LANES : (h + 1) * LANES] = ones_where(column == lane + (halo + h * LANES))
        place = jnp.where(column < halo, column, jnp.where(column >= halo + nodes, column - nodes, -1))
        in_halo = (place == (lane & (2 * halo - 1))) & (lane < 4 * halo)
        first = slots * (lane & (z.fwd_nodes - 1))
        local = row + (g * LANES) % z.fwd_rows
        m.sel_v[rows, 0:LANES] = ones_where((first <= local) & (local < first + slots))
        m.sel_v[rows, LANES : 2 * LANES] = ones_where(in_halo)
    senders = jnp.broadcast_to(send_ref[...], (8, z.edges))
    for i in range(nodes // 16):
        node = iota((16, z.edges), 0) + (halo + i * 16)
        m.own_t[i * 16 : (i + 1) * 16, :] = ones_where(jnp.broadcast_to(senders[0:1], (16, z.edges)) == node)
    wide = jnp.broadcast_to(senders[0:1], (2 * halo, z.edges))
    node = iota((2 * halo, z.edges), 0)
    node = jnp.where(node < halo, node, node + nodes)
    m.halo_t[...] = ones_where(wide == node)
    first = slots * (iota((z.bwd_rows, 2 * LANES), 1) & (LANES - 1))
    local = iota((z.bwd_rows, 2 * LANES), 0)
    rep = ones_where((first <= local) & (local < first + slots))
    m.rep_v[...] = rep
    first = slots * iota((LANES, z.bwd_rows), 0)
    local = iota((LANES, z.bwd_rows), 1)
    m.rep_t[...] = ones_where((first <= local) & (local < first + slots))
    local = iota((z.bwd_rows, LANES), 0).astype(F32)
    slot = local - slots * jnp.floor((local + 0.5) * (1.0 / slots))
    for h in range(nodes // LANES):
        five = jnp.broadcast_to(five_ref[:, h * LANES : (h + 1) * LANES].astype(F32), (LANES, LANES)).T
        spread = dot_nn(rep[:, :LANES], five.astype(BF16))
        m.live_v[h * z.bwd_rows : (h + 1) * z.bwd_rows, :] = jnp.where(slot < slots - spread, 1.0, 0.0)


def both(column):
    return jnp.concatenate([column, column], 1)


def row_mean(value):
    return jnp.sum(value, -1, keepdims=True) * (1.0 / value.shape[-1])


def centred(value):
    centre = value - row_mean(value)
    return centre, lax.rsqrt(row_mean(centre * centre) + NORM_EPS)


def act_and_slope(half):
    turn = jnp.tanh(half)
    above = 1.0 + turn
    act = half * above
    return act, above + act * (1.0 - turn)


def main_kernel(
    z, names, edge_ref, cot_ref, node_ref, ncot_ref, five_ref, send_ref, weight_ref, halo_ref, vec_ref,
    eout_ref, egrad_ref, nout_ref, ntot_ref, border_ref, grad_ref, gvec_ref, *scratch,
):
    m = type("Held", (), {})()
    for name, ref in zip(names, scratch, strict=True):
        setattr(m, name, ref)
    width, nodes, edges, samples, halo = z.width, z.nodes, z.edges, z.samples, z.halo
    two_halo = 2 * halo

    def sample_copy(source, target, sem, s):
        rows = aligned(s, edges)
        return pltpu.make_async_copy(source.at[rows], target.at[rows], sem.at[s])

    for s in range(samples):
        sample_copy(edge_ref, m.edge_v, m.edge_sem, s).start()
    for s in range(samples):
        sample_copy(cot_ref, m.cot_v, m.cot_sem, s).start()

    build_selectors(z, m, five_ref, send_ref)
    m.half_v[...] = weight_ref[...] * jnp.asarray(0.5, BF16)
    m.gmat_v[...] = jnp.zeros_like(m.gmat_v)
    m.vsum_v[...] = jnp.zeros_like(m.vsum_v)
    m.aown_v[...] = jnp.zeros_like(m.aown_v)
    m.ahalo_v[...] = jnp.zeros_like(m.ahalo_v)
    for s in range(samples):
        for side in range(2):
            m.table_v[s * two_halo + side * halo : s * two_halo + (side + 1) * halo, :] = halo_ref[
                side, s * halo : (s + 1) * halo, :
            ]

    send_half = m.half_v[width : 2 * width, :]
    recv_half = m.half_v[2 * width : 3 * width, :]
    bias_edge, gain_edge, shift_edge = vec_ref[0:1, :] * 0.5, vec_ref[1:2, :], vec_ref[2:3, :]
    bias_node, gain_node, shift_node = vec_ref[3:4, :] * 0.5, vec_ref[4:5, :], vec_ref[5:6, :]

    for s in range(samples):
        node = node_ref[s * nodes : (s + 1) * nodes, :]
        high, low = split(dot_nn(node, send_half))
        m.pown_v[s * 2 * nodes : (s * 2 + 1) * nodes, :] = high
        m.pown_v[(s * 2 + 1) * nodes : (s * 2 + 2) * nodes, :] = low
        high, low = split(dot_nn(node, recv_half) + bias_edge)
        out_high, out_low = split(dot_nn(m.table_v[s * two_halo : (s + 1) * two_halo, :], send_half))
        zero = jnp.zeros((2 * LANES - 2 * z.fwd_nodes - 2 * two_halo, width), BF16)
        for c in range(z.fwd_chunks):
            own = slice(c * z.fwd_nodes, (c + 1) * z.fwd_nodes)
            base = (s * z.fwd_chunks + c) * 2 * LANES
            m.psel_v[base : base + 2 * LANES, :] = jnp.concatenate(
                [high[own], low[own], out_high, out_low, zero], 0
            )

    def forward(i, carry):
        s, c = i // z.fwd_chunks, i % z.fwd_chunks
        rows, local = aligned(i, z.fwd_rows), aligned(c, z.fwd_rows)

        @pl.when(c == 0)
        def _():
            sample_copy(edge_ref, m.edge_v, m.edge_sem, s).wait()

        edge = m.edge_v[rows, :]
        own = m.own_v[local, :]
        left = jnp.concatenate([edge, own, own, m.sel_v[local, :]], 1)
        right = jnp.concatenate(
            [m.half_v[0:width, :], m.pown_v[aligned(s, 2 * nodes), :], m.psel_v[aligned(i, 2 * LANES), :]], 0
        )
        act, slope = act_and_slope(dot_nn(left, right))
        act = act.astype(BF16)
        m.act_v[rows, :] = act
        m.slope_v[rows, :] = slope
        centre, inv = centred(dot_nn(act, weight_ref[3 * width : 4 * width, :]))
        live = m.live_v[local, :]
        inv = inv * live
        m.inv_v[rows, :] = inv
        normed = centre * both(inv)
        m.norm_v[rows, :] = normed.astype(BF16)
        update = normed * gain_edge + both(live) * shift_edge
        m.eout_v[rows, :] = (edge.astype(F32) + update).astype(BF16)
        gathered = dot_nn(m.rep_t[0 : z.fwd_nodes, 0 : z.fwd_rows], update.astype(BF16))
        m.gath_v[aligned(i, z.fwd_nodes), :] = gathered.astype(BF16)

        @pl.when(c == z.fwd_chunks - 1)
        def _():
            sample_copy(m.eout_v, eout_ref, m.eout_sem, s).start()

        return carry

    lax.fori_loop(0, samples * z.fwd_chunks, forward, 0)

    def node_part(i, carry):
        rows = aligned(i, 2 * nodes)
        node, gath = node_ref[rows, :], m.gath_v[rows, :]
        joined = jnp.concatenate([node, gath], 1)
        act, slope = act_and_slope(dot_nn(joined, m.half_v[4 * width : 6 * width, :]) + bias_node)
        act = act.astype(BF16)
        centre, inv = centred(dot_nn(act, weight_ref[6 * width : 7 * width, :]))
        normed = centre * inv
        nout_ref[rows, :] = (node.astype(F32) + normed * gain_node + shift_node).astype(BF16)
        back = ncot_ref[rows, :].astype(F32)
        back_normed = back * normed
        scaled, scaled_normed = back * gain_node, back_normed * gain_node
        d_out = (inv * (scaled - row_mean(scaled) - normed * row_mean(scaled_normed))).astype(BF16)
        m.gmat_v[6 * width : 7 * width, :] += dot_tn(act, d_out)
        m.vsum_v[32:40, :] += fold_rows(back_normed)
        m.vsum_v[40:48, :] += fold_rows(back)
        d_pre = dot_nt(d_out, m.half_v[6 * width : 7 * width, :]) * slope
        d_pre = d_pre.astype(BF16)
        m.vsum_v[24:32, :] += fold_rows(d_pre.astype(F32))
        m.gmat_v[4 * width : 6 * width, :] += dot_tn(joined, d_pre)
        d_joined = dot_nt(d_pre, weight_ref[4 * width : 6 * width, :])
        ntot_ref[rows, :] = back + d_joined[:, :width]
        high, low = split(d_joined[:, width:])
        for k in range(2):
            for c in range(z.bwd_chunks):
                own = slice(k * nodes + c * z.bwd_nodes, k * nodes + (c + 1) * z.bwd_nodes)
                m.drep_v[aligned((i * 2 + k) * z.bwd_chunks + c, 2 * LANES), :] = jnp.concatenate(
                    [high[own], low[own]], 0
                )
        return carry

    lax.fori_loop(0, samples // 2, node_part, 0)

    def backward(i, carry):
        s, c = i // z.bwd_chunks, i % z.bwd_chunks
        rows, local = aligned(i, z.bwd_rows), aligned(c, z.bwd_rows)

        @pl.when(c == 0)
        def _():
            sample_copy(cot_ref, m.cot_v, m.cot_sem, s).wait()

        cot = m.cot_v[rows, :].astype(F32)
        d_update = (cot + dot_nn(m.rep_v[...], m.drep_v[aligned(i, 2 * LANES), :])) * both(m.live_v[local, :])
        normed = m.norm_v[rows, :].astype(F32)
        d_normed = d_update * normed
        m.vsum_v[8:16, :] += fold_rows(d_normed)
        m.vsum_v[16:24, :] += fold_rows(d_update)
        scaled, scaled_normed = d_update * gain_edge, d_normed * gain_edge
        d_out = both(m.inv_v[rows, :]) * (scaled - row_mean(scaled) - normed * row_mean(scaled_normed))
        d_out = d_out.astype(BF16)
        d_pre = dot_nt(d_out, m.half_v[3 * width : 4 * width, :]) * m.slope_v[rows, :]
        d_pre = d_pre.astype(BF16)
        m.gmat_v[3 * width : 4 * width, :] += dot_tn(m.act_v[rows, :], d_out)
        m.gmat_v[0:width, :] += dot_tn(m.edge_v[rows, :], d_pre)
        m.recv_v[aligned(i, z.bwd_nodes), :] = dot_nn(m.rep_t[...], d_pre)
        m.aown_v[aligned(s, nodes), :] += dot_nn(m.own_t[:, local], d_pre)
        m.ahalo_v[aligned(s, two_halo), :] += dot_nn(m.halo_t[:, local], d_pre)
        m.egrad_v[rows, :] = (cot + dot_nt(d_pre, weight_ref[0:width, :])).astype(BF16)

        @pl.when(c == z.bwd_chunks - 1)
        def _():
            sample_copy(m.egrad_v, egrad_ref, m.egrad_sem, s).start()

        return carry

    lax.fori_loop(0, samples * z.bwd_chunks, backward, 0)

    send_full = weight_ref[width : 2 * width, :]
    recv_full = weight_ref[2 * width : 3 * width, :]
    out_high, out_low = split(m.ahalo_v[...])
    border_ref[...] = (dot_nt(out_high, send_full) + dot_nt(out_low, send_full)).astype(BF16)
    table = m.table_v[...]
    grad_send = dot_tn(table, out_high) + dot_tn(table, out_low)
    grad_recv = jnp.zeros((width, width), F32)
    for s in range(samples):
        rows = slice(s * nodes, (s + 1) * nodes)
        recv = m.recv_v[rows, :]
        m.vsum_v[0:8, :] += fold_rows(recv)
        recv_high, recv_low = split(recv)
        own_high, own_low = split(m.aown_v[rows, :])
        node = node_ref[rows, :]
        grad_recv += dot_tn(node, recv_high) + dot_tn(node, recv_low)
        grad_send += dot_tn(node, own_high) + dot_tn(node, own_low)
        ntot_ref[rows, :] += (
            dot_nt(recv_high, recv_full) + dot_nt(recv_low, recv_full)
            + dot_nt(own_high, send_full) + dot_nt(own_low, send_full)
        )
    grad_ref[0:width, :] = m.gmat_v[0:width, :].astype(BF16)
    grad_ref[width : 2 * width, :] = grad_send.astype(BF16)
    grad_ref[2 * width : 3 * width, :] = grad_recv.astype(BF16)
    grad_ref[3 * width :, :] = m.gmat_v[3 * width :, :].astype(BF16)
    for k in range(6):
        gvec_ref[k : k + 1, :] = jnp.sum(m.vsum_v[k * 8 : (k + 1) * 8, :], 0, keepdims=True)
    gvec_ref[6:8, :] = jnp.zeros((2, width), F32)
    for s in range(samples):
        sample_copy(m.eout_v, eout_ref, m.eout_sem, s).wait()
        sample_copy(m.egrad_v, egrad_ref, m.egrad_sem, s).wait()


def main_call(z, edge, cot, node, ncot, five, senders, weights, halo, vectors):
    scratch = main_scratch(z)
    rows, per_node, width = z.samples * z.edges, z.samples * z.nodes, z.width
    whole = pl.BlockSpec(memory_space=pltpu.VMEM)
    anywhere = pl.BlockSpec(memory_space=pl.ANY)
    return pl.pallas_call(
        partial(main_kernel, z, tuple(scratch)),
        out_shape=(
            jax.ShapeDtypeStruct((rows, width), BF16),
            jax.ShapeDtypeStruct((rows, width), BF16),
            jax.ShapeDtypeStruct((per_node, width), BF16),
            jax.ShapeDtypeStruct((per_node, width), F32),
            jax.ShapeDtypeStruct((z.samples * 2 * z.halo, width), BF16),
            jax.ShapeDtypeStruct((7 * width, width), BF16),
            jax.ShapeDtypeStruct((8, width), F32),
        ),
        in_specs=[anywhere] * 2 + [whole] * 7,
        out_specs=(anywhere, anywhere, whole, whole, whole, whole, whole),
        scratch_shapes=list(scratch.values()),
        compiler_params=pltpu.CompilerParams(vmem_limit_bytes=VMEM_LIMIT),
        name="edge_node_round",
    )(edge, cot, node, ncot, five, senders, weights, halo, vectors)


def dot_exact(left, right, dims):
    return lax.dot_general(left, right, (dims, ((), ())), precision=HIGH, preferred_element_type=F32)


BLOCK = 32
COUNT = 4


def factor_block(packed):
    sub = iota((8, LANES), 0)
    lane = iota((8, LANES), 1)
    tiles = BLOCK // 8
    group = lane & (LANES - BLOCK)
    parts = [packed[8 * r : 8 * r + 8, :] for r in range(tiles)]
    columns = [
        [jnp.take_along_axis(parts[r], group + l, axis=1) if r >= l // 8 else None for r in range(tiles)]
        for l in range(BLOCK)
    ]
    inverse = [jnp.where((lane & (BLOCK - 1)) == sub + 8 * r, 1.0, 0.0) for r in range(tiles)]

    def line(tile, s):
        return jnp.broadcast_to(tile[s : s + 1, :], (8, LANES))

    for j in range(BLOCK):
        rj, sj = j // 8, j % 8
        scale = lax.rsqrt(line(columns[j][rj], sj))
        below = [None if r < rj else columns[j][r] * scale for r in range(tiles)]
        below[rj] = jnp.where(sub > sj, below[rj], 0.0)
        for l in range(j + 1, BLOCK):
            weight = line(below[l // 8], l % 8)
            for r in range(l // 8, tiles):
                columns[l][r] = columns[l][r] - below[r] * weight
        row = line(inverse[rj], sj) * scale
        inverse[rj] = jnp.where(sub == sj, row, inverse[rj] - below[rj] * row)
        for r in range(rj + 1, tiles):
            inverse[r] = inverse[r] - below[r] * row
    return jnp.concatenate(inverse, 0)


def orthogonalize(work_v, width):
    per_half = LANES // BLOCK
    group = iota((BLOCK, LANES), 1) // BLOCK
    for b in range(width // BLOCK):
        half = b // per_half
        first = b * BLOCK
        rows = slice(first, first + BLOCK)
        lanes = slice(half * LANES, (half + 1) * LANES)
        place = [(b + k) % COUNT for k in range(COUNT)]
        packed = work_v[0, rows, lanes]
        for k in range(1, COUNT):
            packed = jnp.where(group == place[k], work_v[k, rows, lanes], packed)
        inverse = factor_block(packed)
        spread = jnp.concatenate([jnp.where(group == place[k], inverse, 0.0) for k in range(COUNT)], 0)
        start = (first + BLOCK) // LANES * LANES
        stack = jnp.concatenate([work_v[(g - b) % COUNT, rows, start:] for g in range(COUNT)], 0)
        solved = dot_exact(spread, stack, ((1,), (0,)))
        for k in range(COUNT):
            work_v[k, rows, width:] = solved[k * BLOCK : (k + 1) * BLOCK, width - start :]
        edges = [first + BLOCK, min(first + 2 * BLOCK, width), width]
        for low, high in zip(edges[:-1], edges[1:], strict=True):
            if low >= high:
                continue
            column = iota((high - low, LANES), 1) // BLOCK
            for k in range(COUNT):
                turned = dot_exact(work_v[k, low:high, lanes], spread, ((1,), (1,)))
                turned = jnp.where(column == k, turned, 0.0)
                work_v[k, low:high, start:] -= dot_exact(turned, solved, ((1,), (0,)))


def matrix_of(row, width):
    return sum((row >= bound * width).astype(jnp.int32) for bound in (3, 4, 6))


def update_kernel(
    grad_ref, gvec_ref, kern_ref, kfirst_ref, ksecond_ref, vec_ref, vfirst_ref, vsecond_ref, stat_ref, bases_ref,
    kern_out, kfirst_out, ksecond_out, half_out, vec_out, vfirst_out, vsecond_out, stat_out, bases_out, work_v,
):
    width = stat_ref.shape[-1]
    shard = kern_ref.shape[0]
    correct = 1.0 - BETA_ONE**STEP
    correct_two = 1.0 - BETA_TWO**STEP
    bounds = [0, 3 * width, 4 * width, 6 * width, 7 * width]
    half = LANES // BLOCK
    for k in range(COUNT):
        rows = grad_ref[bounds[k] : bounds[k + 1], :]
        stat = BETA_TWO * stat_ref[k] + (1.0 - BETA_TWO) * dot_tn(rows, rows)
        stat_out[k] = stat
        turned = dot_exact(bases_ref[k], stat, ((0,), (0,)))
        order = [h * half + (g - k) % half for h in range(width // LANES) for g in range(half)]
        moved = jnp.concatenate([turned[i * BLOCK : (i + 1) * BLOCK, :] for i in order], 0)
        work_v[k, :, 0:width] = dot_exact(turned, moved, ((1,), (1,)))
        work_v[k, :, width:] = turned

    first_row = lax.axis_index("fs") * shard
    grad = grad_ref[pl.ds(pl.multiple_of(first_row, 64), shard), :].astype(F32)
    one = matrix_of(first_row, width)
    two = matrix_of(first_row + shard - 1, width)
    in_two = matrix_of(first_row + iota((shard, width), 0), width) != one
    basis_one, basis_two = bases_ref[one], bases_ref[two]
    rotated = jnp.where(
        in_two, dot_exact(grad, basis_two, ((1,), (0,))), dot_exact(grad, basis_one, ((1,), (0,)))
    )
    first_new = BETA_ONE * kfirst_ref[...] + (1.0 - BETA_ONE) * rotated
    second_new = BETA_TWO * ksecond_ref[...] + (1.0 - BETA_TWO) * rotated * rotated
    kfirst_out[...] = first_new
    ksecond_out[...] = second_new
    step = first_new / correct / (jnp.sqrt(second_new / correct_two) + ADAM_EPS)
    turned = jnp.where(in_two, dot_exact(step, basis_two, ((1,), (1,))), dot_exact(step, basis_one, ((1,), (1,))))
    kern = kern_ref[...]
    kern_new = kern - RATE_MATRIX * (turned + DECAY_RATE * kern)
    kern_out[...] = kern_new
    half_out[...] = kern_new.astype(BF16)
    gvec = gvec_ref[0:6, :]
    first_new = BETA_ONE * vfirst_ref[...] + (1.0 - BETA_ONE) * gvec
    second_new = BETA_TWO * vsecond_ref[...] + (1.0 - BETA_TWO) * gvec * gvec
    vfirst_out[...] = first_new
    vsecond_out[...] = second_new
    vec_out[...] = vec_ref[...] - RATE_VECTOR * (first_new / correct) / (jnp.sqrt(second_new / correct_two) + ADAM_EPS)

    orthogonalize(work_v, width)
    for k in range(COUNT):
        bases_out[k] = work_v[k, :, width:].T


def update_call(grad, gvec, kern, kfirst, ksecond, vec, vfirst, vsecond, stat, bases):
    shard, width = kern.shape
    whole = pl.BlockSpec(memory_space=pltpu.VMEM)
    rows = jax.ShapeDtypeStruct((shard, width), F32)
    six = jax.ShapeDtypeStruct(vec.shape, F32)
    square = jax.ShapeDtypeStruct(stat.shape, F32)
    return pl.pallas_call(
        update_kernel,
        out_shape=(rows, rows, rows, jax.ShapeDtypeStruct((shard, width), BF16), six, six, six, square, square),
        in_specs=[whole] * 10,
        out_specs=(whole,) * 9,
        scratch_shapes=[pltpu.VMEM((COUNT, width, 2 * width), F32)],
        compiler_params=pltpu.CompilerParams(vmem_limit_bytes=VMEM_LIMIT),
        name="update",
    )(grad, gvec, kern, kfirst, ksecond, vec, vfirst, vsecond, stat, bases)


def exchange(low_part, high_part):
    count = lax.axis_size("nodes")
    up = [(i, i + 1) for i in range(count - 1)]
    down = [(i + 1, i) for i in range(count - 1)]
    return lax.ppermute(high_part, "nodes", up), lax.ppermute(low_part, "nodes", down)


def on_device(
    edge_latent, node_latent, edge_cot, node_cot, five_flag, senders, send_rows, kernels, kernel_first, kernel_second,
    vectors, vector_first, vector_second, statistics, bases,
):
    samples, nodes, width = node_latent.shape
    slots = senders.shape[0] // nodes
    halo = send_rows.shape[1]
    z = Sizes(samples, nodes, slots, halo, width)
    weights = lax.all_gather(kernels.astype(BF16), "fs", axis=0, tiled=True)
    packed = jnp.take(node_latent, send_rows.reshape(-1), axis=1).reshape(samples, 2, halo, width)
    below, above = exchange(packed[:, 0], packed[:, 1])
    around = jnp.stack([below.reshape(samples * halo, width), above.reshape(samples * halo, width)])
    edge_out, edge_grad, node_out, node_total, border, grad, gvec = main_call(
        z,
        edge_latent.reshape(-1, width),
        edge_cot.reshape(-1, width),
        node_latent.reshape(-1, width),
        node_cot.reshape(-1, width),
        five_flag.reshape(1, -1),
        senders.reshape(1, -1),
        weights,
        around,
        vectors,
    )
    border = border.reshape(samples, 2, halo, width)
    below, above = exchange(border[:, 0], border[:, 1])
    node_total = node_total.reshape(samples, nodes, width)
    node_total = node_total.at[:, send_rows[0]].add(below.astype(F32))
    node_total = node_total.at[:, send_rows[1]].add(above.astype(F32))
    grad = lax.psum(grad, ("nodes", "fs"))
    gvec = lax.psum(gvec, ("nodes", "fs"))
    kernel_new, first_new, second_new, half, vec_new, vfirst_new, vsecond_new, stat_new, bases_new = update_call(
        grad, gvec, kernels, kernel_first, kernel_second, vectors, vector_first, vector_second, statistics, bases
    )
    weights_half = lax.all_gather(half, "fs", axis=0, tiled=True)
    return (
        edge_out.reshape(edge_latent.shape),
        node_out.reshape(node_latent.shape),
        edge_grad.reshape(edge_latent.shape),
        node_total.astype(BF16),
        kernel_new, first_new, second_new, vec_new, vfirst_new, vsecond_new, stat_new, bases_new, weights_half,
    )


def solution(mesh):
    in_specs = (
        P("fs", "nodes", None),
        P("fs", "nodes", None),
        P("fs", "nodes", None),
        P("fs", "nodes", None),
        P("nodes"),
        P("nodes"),
        P("nodes", None),
        P("fs", None),
        P("fs", None),
        P("fs", None),
        P(),
        P(),
        P(),
        P(),
        P(),
    )
    out_specs = (
        P("fs", "nodes", None),
        P("fs", "nodes", None),
        P("fs", "nodes", None),
        P("fs", "nodes", None),
        P("fs", None),
        P("fs", None),
        P("fs", None),
        P(),
        P(),
        P(),
        P(),
        P(),
        P(),
    )
    return jax.shard_map(
        on_device, mesh=mesh, in_specs=in_specs, out_specs=out_specs, check_vma=False
    )
```

time: 744 us -> 240 us (0.32)
  other arithmetic: 361 us -> 5.07 us
  local copies, waits for them, and re-layouts: 154 us -> 8.23 us
  matrix products: 70 us -> 0 us
  waiting for transfers between devices: 8.8 us -> 76.4 us
  Pallas kernels: 0 us -> 62.1 us
  starting transfers between devices: 52.5 us -> 12 us
  blocking collectives: 73.6 us -> 61.8 us
    another operation x27 -> x1, other arithmetic: 237 us -> 0.64 us  [on_device(): jnp.stack([below.reshape(samples * halo, width), above.reshape(samples *...]
    psum x1, waiting for transfers between devices: 8.72 us -> 76.4 us  [on_device(): grad = lax.psum(grad, ('nodes', 'fs'))]
    dot_general x53 -> x0, matrix products: 62.9 us -> none  [the longest x16 25.1 us: cols_product(): lax.dot_general(left, right, (((1,), (1,)), ((), ())), preferred_element_...]
    pallas_call x0 -> x2, Pallas kernels: none -> 62.1 us  [the longest x1 33.5 us: main_call(): pl.pallas_call(partial(main_kernel, z, tuple(scratch)), out_shape=(jax.Sh...]
    scatter-add x12 -> x2, other arithmetic: 47 us -> 2.41 us  [the longest x1 1.3 us: on_device(): node_total = node_total.at[:, send_rows[1]].add(above.astype(F32))]
    ppermute x16 -> x4, starting transfers between devices: 52.5 us -> 12 us  [the longest x2 9.39 us: exchange(): lax.ppermute(high_part, 'nodes', up)]
    unnamed x467 -> x8, local copies, waits for them, and re-layouts: 34.9 us -> 1.83 us
    gather x20 -> x1, local copies, waits for them, and re-layouts: 32 us -> 1.63 us  [on_device(): jnp.take(node_latent, send_rows.reshape(-1), axis=1)]
  transfers between devices with their start and end apart: 18 -> 5, of which waited for: 1 -> 1; matrix products, arithmetic and copies ran while one was open for 11% -> 4% of each run, Pallas kernels for 0% -> 0%
where the time goes in v1:
time: 240 us
  waiting for transfers between devices  76.4 us (32%)
  Pallas kernels  62.1 us (26%)
  blocking collectives  61.8 us (26%)
  between operations  14.2 us (6%)
  starting transfers between devices  12 us (5%)
  local copies, waits for them, and re-layouts  8.23 us (3%)
  other arithmetic  5.07 us (2%)
    psum x1, waiting for transfers between devices, on_device(): grad = lax.psum(grad, ('nodes', 'fs'))  76.4 us
    psum x1, blocking collectives, on_device(): gvec = lax.psum(gvec, ('nodes', 'fs'))  42.6 us
    pallas_call x1, Pallas kernels, main_call(): pl.pallas_call(partial(main_kernel, z, tuple(scratch)), out_shape=(jax.Sh...  33.5 us
    pallas_call x1, Pallas kernels, update_call(): pl.pallas_call(update_kernel, out_shape=(rows, rows, rows, jax.ShapeDtype...  28.6 us
    all_gather x1, blocking collectives, on_device(): weights = lax.all_gather(kernels.astype(BF16), 'fs', axis=0, tiled=True)  9.79 us
    all_gather x1, blocking collectives, on_device(): weights_half = lax.all_gather(half, 'fs', axis=0, tiled=True)  9.42 us
    ppermute x2, starting transfers between devices, exchange(): lax.ppermute(high_part, 'nodes', up)  9.39 us
  transfers between devices with their start and end apart: 5, of which 1 were waited for; matrix products, arithmetic and copies ran while one was open for 4% of the time, Pallas kernels for 0%

profile of v1, /device:TPU:0, one launch (start us, length us, event | category | flops | bytes accessed | tf_op | source)
XLA Modules:
  0.0 239.9 jit_solution(17042053156953816436)
XLA Ops:
  7.2 0.0 all-reduce.2.cloned.1.call-start
  7.2 0.8 reshape.161
  8.0 0.7 compare_and_fusion
  8.7 1.6 gather_fusion
  10.3 0.1 copy_select_fusion
  10.4 4.8 %collective-permute-start = (bf16[4,16,256]{2,1,0:T(8,128)(2,1)S(1)}, bf16[4,16,256]{2,1,0:T(8,128)(2,1)S(1)}, u32[]{:S(2)}, u32[]{:S(2)}) collective-permute-start(bf16[4,16,256]{2,1,0:T(8,128)(2,1)S(1)} %get-tuple-element.73), channel_id=1, source_target_pairs={{0,1},{1,2},{2,3},{3,4},{4,5},{5,6},{6,7},{8,9},{9,10},{10,11},{11... | collective-permute-start | bytes 98312 | tf_op jit(solution)/shard_map/ppermute | solution.py:525
  15.2 1.3 collective-permute-start.1
  16.5 1.0 convert_element_type.12
  17.6 9.8 %all_gather.6.weight_ref = bf16[1792,256]{1,0:T(8,128)(2,1)} all-gather(bf16[448,256]{1,0:T(8,128)(2,1)S(1)} %convert_element_type.12), channel_id=1, replica_groups=mesh['fs'=4,'nodes'=8] {'fs'}, dimensions={0}, use_global_device_ids=true | all-gather | bytes 1146880 | tf_op jit(solution)/shard_map/all_gather | solution.py:536
  27.4 1.3 reshape.160.send_ref
  28.7 0.0 collective-permute-done
  28.7 0.0 collective-permute-done.1
  28.7 0.6 pad_maximum_fusion.halo_ref
  29.3 0.0 copy-start.1
  29.3 33.5 %edge_node_round.1 = (bf16[6144,256]{1,0:T(8,128)(2,1)}, bf16[6144,256]{1,0:T(8,128)(2,1)}, bf16[1024,256]{1,0:T(8,128)(2,1)}, f32[1024,256]{1,0:T(8,128)}, bf16...) custom-call(bf16[6144,256]{1,0:T(8,128)(2,1)} %bitcast.39, bf16[6144,256]{1,0:T(8,128)(2,1)} %bitcast.40, ...), custom_call_target="tpu_custom_call" | custom-call | tf_op jit(solution)/shard_map/edge_node_round/pallas_call | solution.py:361
  62.8 0.0 copy-start
  62.8 0.0 all-reduce.2.cloned.1.call-update
  62.9 0.8 fusion.3
  63.7 4.5 %collective-permute-start.2 = (bf16[4,16,256]{2,0,1:T(4,128)(2,1)S(1)}, bf16[4,16,256]{2,0,1:T(4,128)(2,1)S(1)}, u32[]{:S(2)}, u32[]{:S(2)}) collective-permute-start(bf16[4,16,256]{2,0,1:T(4,128)(2,1)S(1)} %bitcast.46), channel_id=1, source_target_pairs={{0,1},{1,2},{2,3},{3,4},{4,5},{5,6},{6,7},{8,9},{9,10},{10,11},{11... | collective-permute-start | bytes 98312 | tf_op jit(solution)/shard_map/ppermute | solution.py:525
  68.2 0.0 copy-done.1
  68.3 1.3 collective-permute-start.3
  69.6 1.9 copy.35
  71.5 0.0 copy-done
  71.5 42.6 %psum.15.gvec_ref = f32[8,256]{1,0:T(8,128)} all-reduce(f32[8,256]{1,0:T(8,128)S(1)} %copy-done), channel_id=1, replica_groups=mesh['fs'=4,'nodes'=8] {'nodes','fs'}, use_global_device_ids=true, to_apply=%region_3.4 | all-reduce | flops 2048 | bytes 16384 | tf_op jit(solution)/shard_map/psum | solution.py:558
  114.1 0.0 collective-permute-done.2
  114.1 1.1 scatter_fusion
  115.3 0.0 collective-permute-done.3
  115.3 1.3 scatter_fusion.1
  116.6 0.2 convert_element_type.15
  116.8 0.9 copy.37
  117.6 76.4 %all-reduce.2.cloned.1.call-done.grad_ref = bf16[1792,256]{1,0:T(8,128)(2,1)} async-done(((bf16[1792,256]{1,0:T(8,128)(2,1)}), bf16[1792,256]{1,0:T(8,128)(2,1)}) %all-reduce.2.cloned.1.call-update) | async-done | bytes 917520 | tf_op jit(solution)/shard_map/psum | solution.py:557
  194.0 28.6 %update.1 = (f32[448,256]{1,0:T(8,128)}, f32[448,256]{1,0:T(8,128)}, f32[448,256]{1,0:T(8,128)}, bf16[448,256]{1,0:T(8,128)(2,1)}, f32[6,256]{1,0:T(8,128)}, /*i...) custom-call(bf16[1792,256]{1,0:T(8,128)(2,1)} %all-reduce.2.cloned.1.call-done.grad_ref, ...), custom_call_target="tpu_custom_call" | custom-call | tf_op jit(solution)/shard_map/update/pallas_call | solution.py:510
  222.7 9.4 %all_gather.7 = bf16[1792,256]{1,0:T(8,128)(2,1)S(1)} all-gather(bf16[448,256]{1,0:T(8,128)(2,1)} %get-tuple-element.44), channel_id=1, replica_groups=mesh['fs'=4,'nodes'=8] {'fs'}, dimensions={0}, use_global_device_ids=true | all-gather | bytes 1146880 | tf_op jit(solution)/shard_map/all_gather | solution.py:562
  232.1 0.9 copy.49
  (8 shorter events, 0.1 us)
Async XLA Ops:
  7.2 186.9 %all-reduce.2.cloned.1.call-start = ((), (), s32[]{:S(2)}) async-start(), calls=%async_computation | async-start | bytes 1835008 | tf_op jit(solution)/shard_map/psum | solution.py:557
  10.4 18.3 %collective-permute-start = (bf16[4,16,256]{2,1,0:T(8,128)(2,1)S(1)}, bf16[4,16,256]{2,1,0:T(8,128)(2,1)S(1)}, u32[]{:S(2)}, u32[]{:S(2)}) collective-permute-start(bf16[4,16,256]{2,1,0:T(8,128)(2,1)S(1)} %get-tuple-element.73), channel_id=1, source_target_pairs={{0,1},{1,2},{2,3},{3,4},{4,5},{5,6},{6,7},{8,9},{9,10},{10,11},{11... | collective-permute-start | bytes 98312 | tf_op jit(solution)/shard_map/ppermute | solution.py:525
  15.2 13.4 %collective-permute-start.1 = (bf16[4,16,256]{2,1,0:T(8,128)(2,1)S(1)}, bf16[4,16,256]{2,1,0:T(8,128)(2,1)S(1)}, u32[]{:S(2)}, u32[]{:S(2)}) collective-permute-start(bf16[4,16,256]{2,1,0:T(8,128)(2,1)S(1)} %get-tuple-element.74), channel_id=1, source_target_pairs={{1,0},{2,1},{3,2},{4,3},{5,4},{6,5},{7,6},{9,8},{10,9},{11,10},{12... | collective-permute-start | bytes 98312 | tf_op jit(solution)/shard_map/ppermute | solution.py:525
  29.3 38.9 %copy-start.1 = (s32[2,16]{1,0:T(2,128)S(1)}, s32[2,16]{1,0:T(2,128)}, u32[]{:S(2)}) copy-start(s32[2,16]{1,0:T(2,128)} %param.21) | copy-start | bytes 388
  62.8 8.7 %copy-start = (f32[8,256]{1,0:T(8,128)S(1)}, f32[8,256]{1,0:T(8,128)}, u32[]{:S(2)}) copy-start(f32[8,256]{1,0:T(8,128)} %get-tuple-element.35) | copy-start | bytes 24580
  63.7 50.5 %collective-permute-start.2 = (bf16[4,16,256]{2,0,1:T(4,128)(2,1)S(1)}, bf16[4,16,256]{2,0,1:T(4,128)(2,1)S(1)}, u32[]{:S(2)}, u32[]{:S(2)}) collective-permute-start(bf16[4,16,256]{2,0,1:T(4,128)(2,1)S(1)} %bitcast.46), channel_id=1, source_target_pairs={{0,1},{1,2},{2,3},{3,4},{4,5},{5,6},{6,7},{8,9},{9,10},{10,11},{11... | collective-permute-start | bytes 98312 | tf_op jit(solution)/shard_map/ppermute | solution.py:525
  68.3 47.0 %collective-permute-start.3 = (bf16[4,16,256]{2,0,1:T(4,128)(2,1)S(1)}, bf16[4,16,256]{2,0,1:T(4,128)(2,1)S(1)}, u32[]{:S(2)}, u32[]{:S(2)}) collective-permute-start(bf16[4,16,256]{2,0,1:T(4,128)(2,1)S(1)} %bitcast.47), channel_id=1, source_target_pairs={{1,0},{2,1},{3,2},{4,3},{5,4},{6,5},{7,6},{9,8},{10,9},{11,10},{12... | collective-permute-start | bytes 98312 | tf_op jit(solution)/shard_map/ppermute | solution.py:525
Sparse Core Ops, SparseCore 0:
  63.0 131.0 all-reduce.1

commit v2 on v1

--- a/solution.py
+++ b/solution.py
@@ -324,7 +324,12 @@
     send_full = weight_ref[width : 2 * width, :]
     recv_full = weight_ref[2 * width : 3 * width, :]
     out_high, out_low = split(m.ahalo_v[...])
-    border_ref[...] = (dot_nt(out_high, send_full) + dot_nt(out_low, send_full)).astype(BF16)
+    border = (dot_nt(out_high, send_full) + dot_nt(out_low, send_full)).astype(BF16)
+    for s in range(samples):
+        for side in range(2):
+            border_ref[side, s * halo : (s + 1) * halo, :] = border[
+                s * two_halo + side * halo : s * two_halo + (side + 1) * halo, :
+            ]
     table = m.table_v[...]
     grad_send = dot_tn(table, out_high) + dot_tn(table, out_low)
     grad_recv = jnp.zeros((width, width), F32)
@@ -365,7 +370,7 @@
             jax.ShapeDtypeStruct((rows, width), BF16),
             jax.ShapeDtypeStruct((per_node, width), BF16),
             jax.ShapeDtypeStruct((per_node, width), F32),
-            jax.ShapeDtypeStruct((z.samples * 2 * z.halo, width), BF16),
+            jax.ShapeDtypeStruct((2, z.samples * z.halo, width), BF16),
             jax.ShapeDtypeStruct((7 * width, width), BF16),
             jax.ShapeDtypeStruct((8, width), F32),
         ),
@@ -518,11 +523,256 @@
     )(grad, gvec, kern, kfirst, ksecond, vec, vfirst, vsecond, stat, bases)
 
 
-def exchange(low_part, high_part):
+MESH = pl.DeviceIdType.MESH
+
+
+def greet(partners):
+    barrier = pltpu.get_barrier_semaphore()
+    count = 0
+    for device, exists in partners:
+        if exists is None:
+            pl.semaphore_signal(barrier, inc=1, device_id=device, device_id_type=MESH)
+            count = count + 1
+        else:
+            pl.when(exists)(partial(pl.semaphore_signal, barrier, inc=1, device_id=device, device_id_type=MESH))
+            count = count + exists.astype(jnp.int32)
+    pl.semaphore_wait(barrier, count)
+
+
+def send(source, target, sems, slot, device):
+    return pltpu.make_async_remote_copy(
+        src_ref=source, dst_ref=target, send_sem=sems.at[0, slot], recv_sem=sems.at[1, slot],
+        device_id=device, device_id_type=MESH,
+    )
+
+
+class Gather:
+    PARTS = 4
+
+    def __init__(self, rows_v, sems, shard, fs, node):
+        self.rows_v, self.sems, self.shard, self.fs, self.node = rows_v, sems, shard, fs, node
+        self.next, self.far = (fs ^ 1, node), (fs ^ 2, node)
+
+    def piece(self, owner, part):
+        size = self.shard // self.PARTS
+        return self.rows_v.at[pl.ds(pl.multiple_of(owner * self.shard + part * size, 16), size)]
+
+    def copy(self, owner, part, slot, device):
+        return send(self.piece(owner, part), self.piece(owner, part), self.sems, slot * self.PARTS + part, device)
+
+    def start(self):
+        for part in range(self.PARTS):
+            self.copy(self.fs, part, 0, self.far).start()
+        for part in range(self.PARTS):
+            self.copy(self.fs, part, 1, self.next).start()
+
+    def finish(self):
+        for part in range(self.PARTS):
+            self.copy(self.fs, part, 0, self.far).wait_recv()
+            self.copy(self.fs ^ 2, part, 2, self.next).start()
+        for part in range(self.PARTS):
+            self.copy(self.fs, part, 0, self.far).wait_send()
+            self.copy(self.fs, part, 1, self.next).wait()
+            self.copy(self.fs ^ 2, part, 2, self.next).wait()
+
+
+def list_matrix(send_ref, side, nodes):
+    halo = send_ref.shape[1]
+    listed = jnp.broadcast_to(send_ref[side : side + 1, :], (nodes, halo))
+    return ones_where(listed == iota((nodes, halo), 0))
+
+
+def sides(node, count):
+    return ((node - 1, node > 0), (node + 1, node < count - 1))
+
+
+def fetch_kernel(samples, count, kern_ref, node_ref, send_ref, rows_out, halo_out, rows_v, halo_v, list_v, sems, halo_sems, out_sem):
+    fs, node = lax.axis_index("fs"), lax.axis_index("nodes")
+    shard = kern_ref.shape[0]
+    nodes = node_ref.shape[0] // samples
+    halo = send_ref.shape[1]
+    gather = Gather(rows_v, sems, shard, fs, node)
+    around = sides(node, count)
+    rows_v[pl.ds(pl.multiple_of(fs * shard, 16), shard), :] = kern_ref[...].astype(BF16)
+    halo_v[...] = jnp.zeros_like(halo_v)
+    greet([(gather.next, None), (gather.far, None)] + [((fs, other), exists) for other, exists in around])
+    gather.start()
+    for side in range(2):
+        chosen = list_matrix(send_ref, side, nodes)
+        for s in range(samples):
+            list_v[side, s * halo : (s + 1) * halo, :] = dot_tn(
+                chosen, node_ref[s * nodes : (s + 1) * nodes, :]
+            ).astype(BF16)
+    for side, (other, exists) in enumerate(around):
+        pl.when(exists)(lambda side=side, other=other: send(list_v.at[side], halo_v.at[1 - side], halo_sems, side, (fs, other)).start())
+    gather.finish()
+    out = pltpu.make_async_copy(rows_v, rows_out, out_sem)
+    out.start()
+    for side, (other, exists) in enumerate(around):
+        def settle(side=side, other=other):
+            send(list_v.at[side], halo_v.at[1 - side], halo_sems, side, (fs, other)).wait_send()
+            send(list_v.at[1 - side], halo_v.at[side], halo_sems, 1 - side, (fs, other)).wait_recv()
+        pl.when(exists)(settle)
+    halo_out[...] = halo_v[...]
+    out.wait()
+
+
+def fetch_call(kern, node, send_rows, samples):
+    shard, width = kern.shape
+    halo = send_rows.shape[1]
+    whole, anywhere = pl.BlockSpec(memory_space=pltpu.VMEM), pl.BlockSpec(memory_space=pl.ANY)
+    total = lax.axis_size("fs") * shard
+    two = (2, samples * halo, width)
+    return pl.pallas_call(
+        partial(fetch_kernel, samples, lax.axis_size("nodes")),
+        out_shape=(jax.ShapeDtypeStruct((total, width), BF16), jax.ShapeDtypeStruct(two, BF16)),
+        in_specs=[whole] * 3,
+        out_specs=(anywhere, whole),
+        scratch_shapes=[
+            pltpu.VMEM((total, width), BF16),
+            pltpu.VMEM(two, BF16),
+            pltpu.VMEM(two, BF16),
+            pltpu.SemaphoreType.DMA((2, 3 * Gather.PARTS)),
+            pltpu.SemaphoreType.DMA((2, 2)),
+            pltpu.SemaphoreType.DMA,
+        ],
+        compiler_params=pltpu.CompilerParams(
+            collective_id=0, has_side_effects=True, vmem_limit_bytes=VMEM_LIMIT
+        ),
+        name="fetch",
+    )(kern, node, send_rows)
+
+
+def reduce_plan(rows, fs_count, node_count):
+    bits = [("fs", b) for b in range(fs_count.bit_length() - 1)] + [
+        ("nodes", b) for b in range(node_count.bit_length() - 1)
+    ]
+    steps = []
+    for i, (axis, bit) in enumerate(bits):
+        halved = rows % 32 == 0 and i < len(bits) - 1
+        rows = rows // 2 if halved else rows
+        steps.append((axis, bit, rows, halved))
+    return steps
+
+
+def reduce_kernel(
+    samples, plan, count, grad_ref, gvec_ref, border_ref, total_ref, send_ref,
+    grad_out, gvec_out, node_out, sum_v, out_v, land_v, send_v, vland_v, vsend_v, ret_v, sems, vsems, halo_sems, out_sem,
+):
+    fs, node = lax.axis_index("fs"), lax.axis_index("nodes")
+    nodes = total_ref.shape[0] // samples
+    halo = send_ref.shape[1]
+    width = grad_ref.shape[1]
+    around = sides(node, count)
+
+    def partner(axis, bit):
+        return (fs ^ (1 << bit), node) if axis == "fs" else (fs, node ^ (1 << bit))
+
+    ret_v[...] = jnp.zeros_like(ret_v)
+    greet(
+        [(partner(axis, bit), None) for axis, bit, _, _ in plan] + [((fs, other), exists) for other, exists in around]
+    )
+
+    def give_back(side, other):
+        return send(border_ref.at[side], ret_v.at[1 - side], halo_sems, side, (fs, other))
+
+    for side, (other, exists) in enumerate(around):
+        pl.when(exists)(lambda side=side, other=other: give_back(side, other).start())
+
+    first, place, copies, regions = 0, 0, [], []
+    vsum = gvec_ref[...]
+    for i, (axis, bit, rows, halved) in enumerate(plan):
+        mine = ((fs if axis == "fs" else node) >> bit) & 1
+        keep = pl.multiple_of(first + mine * rows, 16) if halved else first
+        give = pl.multiple_of(first + (1 - mine) * rows, 16) if halved else first
+        if i == 0:
+            source = grad_ref.at[pl.ds(give, rows)]
+        else:
+            source = send_v.at[pl.ds(place, rows)]
+            source[...] = sum_v[pl.ds(give, rows), :].astype(BF16)
+        copy = send(source, land_v.at[pl.ds(place, rows)], sems, i, partner(axis, bit))
+        copy.start()
+        vsend_v[i] = vsum
+        vcopy = send(vsend_v.at[i], vland_v.at[i], vsems, i, partner(axis, bit))
+        vcopy.start()
+        copy.wait_recv()
+        held = grad_ref if i == 0 else sum_v if halved else send_v
+        own = keep if i == 0 or halved else place
+        total = held[pl.ds(own, rows), :].astype(F32) + land_v[pl.ds(place, rows), :].astype(F32)
+        if i == len(plan) - 1:
+            out_v[pl.ds(keep, rows), :] = total.astype(BF16)
+        else:
+            sum_v[pl.ds(keep, rows), :] = total
+        vcopy.wait_recv()
+        vsum = vsum + vland_v[i]
+        copies += [copy, vcopy]
+        regions.append((axis, bit, rows, halved, keep))
+        first, place = keep, place + rows
+    for side, (other, exists) in enumerate(around):
+        def settle(side=side, other=other):
+            give_back(side, other).wait_send()
+            give_back(1 - side, other).wait_recv()
+        pl.when(exists)(settle)
+    slot = len(plan)
+    for axis, bit, rows, halved, keep in reversed(regions):
+        if not halved:
+            continue
+        region = out_v.at[pl.ds(keep, rows)]
+        copy = send(region, region, sems, slot, partner(axis, bit))
+        copy.start()
+        copies.append(copy)
+        slot += 1
+        if axis == "fs" and bit == 0:
+            low, high = (list_matrix(send_ref, side, nodes) for side in range(2))
+            for s in range(samples):
+                rows_s = slice(s * nodes, (s + 1) * nodes)
+                part = slice(s * halo, (s + 1) * halo)
+                node_out[rows_s, :] = (
+                    total_ref[rows_s, :] + dot_nn(low, ret_v[0, part, :]) + dot_nn(high, ret_v[1, part, :])
+                ).astype(BF16)
+            gvec_out[...] = vsum
+        copy.wait_recv()
+    out = pltpu.make_async_copy(out_v, grad_out, out_sem)
+    out.start()
+    for copy in copies:
+        copy.wait_send()
+    out.wait()
+
+
+def reduce_call(grad, gvec, border, total, send_rows, samples):
+    rows, width = grad.shape
     count = lax.axis_size("nodes")
-    up = [(i, i + 1) for i in range(count - 1)]
-    down = [(i + 1, i) for i in range(count - 1)]
-    return lax.ppermute(high_part, "nodes", up), lax.ppermute(low_part, "nodes", down)
+    plan = reduce_plan(rows, lax.axis_size("fs"), count)
+    landing = sum(step[2] for step in plan)
+    gathers = sum(step[3] for step in plan)
+    whole, anywhere = pl.BlockSpec(memory_space=pltpu.VMEM), pl.BlockSpec(memory_space=pl.ANY)
+    return pl.pallas_call(
+        partial(reduce_kernel, samples, plan, count),
+        out_shape=(
+            jax.ShapeDtypeStruct(grad.shape, BF16),
+            jax.ShapeDtypeStruct(gvec.shape, F32),
+            jax.ShapeDtypeStruct(total.shape, BF16),
+        ),
+        in_specs=[whole] * 5,
+        out_specs=(anywhere, whole, whole),
+        scratch_shapes=[
+            pltpu.VMEM((rows, width), F32),
+            pltpu.VMEM((rows, width), BF16),
+            pltpu.VMEM((landing, width), BF16),
+            pltpu.VMEM((landing, width), BF16),
+            pltpu.VMEM((len(plan),) + gvec.shape, F32),
+            pltpu.VMEM((len(plan),) + gvec.shape, F32),
+            pltpu.VMEM(border.shape, BF16),
+            pltpu.SemaphoreType.DMA((2, len(plan) + gathers)),
+            pltpu.SemaphoreType.DMA((2, len(plan))),
+            pltpu.SemaphoreType.DMA((2, 2)),
+            pltpu.SemaphoreType.DMA,
+        ],
+        compiler_params=pltpu.CompilerParams(
+            collective_id=1, has_side_effects=True, vmem_limit_bytes=VMEM_LIMIT
+        ),
+        name="reduce",
+    )(grad, gvec, border, total, send_rows)
 
 
 def on_device(
@@ -533,10 +783,7 @@
     slots = senders.shape[0] // nodes
     halo = send_rows.shape[1]
     z = Sizes(samples, nodes, slots, halo, width)
-    weights = lax.all_gather(kernels.astype(BF16), "fs", axis=0, tiled=True)
-    packed = jnp.take(node_latent, send_rows.reshape(-1), axis=1).reshape(samples, 2, halo, width)
-    below, above = exchange(packed[:, 0], packed[:, 1])
-    around = jnp.stack([below.reshape(samples * halo, width), above.reshape(samples * halo, width)])
+    weights, around = fetch_call(kernels, node_latent.reshape(-1, width), send_rows, samples)
     edge_out, edge_grad, node_out, node_total, border, grad, gvec = main_call(
         z,
         edge_latent.reshape(-1, width),
@@ -549,13 +796,7 @@
         around,
         vectors,
     )
-    border = border.reshape(samples, 2, halo, width)
-    below, above = exchange(border[:, 0], border[:, 1])
-    node_total = node_total.reshape(samples, nodes, width)
-    node_total = node_total.at[:, send_rows[0]].add(below.astype(F32))
-    node_total = node_total.at[:, send_rows[1]].add(above.astype(F32))
-    grad = lax.psum(grad, ("nodes", "fs"))
-    gvec = lax.psum(gvec, ("nodes", "fs"))
+    grad, gvec, node_grad = reduce_call(grad, gvec, border, node_total, send_rows, samples)
     kernel_new, first_new, second_new, half, vec_new, vfirst_new, vsecond_new, stat_new, bases_new = update_call(
         grad, gvec, kernels, kernel_first, kernel_second, vectors, vector_first, vector_second, statistics, bases
     )
@@ -564,7 +805,7 @@
         edge_out.reshape(edge_latent.shape),
         node_out.reshape(node_latent.shape),
         edge_grad.reshape(edge_latent.shape),
-        node_total.astype(BF16),
+        node_grad.reshape(node_latent.shape),
         kernel_new, first_new, second_new, vec_new, vfirst_new, vsecond_new, stat_new, bases_new, weights_half,
     )
 

time: 240 us -> 129 us (0.54)
  waiting for transfers between devices: 76.4 us -> 0 us
  Pallas kernels: 62.1 us -> 115 us
  blocking collectives: 61.8 us -> 9.93 us
  between operations: 14.2 us -> 0.68 us
  starting transfers between devices: 12 us -> 0 us
  local copies, waits for them, and re-layouts: 8.23 us -> 3.02 us
  other arithmetic: 5.07 us -> 0 us
    psum x1 -> x0, waiting for transfers between devices: 76.4 us -> none  [on_device(): grad = lax.psum(grad, ('nodes', 'fs'))]
    pallas_call x0 -> x2, Pallas kernels: none -> 53 us  [the longest x1 39.3 us: reduce_call(): pl.pallas_call(partial(reduce_kernel, samples, plan, count), out_shape=(j...]
    psum x1 -> x0, blocking collectives: 42.6 us -> none  [on_device(): gvec = lax.psum(gvec, ('nodes', 'fs'))]
    ppermute x4 -> x0, starting transfers between devices: 12 us -> none  [the longest x2 9.39 us: exchange(): lax.ppermute(high_part, 'nodes', up)]
    all_gather x1 -> x0, blocking collectives: 9.79 us -> none  [on_device(): weights = lax.all_gather(kernels.astype(BF16), 'fs', axis=0, tiled=True)]
    reshape x2 -> x0, local copies, waits for them, and re-layouts: 2.68 us -> none  [the longest x1 1.92 us: on_device(): node_total = node_total.reshape(samples, nodes, width)]
    scatter-add x2 -> x0, other arithmetic: 2.41 us -> none  [the longest x1 1.3 us: on_device(): node_total = node_total.at[:, send_rows[1]].add(above.astype(F32))]
  transfers between devices with their start and end apart: 5 -> 0, of which waited for: 1 -> 0; matrix products, arithmetic and copies ran while one was open for 4% -> 0% of each run, Pallas kernels for 0% -> 0%
where the time goes in v2:
time: 129 us
  Pallas kernels  115 us (89%)
  blocking collectives  9.93 us (8%)
  local copies, waits for them, and re-layouts  3.02 us (2%)
    pallas_call x1, Pallas kernels, reduce_call(): pl.pallas_call(partial(reduce_kernel, samples, plan, count), out_shape=(j...  39.3 us
    pallas_call x1, Pallas kernels, main_call(): pl.pallas_call(partial(main_kernel, z, tuple(scratch)), out_shape=(jax.Sh...  33.5 us
    pallas_call x1, Pallas kernels, update_call(): pl.pallas_call(update_kernel, out_shape=(rows, rows, rows, jax.ShapeDtype...  28.6 us
    pallas_call x1, Pallas kernels, fetch_call(): pl.pallas_call(partial(fetch_kernel, samples, lax.axis_size('nodes')), ou...  13.7 us
    all_gather x1, blocking collectives, on_device(): weights_half = lax.all_gather(half, 'fs', axis=0, tiled=True)  9.93 us

profile of v2, /device:TPU:0, one launch (start us, length us, event | category | flops | bytes accessed | tf_op | source)
XLA Modules:
  0.0 128.7 jit_solution(14235836043273606626)
XLA Ops:
  0.6 1.3 %reshape.62.send_ref = s32[1,1536]{1,0:T(1,128)} reshape(s32[1536]{0:T(1024)} %param.20) | data formatting | bytes 12288 | tf_op jit(solution)/shard_map/reshape | solution.py:794
  1.9 13.7 %fetch.1 = (bf16[1792,256]{1,0:T(8,128)(2,1)}, bf16[2,64,256]{2,1,0:T(8,128)(2,1)}) custom-call(f32[448,256]{1,0:T(8,128)} %kern_ref.3, bf16[1024,256]{1,0:T(8,128)(2,1)} %bitcast.11, s32[2,16]{1,0:T(2,128)} %send_ref.3), custom_call_target="tpu_custom_call" | custom-call | tf_op jit(solution)/shard_map/fetch/pallas_call | solution.py:626
  15.7 33.5 %edge_node_round.1 = (bf16[6144,256]{1,0:T(8,128)(2,1)}, bf16[6144,256]{1,0:T(8,128)(2,1)}, bf16[1024,256]{1,0:T(8,128)(2,1)}, f32[1024,256]{1,0:T(8,128)}, bf16...) custom-call(bf16[6144,256]{1,0:T(8,128)(2,1)} %bitcast.9, bf16[6144,256]{1,0:T(8,128)(2,1)} %bitcast.10, ...), custom_call_target="tpu_custom_call" | custom-call | tf_op jit(solution)/shard_map/edge_node_round/pallas_call | solution.py:366
  49.1 39.3 %reduce.1 = (bf16[1792,256]{1,0:T(8,128)(2,1)}, f32[8,256]{1,0:T(8,128)}, bf16[1024,256]{1,0:T(8,128)(2,1)}) custom-call(bf16[1792,256]{1,0:T(8,128)(2,1)} %get-tuple-element.39.grad_ref, f32[8,256]{1,0:T(8,128)} %get-tuple-element.40.gvec_ref, bf16[2,64,256]{2,1,0:T(8,128)(2,1)} %get-tuple-element.41.border_ref, f32[1024,256]{1,0:T(8,128)} %get-tuple-element.42.total_ref, ...), custom_call_target="tpu_custom_call" | custom-call | tf_op jit(solution)/shard_map/reduce/pallas_call | solution.py:749
  88.5 0.0 copy-start
  88.5 28.6 %update.1 = (f32[448,256]{1,0:T(8,128)}, f32[448,256]{1,0:T(8,128)}, f32[448,256]{1,0:T(8,128)}, bf16[448,256]{1,0:T(8,128)(2,1)}, f32[6,256]{1,0:T(8,128)}, /*i...) custom-call(bf16[1792,256]{1,0:T(8,128)(2,1)} %get-tuple-element.44.grad_ref, ...), custom_call_target="tpu_custom_call" | custom-call | tf_op jit(solution)/shard_map/update/pallas_call | solution.py:515
  117.1 9.9 %all_gather.3 = bf16[1792,256]{1,0:T(8,128)(2,1)S(1)} all-gather(bf16[448,256]{1,0:T(8,128)(2,1)} %get-tuple-element.54), channel_id=1, replica_groups=mesh['fs'=4,'nodes'=8] {'fs'}, dimensions={0}, use_global_device_ids=true | all-gather | bytes 1146880 | tf_op jit(solution)/shard_map/all_gather | solution.py:803
  127.0 0.0 copy-done
  127.0 0.8 copy.30
  127.8 0.9 copy.31
Async XLA Ops:
  88.5 38.6 %copy-start = (bf16[1024,256]{1,0:T(8,128)(2,1)S(1)}, bf16[1024,256]{1,0:T(8,128)(2,1)}, u32[]{:S(2)}) copy-start(bf16[1024,256]{1,0:T(8,128)(2,1)} %get-tuple-element.43) | copy-start | bytes 1572868

commit v3 on v2

--- a/solution.py
+++ b/solution.py
@@ -100,6 +100,11 @@
         table_v=pltpu.VMEM((per_halo, width), BF16),
         gmat_v=pltpu.VMEM((7 * width, width), F32),
         vsum_v=pltpu.VMEM((6 * 8, width), F32),
+        pre_v=pltpu.VMEM((2, z.fwd_rows, width), F32),
+        raw_v=pltpu.VMEM((2, z.fwd_rows, width), F32),
+        upd_v=pltpu.VMEM((2, z.fwd_rows, width), BF16),
+        dout_v=pltpu.VMEM((2, z.bwd_rows, width), BF16),
+        dpre_v=pltpu.VMEM((2, z.bwd_rows, width), BF16),
         edge_sem=pltpu.SemaphoreType.DMA((z.samples,)),
         cot_sem=pltpu.SemaphoreType.DMA((z.samples,)),
         eout_sem=pltpu.SemaphoreType.DMA((z.samples,)),
@@ -217,42 +222,65 @@
                 [high[own], low[own], out_high, out_low, zero], 0
             )
 
-    def forward(i, carry):
-        s, c = i // z.fwd_chunks, i % z.fwd_chunks
-        rows, local = aligned(i, z.fwd_rows), aligned(c, z.fwd_rows)
-
-        @pl.when(c == 0)
-        def _():
-            sample_copy(edge_ref, m.edge_v, m.edge_sem, s).wait()
-
-        edge = m.edge_v[rows, :]
+    per = z.fwd_chunks
+    last = samples * per - 1
+
+    def join_edges(i, slot):
+        s, c = i // per, i % per
+        local = aligned(c, z.fwd_rows)
         own = m.own_v[local, :]
-        left = jnp.concatenate([edge, own, own, m.sel_v[local, :]], 1)
+        left = jnp.concatenate([m.edge_v[aligned(i, z.fwd_rows), :], own, own, m.sel_v[local, :]], 1)
         right = jnp.concatenate(
             [m.half_v[0:width, :], m.pown_v[aligned(s, 2 * nodes), :], m.psel_v[aligned(i, 2 * LANES), :]], 0
         )
-        act, slope = act_and_slope(dot_nn(left, right))
+        m.pre_v[slot] = dot_nn(left, right)
+
+    def activate(i, slot):
+        rows = aligned(i, z.fwd_rows)
+        act, slope = act_and_slope(m.pre_v[slot])
         act = act.astype(BF16)
         m.act_v[rows, :] = act
         m.slope_v[rows, :] = slope
-        centre, inv = centred(dot_nn(act, weight_ref[3 * width : 4 * width, :]))
+        m.raw_v[slot] = dot_nn(act, weight_ref[3 * width : 4 * width, :])
+
+    def update_edges(i, slot):
+        rows, local = aligned(i, z.fwd_rows), aligned(i % per, z.fwd_rows)
+        centre, inv = centred(m.raw_v[slot])
         live = m.live_v[local, :]
         inv = inv * live
         m.inv_v[rows, :] = inv
         normed = centre * both(inv)
         m.norm_v[rows, :] = normed.astype(BF16)
         update = normed * gain_edge + both(live) * shift_edge
-        m.eout_v[rows, :] = (edge.astype(F32) + update).astype(BF16)
-        gathered = dot_nn(m.rep_t[0 : z.fwd_nodes, 0 : z.fwd_rows], update.astype(BF16))
+        m.eout_v[rows, :] = (m.edge_v[rows, :].astype(F32) + update).astype(BF16)
+        m.upd_v[slot] = update.astype(BF16)
+
+    def gather_updates(i, slot):
+        gathered = dot_nn(m.rep_t[0 : z.fwd_nodes, 0 : z.fwd_rows], m.upd_v[slot])
         m.gath_v[aligned(i, z.fwd_nodes), :] = gathered.astype(BF16)
 
-        @pl.when(c == z.fwd_chunks - 1)
-        def _():
-            sample_copy(m.eout_v, eout_ref, m.eout_sem, s).start()
-
+    def edge_in(s):
+        return sample_copy(edge_ref, m.edge_v, m.edge_sem, s)
+
+    edge_in(0).wait()
+    join_edges(0, 0)
+
+    def forward(s, carry):
+        pl.when(s < samples - 1)(lambda: edge_in(s + 1).wait())
+        for c in range(per):
+            i = s * per + c
+            join_edges(jnp.minimum(i + 1, last), (c + 1) % 2)
+            gather_updates(jnp.maximum(i - 2, 0), c % 2)
+            activate(i, c % 2)
+            update_edges(jnp.maximum(i - 1, 0), (c + 1) % 2)
+        pl.when(s > 0)(lambda: sample_copy(m.eout_v, eout_ref, m.eout_sem, s - 1).start())
         return carry
 
-    lax.fori_loop(0, samples * z.fwd_chunks, forward, 0)
+    lax.fori_loop(0, samples, forward, 0)
+    gather_updates(last - 1, 0)
+    update_edges(last, 1)
+    gather_updates(last, 1)
+    sample_copy(m.eout_v, eout_ref, m.eout_sem, samples - 1).start()
 
     def node_part(i, carry):
         rows = aligned(i, 2 * nodes)
@@ -287,39 +315,63 @@
 
     lax.fori_loop(0, samples // 2, node_part, 0)
 
-    def backward(i, carry):
-        s, c = i // z.bwd_chunks, i % z.bwd_chunks
-        rows, local = aligned(i, z.bwd_rows), aligned(c, z.bwd_rows)
-
-        @pl.when(c == 0)
-        def _():
-            sample_copy(cot_ref, m.cot_v, m.cot_sem, s).wait()
-
-        cot = m.cot_v[rows, :].astype(F32)
-        d_update = (cot + dot_nn(m.rep_v[...], m.drep_v[aligned(i, 2 * LANES), :])) * both(m.live_v[local, :])
+    halves = z.bwd_rows // z.fwd_rows
+    pairs = samples * z.bwd_chunks
+
+    def spread_back(i, slot):
+        half = slice((slot % halves) * z.fwd_rows, (slot % halves + 1) * z.fwd_rows)
+        m.pre_v[slot] = dot_nn(m.rep_v[half, :], m.drep_v[aligned(i // halves, 2 * LANES), :])
+
+    def norm_back(i, slot, pair):
+        rows, local = aligned(i, z.fwd_rows), aligned(i % per, z.fwd_rows)
+        d_update = (m.cot_v[rows, :].astype(F32) + m.pre_v[slot]) * both(m.live_v[local, :])
         normed = m.norm_v[rows, :].astype(F32)
         d_normed = d_update * normed
         m.vsum_v[8:16, :] += fold_rows(d_normed)
         m.vsum_v[16:24, :] += fold_rows(d_update)
         scaled, scaled_normed = d_update * gain_edge, d_normed * gain_edge
         d_out = both(m.inv_v[rows, :]) * (scaled - row_mean(scaled) - normed * row_mean(scaled_normed))
-        d_out = d_out.astype(BF16)
-        d_pre = dot_nt(d_out, m.half_v[3 * width : 4 * width, :]) * m.slope_v[rows, :]
-        d_pre = d_pre.astype(BF16)
+        m.dout_v[pair, slot * z.fwd_rows : (slot + 1) * z.fwd_rows, :] = d_out.astype(BF16)
+
+    def activate_back(i, slot, pair):
+        part = slice(slot * z.fwd_rows, (slot + 1) * z.fwd_rows)
+        d_act = dot_nt(m.dout_v[pair, part, :], m.half_v[3 * width : 4 * width, :])
+        m.dpre_v[pair, part, :] = (d_act * m.slope_v[aligned(i, z.fwd_rows), :]).astype(BF16)
+
+    def weights_back(p, pair):
+        s, c = p // z.bwd_chunks, p % z.bwd_chunks
+        rows, local = aligned(p, z.bwd_rows), aligned(c, z.bwd_rows)
+        d_out, d_pre = m.dout_v[pair], m.dpre_v[pair]
         m.gmat_v[3 * width : 4 * width, :] += dot_tn(m.act_v[rows, :], d_out)
         m.gmat_v[0:width, :] += dot_tn(m.edge_v[rows, :], d_pre)
-        m.recv_v[aligned(i, z.bwd_nodes), :] = dot_nn(m.rep_t[...], d_pre)
+        m.recv_v[aligned(p, z.bwd_nodes), :] = dot_nn(m.rep_t[...], d_pre)
         m.aown_v[aligned(s, nodes), :] += dot_nn(m.own_t[:, local], d_pre)
         m.ahalo_v[aligned(s, two_halo), :] += dot_nn(m.halo_t[:, local], d_pre)
-        m.egrad_v[rows, :] = (cot + dot_nt(d_pre, weight_ref[0:width, :])).astype(BF16)
-
-        @pl.when(c == z.bwd_chunks - 1)
-        def _():
-            sample_copy(m.egrad_v, egrad_ref, m.egrad_sem, s).start()
-
+        m.egrad_v[rows, :] = (m.cot_v[rows, :].astype(F32) + dot_nt(d_pre, weight_ref[0:width, :])).astype(BF16)
+
+    m.dout_v[1] = jnp.zeros_like(m.dout_v[1])
+    m.dpre_v[1] = jnp.zeros_like(m.dpre_v[1])
+    spread_back(0, 0)
+
+    def backward(s, carry):
+        sample_copy(cot_ref, m.cot_v, m.cot_sem, s).wait()
+        for k in range(z.bwd_chunks):
+            p = s * z.bwd_chunks + k
+            i = p * halves
+            spread_back(i + 1, 1)
+            activate_back(jnp.maximum(i - 1, 0), 1, 1 - k)
+            norm_back(i, 0, k)
+            weights_back(jnp.maximum(p - 1, 0), 1 - k)
+            spread_back(jnp.minimum(i + 2, last), 0)
+            activate_back(i, 0, k)
+            norm_back(i + 1, 1, k)
+        pl.when(s > 0)(lambda: sample_copy(m.egrad_v, egrad_ref, m.egrad_sem, s - 1).start())
         return carry
 
-    lax.fori_loop(0, samples * z.bwd_chunks, backward, 0)
+    lax.fori_loop(0, samples, backward, 0)
+    activate_back(last, 1, 1)
+    weights_back(pairs - 1, 1)
+    sample_copy(m.egrad_v, egrad_ref, m.egrad_sem, samples - 1).start()
 
     send_full = weight_ref[width : 2 * width, :]
     recv_full = weight_ref[2 * width : 3 * width, :]
@@ -388,6 +440,21 @@
 
 BLOCK = 32
 COUNT = 4
+HALF = LANES // BLOCK
+
+
+def wide_left(value):
+    high, low = split(value)
+    return jnp.concatenate([high, high, low], 1)
+
+
+def wide_right(value):
+    high, low = split(value)
+    return jnp.concatenate([high, low, high], 1)
+
+
+def dot_three(left, right):
+    return dot_nt(wide_left(left), wide_right(right))
 
 
 def factor_block(packed):
@@ -421,75 +488,110 @@
     return jnp.concatenate(inverse, 0)
 
 
-def orthogonalize(work_v, width):
-    per_half = LANES // BLOCK
+def turned_blocks(k, width):
+    return [h * HALF + (g - k) % HALF for h in range(width // LANES) for g in range(HALF)]
+
+
+def pick_rows(value, blocks):
+    return jnp.concatenate([value[i * BLOCK : (i + 1) * BLOCK, :] for i in blocks], 0)
+
+
+def orthogonalize(work_v, bases_out, width, halfway):
+    blocks = width // BLOCK
     group = iota((BLOCK, LANES), 1) // BLOCK
-    for b in range(width // BLOCK):
-        half = b // per_half
-        first = b * BLOCK
-        rows = slice(first, first + BLOCK)
-        lanes = slice(half * LANES, (half + 1) * LANES)
-        place = [(b + k) % COUNT for k in range(COUNT)]
-        packed = work_v[0, rows, lanes]
-        for k in range(1, COUNT):
-            packed = jnp.where(group == place[k], work_v[k, rows, lanes], packed)
-        inverse = factor_block(packed)
-        spread = jnp.concatenate([jnp.where(group == place[k], inverse, 0.0) for k in range(COUNT)], 0)
-        start = (first + BLOCK) // LANES * LANES
-        stack = jnp.concatenate([work_v[(g - b) % COUNT, rows, start:] for g in range(COUNT)], 0)
-        solved = dot_exact(spread, stack, ((1,), (0,)))
+    square = iota((LANES, LANES), 0) // BLOCK == iota((LANES, LANES), 1) // BLOCK
+
+    def placed(values, b):
+        return [jnp.where(group == (b + k) % COUNT, values[k], jnp.zeros_like(values[k])) for k in range(COUNT)]
+
+    def lanes_of(b):
+        return slice(b // HALF * LANES, (b // HALF + 1) * LANES)
+
+    def rows_of(b):
+        return slice(b * BLOCK, (b + 1) * BLOCK)
+
+    packed = sum(placed([work_v[k, rows_of(0), lanes_of(0)] for k in range(COUNT)], 0))
+    for b in range(blocks):
+        if b == blocks // 2:
+            halfway()
+        lanes, after = lanes_of(b), (b + 1) * BLOCK
+        high, low = split(factor_block(packed).astype(F32))
+        high, low = placed([high] * COUNT, b), placed([low] * COUNT, b)
+        if b < blocks - 1:
+            spread_high, spread_low = jnp.concatenate(high, 0), jnp.concatenate(low, 0)
+            spread = jnp.concatenate([spread_high, spread_low, spread_high], 1)
+            ahead = jnp.concatenate([work_v[k, rows_of(b + 1), lanes] for k in range(COUNT)], 0)
+            turned = jnp.where(square, dot_nt(wide_left(ahead), spread), 0.0)
+            order = [(g - b - 1) % COUNT for g in range(COUNT)]
+            update = dot_nt(wide_left(turned), pick_rows(wide_right(turned), order))
+            current = placed([work_v[k, rows_of(b + 1), lanes_of(b + 1)] for k in range(COUNT)], b + 1)
+            packed = sum(current) - sum(update[rows_of(k), :] for k in range(COUNT))
+        start = after // LANES * LANES
         for k in range(COUNT):
-            work_v[k, rows, width:] = solved[k * BLOCK : (k + 1) * BLOCK, width - start :]
-        edges = [first + BLOCK, min(first + 2 * BLOCK, width), width]
-        for low, high in zip(edges[:-1], edges[1:], strict=True):
-            if low >= high:
+            four_high = jnp.concatenate([high[k]] * HALF, 0)
+            four_low = jnp.concatenate([low[k]] * HALF, 0)
+            below = wide_left(work_v[k, after:, lanes])
+            turned = dot_nt(below, jnp.concatenate([four_high, four_low, four_high], 1))
+            mine = iota((width, LANES), 1) // BLOCK == b % HALF
+            bases_out[k, :, lanes] = jnp.where(mine, turned[width - after :, :], bases_out[k, :, lanes])
+            if b == blocks - 1:
                 continue
-            column = iota((high - low, LANES), 1) // BLOCK
-            for k in range(COUNT):
-                turned = dot_exact(work_v[k, low:high, lanes], spread, ((1,), (1,)))
-                turned = jnp.where(column == k, turned, 0.0)
-                work_v[k, low:high, start:] -= dot_exact(turned, solved, ((1,), (0,)))
+            turned_high, turned_low = split(turned)
+            part = iota(turned.shape, 1) // BLOCK
+            zero = jnp.zeros_like(turned_high)
+            left = jnp.where(part == 2, turned_low, jnp.where(part == 3, zero, turned_high))
+            right = jnp.where(part == 1, turned_low, jnp.where(part == 3, zero, turned_high))
+            right = jnp.concatenate(
+                [
+                    right[(i - b - 1) * BLOCK : (i - b) * BLOCK, :] if i > b else zero[0:BLOCK, :]
+                    for i in turned_blocks(k, width)[start // BLOCK :]
+                ],
+                0,
+            )
+            work_v[k, after:, start:] -= dot_nt(left, right)
+
+
+def matrix_bounds(width):
+    return [0, 3 * width, 4 * width, 6 * width, 7 * width]
+
+
+def new_statistics(grad_ref, stat_ref, k):
+    width = stat_ref.shape[-1]
+    bounds = matrix_bounds(width)
+    rows = grad_ref[bounds[k] : bounds[k + 1], :]
+    return BETA_TWO * stat_ref[k] + (1.0 - BETA_TWO) * dot_tn(rows, rows)
 
 
 def matrix_of(row, width):
-    return sum((row >= bound * width).astype(jnp.int32) for bound in (3, 4, 6))
-
-
-def update_kernel(
+    return sum((row >= bound).astype(jnp.int32) for bound in matrix_bounds(width)[1:-1])
+
+
+def adam_kernel(
     grad_ref, gvec_ref, kern_ref, kfirst_ref, ksecond_ref, vec_ref, vfirst_ref, vsecond_ref, stat_ref, bases_ref,
-    kern_out, kfirst_out, ksecond_out, half_out, vec_out, vfirst_out, vsecond_out, stat_out, bases_out, work_v,
+    kern_out, kfirst_out, ksecond_out, half_out, vec_out, vfirst_out, vsecond_out, stat_out,
 ):
     width = stat_ref.shape[-1]
     shard = kern_ref.shape[0]
     correct = 1.0 - BETA_ONE**STEP
     correct_two = 1.0 - BETA_TWO**STEP
-    bounds = [0, 3 * width, 4 * width, 6 * width, 7 * width]
-    half = LANES // BLOCK
-    for k in range(COUNT):
-        rows = grad_ref[bounds[k] : bounds[k + 1], :]
-        stat = BETA_TWO * stat_ref[k] + (1.0 - BETA_TWO) * dot_tn(rows, rows)
-        stat_out[k] = stat
-        turned = dot_exact(bases_ref[k], stat, ((0,), (0,)))
-        order = [h * half + (g - k) % half for h in range(width // LANES) for g in range(half)]
-        moved = jnp.concatenate([turned[i * BLOCK : (i + 1) * BLOCK, :] for i in order], 0)
-        work_v[k, :, 0:width] = dot_exact(turned, moved, ((1,), (1,)))
-        work_v[k, :, width:] = turned
-
     first_row = lax.axis_index("fs") * shard
-    grad = grad_ref[pl.ds(pl.multiple_of(first_row, 64), shard), :].astype(F32)
+    grad = grad_ref[pl.ds(pl.multiple_of(first_row, 64), shard), :]
     one = matrix_of(first_row, width)
     two = matrix_of(first_row + shard - 1, width)
     in_two = matrix_of(first_row + iota((shard, width), 0), width) != one
     basis_one, basis_two = bases_ref[one], bases_ref[two]
-    rotated = jnp.where(
-        in_two, dot_exact(grad, basis_two, ((1,), (0,))), dot_exact(grad, basis_one, ((1,), (0,)))
-    )
+
+    def turn(basis):
+        high, low = split(basis)
+        return dot_nn(grad, high) + dot_nn(grad, low)
+
+    rotated = jnp.where(in_two, turn(basis_two), turn(basis_one))
     first_new = BETA_ONE * kfirst_ref[...] + (1.0 - BETA_ONE) * rotated
     second_new = BETA_TWO * ksecond_ref[...] + (1.0 - BETA_TWO) * rotated * rotated
     kfirst_out[...] = first_new
     ksecond_out[...] = second_new
     step = first_new / correct / (jnp.sqrt(second_new / correct_two) + ADAM_EPS)
-    turned = jnp.where(in_two, dot_exact(step, basis_two, ((1,), (1,))), dot_exact(step, basis_one, ((1,), (1,))))
+    turned = jnp.where(in_two, dot_three(step, basis_two), dot_three(step, basis_one))
     kern = kern_ref[...]
     kern_new = kern - RATE_MATRIX * (turned + DECAY_RATE * kern)
     kern_out[...] = kern_new
@@ -500,27 +602,36 @@
     vfirst_out[...] = first_new
     vsecond_out[...] = second_new
     vec_out[...] = vec_ref[...] - RATE_VECTOR * (first_new / correct) / (jnp.sqrt(second_new / correct_two) + ADAM_EPS)
-
-    orthogonalize(work_v, width)
     for k in range(COUNT):
-        bases_out[k] = work_v[k, :, width:].T
-
-
-def update_call(grad, gvec, kern, kfirst, ksecond, vec, vfirst, vsecond, stat, bases):
+        stat_out[k] = new_statistics(grad_ref, stat_ref, k)
+
+
+def adam_call(grad, gvec, kern, kfirst, ksecond, vec, vfirst, vsecond, stat, bases):
     shard, width = kern.shape
     whole = pl.BlockSpec(memory_space=pltpu.VMEM)
     rows = jax.ShapeDtypeStruct((shard, width), F32)
     six = jax.ShapeDtypeStruct(vec.shape, F32)
-    square = jax.ShapeDtypeStruct(stat.shape, F32)
     return pl.pallas_call(
-        update_kernel,
-        out_shape=(rows, rows, rows, jax.ShapeDtypeStruct((shard, width), BF16), six, six, six, square, square),
+        adam_kernel,
+        out_shape=(
+            rows, rows, rows, jax.ShapeDtypeStruct((shard, width), BF16), six, six, six,
+            jax.ShapeDtypeStruct(stat.shape, F32),
+        ),
         in_specs=[whole] * 10,
-        out_specs=(whole,) * 9,
-        scratch_shapes=[pltpu.VMEM((COUNT, width, 2 * width), F32)],
+        out_specs=(whole,) * 8,
         compiler_params=pltpu.CompilerParams(vmem_limit_bytes=VMEM_LIMIT),
-        name="update",
+        name="adam",
     )(grad, gvec, kern, kfirst, ksecond, vec, vfirst, vsecond, stat, bases)
+
+
+def prepare_bases(stat_ref, bases_ref, work_v, width):
+    for k in range(COUNT):
+        order = turned_blocks(k, width)
+        stat = stat_ref[k]
+        flipped = bases_ref[k].T
+        proj_rows = dot_three(flipped, stat)
+        work_v[k, 0:width, :] = dot_three(proj_rows, pick_rows(proj_rows, order))
+        work_v[k, width:, :] = dot_three(stat, pick_rows(flipped, order))
 
 
 MESH = pl.DeviceIdType.MESH
@@ -566,10 +677,12 @@
         for part in range(self.PARTS):
             self.copy(self.fs, part, 1, self.next).start()
 
-    def finish(self):
+    def forward(self):
         for part in range(self.PARTS):
             self.copy(self.fs, part, 0, self.far).wait_recv()
             self.copy(self.fs ^ 2, part, 2, self.next).start()
+
+    def finish(self):
         for part in range(self.PARTS):
             self.copy(self.fs, part, 0, self.far).wait_send()
             self.copy(self.fs, part, 1, self.next).wait()
@@ -605,6 +718,7 @@
             ).astype(BF16)
     for side, (other, exists) in enumerate(around):
         pl.when(exists)(lambda side=side, other=other: send(list_v.at[side], halo_v.at[1 - side], halo_sems, side, (fs, other)).start())
+    gather.forward()
     gather.finish()
     out = pltpu.make_async_copy(rows_v, rows_out, out_sem)
     out.start()
@@ -643,136 +757,222 @@
     )(kern, node, send_rows)
 
 
-def reduce_plan(rows, fs_count, node_count):
-    bits = [("fs", b) for b in range(fs_count.bit_length() - 1)] + [
-        ("nodes", b) for b in range(node_count.bit_length() - 1)
-    ]
-    steps = []
-    for i, (axis, bit) in enumerate(bits):
-        halved = rows % 32 == 0 and i < len(bits) - 1
-        rows = rows // 2 if halved else rows
-        steps.append((axis, bit, rows, halved))
-    return steps
+class Cube:
+    def __init__(self, count, fs=None, node=None):
+        bits = count.bit_length() - 1
+        self.node_bits = min(2, bits)
+        self.size = 2 << self.node_bits
+        self.extra = list(range(self.node_bits, bits))
+        self.fs, self.node = fs, node
+        if fs is not None:
+            self.me = (fs >> 1) + 2 * (node & ((1 << self.node_bits) - 1))
+        self.far_first = sorted(range(1, self.size), key=lambda r: (-r.bit_count(), -r))
+
+    def device(self, r):
+        return self.fs ^ (2 * (r & 1)), self.node ^ (r >> 1)
+
+    def over(self, bit):
+        return self.fs, self.node ^ (1 << bit)
+
+
+def tree_sum(parts):
+    while len(parts) > 1:
+        parts = [left + right for left, right in zip(parts[::2], parts[1::2], strict=True)]
+    return parts[0]
 
 
 def reduce_kernel(
-    samples, plan, count, grad_ref, gvec_ref, border_ref, total_ref, send_ref,
-    grad_out, gvec_out, node_out, sum_v, out_v, land_v, send_v, vland_v, vsend_v, ret_v, sems, vsems, halo_sems, out_sem,
+    samples, count, grad_ref, gvec_ref, border_ref, total_ref, send_ref,
+    grad_out, gvec_out, node_out, half_v, land_v, sum_v, cube_v, extra_v, out_v, total_v, vsend_v, vland_v, ret_v,
+    core_sems, cube_sems, extra_sems, back_sems, last_sems, vec_sems, halo_sems, local_sems,
 ):
     fs, node = lax.axis_index("fs"), lax.axis_index("nodes")
+    cube = Cube(count, fs, node)
     nodes = total_ref.shape[0] // samples
     halo = send_ref.shape[1]
-    width = grad_ref.shape[1]
+    rows = grad_ref.shape[0] // 2
+    size = rows // cube.size
     around = sides(node, count)
-
-    def partner(axis, bit):
-        return (fs ^ (1 << bit), node) if axis == "fs" else (fs, node ^ (1 << bit))
-
+    twin = (fs ^ 1, node)
+    keep, give = (fs & 1) * rows, (1 - (fs & 1)) * rows
+
+    def chunk(ref, r, base=0):
+        return ref.at[pl.ds(pl.multiple_of(base + (cube.me ^ r) * size, 16), size)]
+
+    mine = pltpu.make_async_copy(grad_ref.at[pl.ds(pl.multiple_of(keep, 16), rows)], half_v, local_sems.at[0])
+    mine.start()
+    fetch_total = pltpu.make_async_copy(total_ref, total_v, local_sems.at[1])
+    fetch_total.start()
     ret_v[...] = jnp.zeros_like(ret_v)
+    vsend_v[0] = gvec_ref[...]
     greet(
-        [(partner(axis, bit), None) for axis, bit, _, _ in plan] + [((fs, other), exists) for other, exists in around]
+        [(twin, None)]
+        + [(cube.device(r), None) for r in range(1, cube.size)]
+        + [(cube.over(bit), None) for bit in cube.extra]
+        + [((fs, other), exists) for other, exists in around]
     )
 
     def give_back(side, other):
         return send(border_ref.at[side], ret_v.at[1 - side], halo_sems, side, (fs, other))
 
+    started = []
+
+    def begin(copy):
+        copy.start()
+        started.append(copy)
+        return copy
+
+    order = cube.far_first + [0]
+    core = {r: begin(send(chunk(grad_ref, r, give), chunk(land_v, r), core_sems, r, twin)) for r in order}
+    vec = begin(send(vsend_v.at[0], vland_v.at[0], vec_sems, 0, twin))
     for side, (other, exists) in enumerate(around):
         pl.when(exists)(lambda side=side, other=other: give_back(side, other).start())
-
-    first, place, copies, regions = 0, 0, [], []
-    vsum = gvec_ref[...]
-    for i, (axis, bit, rows, halved) in enumerate(plan):
-        mine = ((fs if axis == "fs" else node) >> bit) & 1
-        keep = pl.multiple_of(first + mine * rows, 16) if halved else first
-        give = pl.multiple_of(first + (1 - mine) * rows, 16) if halved else first
-        if i == 0:
-            source = grad_ref.at[pl.ds(give, rows)]
-        else:
-            source = send_v.at[pl.ds(place, rows)]
-            source[...] = sum_v[pl.ds(give, rows), :].astype(BF16)
-        copy = send(source, land_v.at[pl.ds(place, rows)], sems, i, partner(axis, bit))
-        copy.start()
-        vsend_v[i] = vsum
-        vcopy = send(vsend_v.at[i], vland_v.at[i], vsems, i, partner(axis, bit))
-        vcopy.start()
+    mine.wait()
+    spread, total = {}, None
+    for r in order:
+        core[r].wait_recv()
+        total = chunk(half_v, r)[...].astype(F32) + chunk(land_v, r)[...].astype(F32)
+        if r:
+            chunk(sum_v, r)[...] = total.astype(BF16)
+            spread[r] = begin(send(chunk(sum_v, r), cube_v.at[r], cube_sems, r, cube.device(r)))
+    vec.wait_recv()
+    vsum = vsend_v[0] + vland_v[0]
+    vsend_v[1] = vsum
+    vec = {r: begin(send(vsend_v.at[1], vland_v.at[r], vec_sems, r, cube.device(r))) for r in range(1, cube.size)}
+    for r in reversed(cube.far_first):
+        spread[r].wait_recv()
+        total = total + cube_v[r].astype(F32)
+    for copy in vec.values():
         copy.wait_recv()
-        held = grad_ref if i == 0 else sum_v if halved else send_v
-        own = keep if i == 0 or halved else place
-        total = held[pl.ds(own, rows), :].astype(F32) + land_v[pl.ds(place, rows), :].astype(F32)
-        if i == len(plan) - 1:
-            out_v[pl.ds(keep, rows), :] = total.astype(BF16)
-        else:
-            sum_v[pl.ds(keep, rows), :] = total
+    vsum = tree_sum([vsum] + [vland_v[r] for r in range(1, cube.size)])
+    for e, bit in enumerate(cube.extra):
+        extra_v[2 * e] = total.astype(BF16)
+        vsend_v[2 + e] = vsum
+        copy = begin(send(extra_v.at[2 * e], extra_v.at[2 * e + 1], extra_sems, e, cube.over(bit)))
+        slot = cube.size + e
+        vcopy = begin(send(vsend_v.at[2 + e], vland_v.at[slot], vec_sems, slot, cube.over(bit)))
+        copy.wait_recv()
+        total = extra_v[2 * e].astype(F32) + extra_v[2 * e + 1].astype(F32)
         vcopy.wait_recv()
-        vsum = vsum + vland_v[i]
-        copies += [copy, vcopy]
-        regions.append((axis, bit, rows, halved, keep))
-        first, place = keep, place + rows
+        vsum = vsum + vland_v[slot]
+    own = chunk(out_v, 0, keep)
+    own[...] = total.astype(BF16)
+    back = {r: begin(send(own, own, back_sems, r, cube.device(r))) for r in cube.far_first}
+    last = {0: begin(send(own, own, last_sems, 0, twin))}
+    gvec_out[...] = vsum
     for side, (other, exists) in enumerate(around):
         def settle(side=side, other=other):
             give_back(side, other).wait_send()
             give_back(1 - side, other).wait_recv()
         pl.when(exists)(settle)
-    slot = len(plan)
-    for axis, bit, rows, halved, keep in reversed(regions):
-        if not halved:
-            continue
-        region = out_v.at[pl.ds(keep, rows)]
-        copy = send(region, region, sems, slot, partner(axis, bit))
-        copy.start()
-        copies.append(copy)
-        slot += 1
-        if axis == "fs" and bit == 0:
-            low, high = (list_matrix(send_ref, side, nodes) for side in range(2))
-            for s in range(samples):
-                rows_s = slice(s * nodes, (s + 1) * nodes)
-                part = slice(s * halo, (s + 1) * halo)
-                node_out[rows_s, :] = (
-                    total_ref[rows_s, :] + dot_nn(low, ret_v[0, part, :]) + dot_nn(high, ret_v[1, part, :])
-                ).astype(BF16)
-            gvec_out[...] = vsum
+    fetch_total.wait()
+    low, high = (list_matrix(send_ref, side, nodes) for side in range(2))
+    for s in range(samples):
+        rows_s = slice(s * nodes, (s + 1) * nodes)
+        part = slice(s * halo, (s + 1) * halo)
+        node_out[rows_s, :] = (
+            total_v[rows_s, :] + dot_nn(low, ret_v[0, part, :]) + dot_nn(high, ret_v[1, part, :])
+        ).astype(BF16)
+    for r in reversed(cube.far_first):
+        back[r].wait_recv()
+        part = chunk(out_v, r, keep)
+        last[r] = begin(send(part, part, last_sems, r, twin))
+    out = pltpu.make_async_copy(
+        out_v.at[pl.ds(pl.multiple_of(keep, 16), rows)], grad_out.at[pl.ds(pl.multiple_of(keep, 16), rows)], local_sems.at[0]
+    )
+    out.start()
+    for copy in last.values():
         copy.wait_recv()
-    out = pltpu.make_async_copy(out_v, grad_out, out_sem)
-    out.start()
-    for copy in copies:
+    rest = pltpu.make_async_copy(
+        out_v.at[pl.ds(pl.multiple_of(give, 16), rows)], grad_out.at[pl.ds(pl.multiple_of(give, 16), rows)], local_sems.at[1]
+    )
+    rest.start()
+    for copy in started:
         copy.wait_send()
     out.wait()
+    rest.wait()
 
 
 def reduce_call(grad, gvec, border, total, send_rows, samples):
     rows, width = grad.shape
     count = lax.axis_size("nodes")
-    plan = reduce_plan(rows, lax.axis_size("fs"), count)
-    landing = sum(step[2] for step in plan)
-    gathers = sum(step[3] for step in plan)
+    cube = Cube(count)
+    extra = len(cube.extra)
+    half, size = rows // 2, rows // 2 // cube.size
     whole, anywhere = pl.BlockSpec(memory_space=pltpu.VMEM), pl.BlockSpec(memory_space=pl.ANY)
     return pl.pallas_call(
-        partial(reduce_kernel, samples, plan, count),
+        partial(reduce_kernel, samples, count),
         out_shape=(
             jax.ShapeDtypeStruct(grad.shape, BF16),
             jax.ShapeDtypeStruct(gvec.shape, F32),
             jax.ShapeDtypeStruct(total.shape, BF16),
         ),
-        in_specs=[whole] * 5,
+        in_specs=[anywhere, whole, whole, anywhere, whole],
         out_specs=(anywhere, whole, whole),
         scratch_shapes=[
-            pltpu.VMEM((rows, width), F32),
+            pltpu.VMEM((half, width), BF16),
+            pltpu.VMEM((half, width), BF16),
+            pltpu.VMEM((half, width), BF16),
+            pltpu.VMEM((cube.size, size, width), BF16),
+            pltpu.VMEM((max(2 * extra, 1), size, width), BF16),
             pltpu.VMEM((rows, width), BF16),
-            pltpu.VMEM((landing, width), BF16),
-            pltpu.VMEM((landing, width), BF16),
-            pltpu.VMEM((len(plan),) + gvec.shape, F32),
-            pltpu.VMEM((len(plan),) + gvec.shape, F32),
+            pltpu.VMEM(total.shape, F32),
+            pltpu.VMEM((2 + extra,) + gvec.shape, F32),
+            pltpu.VMEM((cube.size + extra,) + gvec.shape, F32),
             pltpu.VMEM(border.shape, BF16),
-            pltpu.SemaphoreType.DMA((2, len(plan) + gathers)),
-            pltpu.SemaphoreType.DMA((2, len(plan))),
+            pltpu.SemaphoreType.DMA((2, cube.size)),
+            pltpu.SemaphoreType.DMA((2, cube.size)),
+            pltpu.SemaphoreType.DMA((2, max(extra, 1))),
+            pltpu.SemaphoreType.DMA((2, cube.size)),
+            pltpu.SemaphoreType.DMA((2, cube.size)),
+            pltpu.SemaphoreType.DMA((2, cube.size + extra)),
             pltpu.SemaphoreType.DMA((2, 2)),
-            pltpu.SemaphoreType.DMA,
+            pltpu.SemaphoreType.DMA((2,)),
         ],
         compiler_params=pltpu.CompilerParams(
             collective_id=1, has_side_effects=True, vmem_limit_bytes=VMEM_LIMIT
         ),
         name="reduce",
     )(grad, gvec, border, total, send_rows)
+
+
+def finish_kernel(half_ref, stat_ref, bases_ref, bases_out, rows_out, work_v, rows_v, sems, out_sem):
+    fs, node = lax.axis_index("fs"), lax.axis_index("nodes")
+    shard = half_ref.shape[0]
+    width = stat_ref.shape[-1]
+    gather = Gather(rows_v, sems, shard, fs, node)
+    rows_v[pl.ds(pl.multiple_of(fs * shard, 16), shard), :] = half_ref[...]
+    greet([(gather.next, None), (gather.far, None)])
+    gather.start()
+    prepare_bases(stat_ref, bases_ref, work_v, width)
+    bases_out[...] = jnp.zeros_like(bases_out)
+    orthogonalize(work_v, bases_out, width, gather.forward)
+    gather.finish()
+    out = pltpu.make_async_copy(rows_v, rows_out, out_sem)
+    out.start()
+    out.wait()
+
+
+def finish_call(half, stat, bases):
+    shard, width = half.shape
+    whole, anywhere = pl.BlockSpec(memory_space=pltpu.VMEM), pl.BlockSpec(memory_space=pl.ANY)
+    total = lax.axis_size("fs") * shard
+    return pl.pallas_call(
+        finish_kernel,
+        out_shape=(jax.ShapeDtypeStruct(stat.shape, F32), jax.ShapeDtypeStruct((total, width), BF16)),
+        in_specs=[whole] * 3,
+        out_specs=(whole, anywhere),
+        scratch_shapes=[
+            pltpu.VMEM((COUNT, 2 * width, width), F32),
+            pltpu.VMEM((total, width), BF16),
+            pltpu.SemaphoreType.DMA((2, 3 * Gather.PARTS)),
+            pltpu.SemaphoreType.DMA,
+        ],
+        compiler_params=pltpu.CompilerParams(
+            collective_id=2, has_side_effects=True, vmem_limit_bytes=VMEM_LIMIT
+        ),
+        name="finish",
+    )(half, stat, bases)
 
 
 def on_device(
@@ -797,10 +997,10 @@
         vectors,
     )
     grad, gvec, node_grad = reduce_call(grad, gvec, border, node_total, send_rows, samples)
-    kernel_new, first_new, second_new, half, vec_new, vfirst_new, vsecond_new, stat_new, bases_new = update_call(
+    kernel_new, first_new, second_new, half, vec_new, vfirst_new, vsecond_new, stat_new = adam_call(
         grad, gvec, kernels, kernel_first, kernel_second, vectors, vector_first, vector_second, statistics, bases
     )
-    weights_half = lax.all_gather(half, "fs", axis=0, tiled=True)
+    bases_new, weights_half = finish_call(half, stat_new, bases)
     return (
         edge_out.reshape(edge_latent.shape),
         node_out.reshape(node_latent.shape),

time: 129 us -> 96 us (0.74)
  Pallas kernels: 115 us -> 89.7 us
  blocking collectives: 9.93 us -> 0 us
  local copies, waits for them, and re-layouts: 3.02 us -> 5.31 us
    pallas_call x2 -> x3, Pallas kernels: 67.9 us -> 51.6 us  [the longest x1 28.5 us: reduce_call(): pl.pallas_call(partial(reduce_kernel, samples, count), out_shape=(jax.Sha...]
    all_gather x1 -> x0, blocking collectives: 9.93 us -> none  [on_device(): weights_half = lax.all_gather(half, 'fs', axis=0, tiled=True)]
    pallas_call x1, Pallas kernels: 33.5 us -> 24.3 us  [main_call(): pl.pallas_call(partial(main_kernel, z, tuple(scratch)), out_shape=(jax.Sh...]
    unnamed x4 -> x7, local copies, waits for them, and re-layouts: 1.72 us -> 4.01 us
where the time goes in v3:
time: 96 us; the launch traced here: 95.7 us
  Pallas kernels  89.7 us (93%)
  local copies, waits for them, and re-layouts  5.31 us (6%)
    pallas_call x1, Pallas kernels, reduce_call(): pl.pallas_call(partial(reduce_kernel, samples, count), out_shape=(jax.Sha...  28.5 us
    pallas_call x1, Pallas kernels, main_call(): pl.pallas_call(partial(main_kernel, z, tuple(scratch)), out_shape=(jax.Sh...  24.3 us
    pallas_call x1, Pallas kernels, finish_call(): pl.pallas_call(finish_kernel, out_shape=(jax.ShapeDtypeStruct(stat.shape,...  18.4 us
    pallas_call x1, Pallas kernels, fetch_call(): pl.pallas_call(partial(fetch_kernel, samples, lax.axis_size('nodes')), ou...  13.7 us
    pallas_call x1, Pallas kernels, adam_call(): pl.pallas_call(adam_kernel, out_shape=(rows, rows, rows, jax.ShapeDtypeSt...  4.75 us
    unnamed x7, local copies, waits for them, and re-layouts  4.01 us

profile of v3, /device:TPU:0, one launch (start us, length us, event | category | flops | bytes accessed | tf_op | source)
XLA Modules:
  0.0 95.7 jit_solution(13648469479985940888)
XLA Ops:
  0.6 1.3 %reshape.62.send_ref = s32[1,1536]{1,0:T(1,128)} reshape(s32[1536]{0:T(1024)} %param.20) | data formatting | bytes 12288 | tf_op jit(solution)/shard_map/reshape | solution.py:994
  1.9 13.7 %fetch.1 = (bf16[1792,256]{1,0:T(8,128)(2,1)}, bf16[2,64,256]{2,1,0:T(8,128)(2,1)}) custom-call(f32[448,256]{1,0:T(8,128)} %kern_ref.3, bf16[1024,256]{1,0:T(8,128)(2,1)} %bitcast.11, s32[2,16]{1,0:T(2,128)} %send_ref.3), custom_call_target="tpu_custom_call" | custom-call | tf_op jit(solution)/shard_map/fetch/pallas_call | solution.py:740
  15.7 24.3 %edge_node_round.1 = (bf16[6144,256]{1,0:T(8,128)(2,1)}, bf16[6144,256]{1,0:T(8,128)(2,1)}, bf16[1024,256]{1,0:T(8,128)(2,1)}, f32[1024,256]{1,0:T(8,128)}, bf16...) custom-call(bf16[6144,256]{1,0:T(8,128)(2,1)} %bitcast.9, bf16[6144,256]{1,0:T(8,128)(2,1)} %bitcast.10, ...), custom_call_target="tpu_custom_call" | custom-call | tf_op jit(solution)/shard_map/edge_node_round/pallas_call | solution.py:418
  40.0 28.5 %reduce.1 = (bf16[1792,256]{1,0:T(8,128)(2,1)}, f32[8,256]{1,0:T(8,128)}, bf16[1024,256]{1,0:T(8,128)(2,1)}) custom-call(bf16[1792,256]{1,0:T(8,128)(2,1)} %get-tuple-element.40.grad_ref, f32[8,256]{1,0:T(8,128)} %get-tuple-element.41.gvec_ref, bf16[2,64,256]{2,1,0:T(8,128)(2,1)} %get-tuple-element.42.border_ref, f32[1024,256]{1,0:T(8,128)} %get-tuple-element.43.total_ref, ...), custom_call_target="tpu_custom_call" | custom-call | tf_op jit(solution)/shard_map/reduce/pallas_call | solution.py:903
  68.5 0.0 copy-start.1
  68.5 4.7 %adam.1 = (f32[448,256]{1,0:T(8,128)}, f32[448,256]{1,0:T(8,128)}, f32[448,256]{1,0:T(8,128)}, bf16[448,256]{1,0:T(8,128)(2,1)}, f32[6,256]{1,0:T(8,128)}, /*ind...) custom-call(bf16[1792,256]{1,0:T(8,128)(2,1)} %get-tuple-element.45.grad_ref, ...), custom_call_target="tpu_custom_call" | custom-call | tf_op jit(solution)/shard_map/adam/pallas_call | solution.py:614
  73.3 18.4 %finish.1 = (f32[4,256,256]{2,1,0:T(8,128)}, bf16[1792,256]{1,0:T(8,128)(2,1)}) custom-call(bf16[448,256]{1,0:T(8,128)(2,1)} %get-tuple-element.54.half_ref, f32[4,256,256]{2,1,0:T(8,128)} %get-tuple-element.80.stat_ref, f32[4,256,256]{2,1,0:T(8,128)} %bases_ref.3), custom_call_target="tpu_custom_call" | custom-call | tf_op jit(solution)/shard_map/finish/pallas_call | solution.py:960
  91.7 0.0 copy-start
  91.7 0.0 copy-done.1
  91.7 0.8 copy.31
  92.5 2.3 %copy.32 = f32[4,256,256]{2,1,0:T(8,128)} copy(f32[4,256,256]{2,1,0:T(8,128)} %get-tuple-element.81) | data formatting | bytes 2097152
  94.8 0.0 copy-done
  94.8 0.9 copy.33
Async XLA Ops:
  68.5 23.2 %copy-start.1 = (bf16[1024,256]{1,0:T(8,128)(2,1)S(1)}, bf16[1024,256]{1,0:T(8,128)(2,1)}, u32[]{:S(2)}) copy-start(bf16[1024,256]{1,0:T(8,128)(2,1)} %get-tuple-element.44) | copy-start | bytes 1572868
  91.7 3.1 %copy-start = (bf16[1792,256]{1,0:T(8,128)(2,1)S(1)}, bf16[1792,256]{1,0:T(8,128)(2,1)}, u32[]{:S(2)}) copy-start(bf16[1792,256]{1,0:T(8,128)(2,1)} %get-tuple-element.82) | copy-start | bytes 2752516

commit v4 on v1

v4 whole, which is shorter than its diff:
```python
from functools import partial

import jax
import jax.numpy as jnp
from jax import lax
from jax.experimental import pallas as pl
from jax.experimental.pallas import tpu as pltpu
from jax.sharding import PartitionSpec as P

STEP = 5

NORM_EPS = 1e-05
BETA_ONE = 0.5
BETA_TWO = 0.5
RATE_MATRIX = 0.05
RATE_VECTOR = 0.2
DECAY_RATE = 0.01
ADAM_EPS = 1e-08
HIGH = lax.Precision.HIGHEST
F32 = jnp.float32
BF16 = jnp.bfloat16
LANES = 128
VMEM_LIMIT = 56 * 1024 * 1024


def dot_nn(left, right):
    return lax.dot_general(left, right, (((1,), (0,)), ((), ())), preferred_element_type=F32)


def dot_nt(left, right):
    return lax.dot_general(left, right, (((1,), (1,)), ((), ())), preferred_element_type=F32)


def dot_tn(left, right):
    return lax.dot_general(left, right, (((0,), (0,)), ((), ())), preferred_element_type=F32)


def split(value):
    high = value.astype(BF16)
    return high, (value - high.astype(F32)).astype(BF16)


def iota(shape, dim):
    return lax.broadcasted_iota(jnp.int32, shape, dim)


def ones_where(mask):
    return jnp.where(mask, 1.0, 0.0).astype(BF16)


def fold_rows(value):
    rows, width = value.shape
    return jnp.sum(value.reshape(rows // 8, 8, width), 0)


def aligned(index, step):
    return pl.ds(pl.multiple_of(index * step, step), step)


class Sizes:
    def __init__(self, samples, nodes, slots, halo, width):
        self.samples, self.nodes, self.slots = samples, nodes, slots
        self.halo, self.width = halo, width
        self.edges = nodes * slots
        self.fwd_nodes, self.bwd_nodes = 64, 128
        self.fwd_rows = self.fwd_nodes * slots
        self.bwd_rows = self.bwd_nodes * slots
        self.fwd_chunks = nodes // self.fwd_nodes
        self.bwd_chunks = nodes // self.bwd_nodes


def main_scratch(z, shard):
    rows, width = z.samples * z.edges, z.width
    per_node = z.samples * z.nodes
    per_halo = z.samples * 2 * z.halo
    return dict(
        edge_v=pltpu.VMEM((rows, width), BF16),
        cot_v=pltpu.VMEM((rows, width), BF16),
        edge_out_v=pltpu.VMEM((rows, width), BF16),
        act_v=pltpu.VMEM((rows, width), BF16),
        slope_v=pltpu.VMEM((rows, width), F32),
        norm_v=pltpu.VMEM((rows, width), BF16),
        inv_v=pltpu.VMEM((rows, LANES), F32),
        own_v=pltpu.VMEM((z.edges, z.nodes), BF16),
        own_t=pltpu.VMEM((z.nodes, z.edges), BF16),
        halo_t=pltpu.VMEM((2 * z.halo, z.edges), BF16),
        sel_v=pltpu.VMEM((z.edges, 2 * LANES), BF16),
        rep_v=pltpu.VMEM((z.bwd_rows, 2 * LANES), BF16),
        rep_t=pltpu.VMEM((LANES, z.bwd_rows), BF16),
        live_v=pltpu.VMEM((z.edges, LANES), F32),
        half_v=pltpu.VMEM((7 * width, width), BF16),
        pown_v=pltpu.VMEM((z.samples * 2 * z.nodes, width), BF16),
        psel_v=pltpu.VMEM((z.samples * z.fwd_chunks * 2 * LANES, width), BF16),
        gath_v=pltpu.VMEM((per_node, width), BF16),
        drep_v=pltpu.VMEM((z.samples * z.bwd_chunks * 2 * LANES, width), BF16),
        recv_v=pltpu.VMEM((per_node, width), F32),
        aown_v=pltpu.VMEM((per_node, width), F32),
        ahalo_v=pltpu.VMEM((per_halo, width), F32),
        table_v=pltpu.VMEM((per_halo, width), BF16),
        gmat_v=pltpu.VMEM((7 * width, width), F32),
        vsum_v=pltpu.VMEM((6 * 8, width), F32),
        pre_v=pltpu.VMEM((2, z.fwd_rows, width), F32),
        raw_v=pltpu.VMEM((2, z.fwd_rows, width), F32),
        upd_v=pltpu.VMEM((2, z.fwd_rows, width), BF16),
        dout_v=pltpu.VMEM((2, z.bwd_rows, width), BF16),
        dpre_v=pltpu.VMEM((2, z.bwd_rows, width), BF16),
        ncot_v=pltpu.VMEM((per_node, width), BF16),
        total_v=pltpu.VMEM((per_node, width), F32),
        rows_v=pltpu.VMEM((7 * width, width), BF16),
        first_v=pltpu.VMEM((7 * width, width), BF16),
        second_v=pltpu.VMEM((7 * width, width), BF16),
        mom_v=pltpu.VMEM((2, shard, width), F32),
        list_v=pltpu.VMEM((2, z.samples * z.halo, width), BF16),
        halo_v=pltpu.VMEM((2, z.samples * z.halo, width), BF16),
        border_v=pltpu.VMEM((2, z.samples * z.halo, width), BF16),
        ret_v=pltpu.VMEM((2, z.samples * z.halo, width), BF16),
        gout_v=pltpu.VMEM((7 * width, width), BF16),
        edge_sem=pltpu.SemaphoreType.DMA((z.samples,)),
        cot_sem=pltpu.SemaphoreType.DMA((z.samples,)),
        eout_sem=pltpu.SemaphoreType.DMA((z.samples,)),
        egrad_sem=pltpu.SemaphoreType.DMA((z.samples,)),
        local_sem=pltpu.SemaphoreType.DMA((8,)),
        rows_sem=pltpu.SemaphoreType.DMA((2, 12)),
        first_sem=pltpu.SemaphoreType.DMA((2, 3)),
        second_sem=pltpu.SemaphoreType.DMA((2, 3)),
        halo_sem=pltpu.SemaphoreType.DMA((2, 2)),
        ret_sem=pltpu.SemaphoreType.DMA((2, 2)),
    )


def build_selectors(z, m, five_ref, send_ref):
    halo, nodes, slots = z.halo, z.nodes, z.slots
    lane = iota((LANES, LANES), 1)
    row = iota((LANES, LANES), 0)
    for g in range(z.edges // LANES):
        rows = slice(g * LANES, (g + 1) * LANES)
        line = jnp.broadcast_to(send_ref[:, rows].astype(F32), (LANES, LANES))
        column = line.T.astype(jnp.int32)
        for h in range(nodes // LANES):
            m.own_v[rows, h * LANES : (h + 1) * LANES] = ones_where(column == lane + (halo + h * LANES))
        place = jnp.where(column < halo, column, jnp.where(column >= halo + nodes, column - nodes, -1))
        in_halo = (place == (lane & (2 * halo - 1))) & (lane < 4 * halo)
        first = slots * (lane & (z.fwd_nodes - 1))
        local = row + (g * LANES) % z.fwd_rows
        m.sel_v[rows, 0:LANES] = ones_where((first <= local) & (local < first + slots))
        m.sel_v[rows, LANES : 2 * LANES] = ones_where(in_halo)
    senders = jnp.broadcast_to(send_ref[...], (8, z.edges))
    for i in range(nodes // 16):
        node = iota((16, z.edges), 0) + (halo + i * 16)
        m.own_t[i * 16 : (i + 1) * 16, :] = ones_where(jnp.broadcast_to(senders[0:1], (16, z.edges)) == node)
    wide = jnp.broadcast_to(senders[0:1], (2 * halo, z.edges))
    node = iota((2 * halo, z.edges), 0)
    node = jnp.where(node < halo, node, node + nodes)
    m.halo_t[...] = ones_where(wide == node)
    first = slots * (iota((z.bwd_rows, 2 * LANES), 1) & (LANES - 1))
    local = iota((z.bwd_rows, 2 * LANES), 0)
    rep = ones_where((first <= local) & (local < first + slots))
    m.rep_v[...] = rep
    first = slots * iota((LANES, z.bwd_rows), 0)
    local = iota((LANES, z.bwd_rows), 1)
    m.rep_t[...] = ones_where((first <= local) & (local < first + slots))
    local = iota((z.bwd_rows, LANES), 0).astype(F32)
    slot = local - slots * jnp.floor((local + 0.5) * (1.0 / slots))
    for h in range(nodes // LANES):
        five = jnp.broadcast_to(five_ref[:, h * LANES : (h + 1) * LANES].astype(F32), (LANES, LANES)).T
        spread = dot_nn(rep[:, :LANES], five.astype(BF16))
        m.live_v[h * z.bwd_rows : (h + 1) * z.bwd_rows, :] = jnp.where(slot < slots - spread, 1.0, 0.0)


def both(column):
    return jnp.concatenate([column, column], 1)


def row_mean(value):
    return jnp.sum(value, -1, keepdims=True) * (1.0 / value.shape[-1])


def centred(value):
    centre = value - row_mean(value)
    return centre, lax.rsqrt(row_mean(centre * centre) + NORM_EPS)


def act_and_slope(half):
    turn = jnp.tanh(half)
    above = 1.0 + turn
    act = half * above
    return act, above + act * (1.0 - turn)


MESH = pl.DeviceIdType.MESH


def greet(partners):
    barrier = pltpu.get_barrier_semaphore()
    count = 0
    for device, exists in partners:
        if exists is None:
            pl.semaphore_signal(barrier, inc=1, device_id=device, device_id_type=MESH)
            count = count + 1
        else:
            pl.when(exists)(partial(pl.semaphore_signal, barrier, inc=1, device_id=device, device_id_type=MESH))
            count = count + exists.astype(jnp.int32)
    pl.semaphore_wait(barrier, count)


def send(source, target, sems, slot, device):
    return pltpu.make_async_remote_copy(
        src_ref=source, dst_ref=target, send_sem=sems.at[0, slot], recv_sem=sems.at[1, slot],
        device_id=device, device_id_type=MESH,
    )


class Gather:
    def __init__(self, rows_v, sems, shard, fs, node):
        self.rows_v, self.sems, self.shard, self.fs = rows_v, sems, shard, fs
        self.parts = sems.shape[1] // 3
        self.next, self.far = (fs ^ 1, node), (fs ^ 2, node)

    def piece(self, owner, part):
        size = self.shard // self.parts
        return self.rows_v.at[pl.ds(pl.multiple_of(owner * self.shard + part * size, 16), size)]

    def copy(self, owner, part, slot, device):
        return send(self.piece(owner, part), self.piece(owner, part), self.sems, slot * self.parts + part, device)

    def start(self):
        for part in range(self.parts):
            self.copy(self.fs, part, 0, self.far).start()
        for part in range(self.parts):
            self.copy(self.fs, part, 1, self.next).start()

    def forward(self):
        for part in range(self.parts):
            self.copy(self.fs, part, 0, self.far).wait_recv()
            self.copy(self.fs ^ 2, part, 2, self.next).start()

    def finish(self):
        for part in range(self.parts):
            self.copy(self.fs, part, 0, self.far).wait_send()
            self.copy(self.fs, part, 1, self.next).wait()
            self.copy(self.fs ^ 2, part, 2, self.next).wait()


def list_matrix(send_ref, side, nodes):
    halo = send_ref.shape[1]
    listed = jnp.broadcast_to(send_ref[side : side + 1, :], (nodes, halo))
    return ones_where(listed == iota((nodes, halo), 0))


def sides(node, count):
    return ((node - 1, node > 0), (node + 1, node < count - 1))


class Cube:
    def __init__(self, count, fs=None, node=None):
        bits = count.bit_length() - 1
        self.node_bits = min(2, bits)
        self.size = 2 << self.node_bits
        self.extra = list(range(self.node_bits, bits))
        self.fs, self.node = fs, node
        if fs is not None:
            self.me = (fs >> 1) + 2 * (node & ((1 << self.node_bits) - 1))
        self.far_first = sorted(range(1, self.size), key=lambda r: (-r.bit_count(), -r))

    def device(self, r):
        return self.fs ^ (2 * (r & 1)), self.node ^ (r >> 1)

    def over(self, bit):
        return self.fs, self.node ^ (1 << bit)


def tree_sum(parts):
    while len(parts) > 1:
        parts = [left + right for left, right in zip(parts[::2], parts[1::2], strict=True)]
    return parts[0]


class Reduce:
    def __init__(self, cube, first, rows, sum_v, out_v, buffers):
        self.cube, self.sum_v, self.out_v = cube, sum_v, out_v
        self.give_v, self.land_v, self.near_v, self.cube_v, self.acc_v, self.extra_v, self.sems = buffers
        self.half = rows // 2
        self.size = self.half // cube.size
        core = cube.fs & 1
        self.keep, self.give = first + core * self.half, first + (1 - core) * self.half
        self.twin = (cube.fs ^ 1, cube.node)
        self.order = cube.far_first + [0]
        self.started = []

    @staticmethod
    def scratch(cube, rows, width):
        half, extra = rows // 2, max(2 * len(cube.extra), 1)
        size = half // cube.size
        return [
            pltpu.VMEM((half, width), BF16),
            pltpu.VMEM((half, width), BF16),
            pltpu.VMEM((half, width), BF16),
            pltpu.VMEM((cube.size, size, width), BF16),
            pltpu.VMEM((size, width), F32),
            pltpu.VMEM((extra, size, width), BF16),
            pltpu.SemaphoreType.DMA((2, 4 * cube.size + extra)),
        ]

    def rows(self, r, base=0):
        return pl.ds(pl.multiple_of(base + (self.cube.me ^ r) * self.size, 16), self.size)

    def launch(self, source, target, slot, device):
        copy = send(source, target, self.sems, slot, device)
        copy.start()
        self.started.append(copy)
        return copy

    def begin(self):
        self.core = {}
        for r in self.order:
            part = self.give_v.at[self.rows(r)]
            part[...] = self.sum_v[self.rows(r, self.give), :].astype(BF16)
            self.core[r] = self.launch(part, self.land_v.at[self.rows(r)], r, self.twin)

    def spread(self):
        self.near = {}
        for r in self.order:
            self.core[r].wait_recv()
            total = self.sum_v[self.rows(r, self.keep), :] + self.land_v[self.rows(r), :].astype(F32)
            if r:
                part = self.near_v.at[self.rows(r)]
                part[...] = total.astype(BF16)
                self.near[r] = self.launch(part, self.cube_v.at[r], self.cube.size + r, self.cube.device(r))
            else:
                self.acc_v[...] = total

    def meet(self):
        total = self.acc_v[...]
        for r in reversed(self.cube.far_first):
            self.near[r].wait_recv()
            total = total + self.cube_v[r].astype(F32)
        self.far = None
        if self.cube.extra:
            self.exchange(total, 0)
        else:
            self.acc_v[...] = total

    def exchange(self, total, e):
        self.extra_v[2 * e] = total.astype(BF16)
        self.far = self.launch(
            self.extra_v.at[2 * e], self.extra_v.at[2 * e + 1], 4 * self.cube.size + e, self.cube.over(self.cube.extra[e])
        )

    def settle(self):
        total = self.acc_v[...]
        for e in range(len(self.cube.extra)):
            self.far.wait_recv()
            total = self.extra_v[2 * e].astype(F32) + self.extra_v[2 * e + 1].astype(F32)
            if e + 1 < len(self.cube.extra):
                self.exchange(total, e + 1)
        own = self.out_v.at[self.rows(0, self.keep)]
        own[...] = total.astype(BF16)
        size = self.cube.size
        self.back = {r: self.launch(own, own, 2 * size + r, self.cube.device(r)) for r in self.cube.far_first}
        self.last = [self.launch(own, own, 3 * size, self.twin)]

    def forward(self):
        for r in reversed(self.cube.far_first):
            self.back[r].wait_recv()
            part = self.out_v.at[self.rows(r, self.keep)]
            self.last.append(self.launch(part, part, 3 * self.cube.size + r, self.twin))

    def end(self):
        for copy in self.last:
            copy.wait_recv()
        for copy in self.started:
            copy.wait_send()


class VectorSum:
    def __init__(self, cube, send_v, land_v, sems):
        self.cube, self.send_v, self.land_v, self.sems = cube, send_v, land_v, sems
        self.started = []

    @staticmethod
    def scratch(cube, shape):
        extra = len(cube.extra)
        return [
            pltpu.VMEM((2 + extra,) + shape, F32),
            pltpu.VMEM((cube.size + extra,) + shape, F32),
            pltpu.SemaphoreType.DMA((2, cube.size + extra)),
        ]

    def launch(self, source, slot, device):
        copy = send(self.send_v.at[source], self.land_v.at[slot], self.sems, slot, device)
        copy.start()
        self.started.append(copy)
        return copy

    def begin(self, value):
        self.send_v[0] = value
        self.core = self.launch(0, 0, (self.cube.fs ^ 1, self.cube.node))

    def spread(self):
        self.core.wait_recv()
        self.send_v[1] = self.send_v[0] + self.land_v[0]
        self.near = [self.launch(1, r, self.cube.device(r)) for r in range(1, self.cube.size)]

    def meet(self):
        for copy in self.near:
            copy.wait_recv()
        self.total = tree_sum([self.send_v[1]] + [self.land_v[r] for r in range(1, self.cube.size)])
        self.far = self.exchange(0) if self.cube.extra else None

    def exchange(self, e):
        self.send_v[2 + e] = self.total
        return self.launch(2 + e, self.cube.size + e, self.cube.over(self.cube.extra[e]))

    def settle(self):
        for e in range(len(self.cube.extra)):
            self.far.wait_recv()
            self.total = self.total + self.land_v[self.cube.size + e]
            if e + 1 < len(self.cube.extra):
                self.far = self.exchange(e + 1)
        return self.total

    def end(self):
        for copy in self.started:
            copy.wait_send()


def round_kernel(
    z, names, count, edge_ref, cot_ref, node_ref, ncot_ref, five_ref, send_ref, list_ref, kern_ref, kfirst_ref, ksecond_ref,
    vec_ref, eout_ref, egrad_ref, nout_ref, ngrad_ref, grad_ref, gvec_ref, rows_ref, first_ref, second_ref, *scratch,
):
    m = type("Held", (), {})()
    for name, ref in zip(names, scratch[: len(names)], strict=True):
        setattr(m, name, ref)
    spare = scratch[len(names) :]
    fs, node_id = lax.axis_index("fs"), lax.axis_index("nodes")
    cube = Cube(count, fs, node_id)
    around = sides(node_id, count)
    shard = kern_ref.shape[0]
    width, nodes, edges, samples, halo = z.width, z.nodes, z.edges, z.samples, z.halo
    two_halo = 2 * halo

    def sample_copy(source, target, sem, s):
        rows = aligned(s, edges)
        return pltpu.make_async_copy(source.at[rows], target.at[rows], sem.at[s])

    locals_in = [
        pltpu.make_async_copy(source, target, m.local_sem.at[i])
        for i, (source, target) in enumerate(
            [(ncot_ref, m.ncot_v), (kfirst_ref, m.mom_v.at[0]), (ksecond_ref, m.mom_v.at[1])]
        )
    ]
    weight_ref = m.rows_v
    mine = pl.ds(pl.multiple_of(fs * shard, 16), shard)
    weight_ref[mine, :] = kern_ref[...].astype(BF16)
    m.halo_v[...] = jnp.zeros_like(m.halo_v)
    m.ret_v[...] = jnp.zeros_like(m.ret_v)
    gather = Gather(weight_ref, m.rows_sem, shard, fs, node_id)
    moments = [Gather(m.first_v, m.first_sem, shard, fs, node_id), Gather(m.second_v, m.second_sem, shard, fs, node_id)]
    greet(
        [(gather.next, None)]
        + [(cube.device(r), None) for r in range(1, cube.size)]
        + [(cube.over(bit), None) for bit in cube.extra]
        + [((fs, other), exists) for other, exists in around]
    )
    gather.start()
    for copy in locals_in:
        copy.start()
    for s in range(samples):
        sample_copy(edge_ref, m.edge_v, m.edge_sem, s).start()
    for s in range(samples):
        sample_copy(cot_ref, m.cot_v, m.cot_sem, s).start()

    def to_side(source, target, sems, side, other):
        return send(source.at[side], target.at[1 - side], sems, side, (fs, other))

    def start_sides(source, target, sems):
        for side, (other, exists) in enumerate(around):
            pl.when(exists)(lambda side=side, other=other: to_side(source, target, sems, side, other).start())

    def finish_sides(source, target, sems):
        for side, (other, exists) in enumerate(around):
            def settle(side=side, other=other):
                to_side(source, target, sems, side, other).wait_send()
                to_side(source, target, sems, 1 - side, other).wait_recv()
            pl.when(exists)(settle)

    for side in range(2):
        chosen = list_matrix(list_ref, side, nodes)
        for s in range(samples):
            m.list_v[side, s * halo : (s + 1) * halo, :] = dot_tn(
                chosen, node_ref[s * nodes : (s + 1) * nodes, :]
            ).astype(BF16)
    start_sides(m.list_v, m.halo_v, m.halo_sem)
    build_selectors(z, m, five_ref, send_ref)
    gather.forward()
    gather.finish()
    finish_sides(m.list_v, m.halo_v, m.halo_sem)
    rows_out = pltpu.make_async_copy(weight_ref, rows_ref, m.local_sem.at[3])
    rows_out.start()
    for copy in locals_in:
        copy.wait()
    for k, (moment, held) in enumerate(zip(moments, (m.first_v, m.second_v), strict=True)):
        held[mine, :] = m.mom_v[k].astype(BF16)
        moment.start()
    m.half_v[...] = weight_ref[...] * jnp.asarray(0.5, BF16)
    m.gmat_v[...] = jnp.zeros_like(m.gmat_v)
    m.vsum_v[...] = jnp.zeros_like(m.vsum_v)
    m.aown_v[...] = jnp.zeros_like(m.aown_v)
    m.ahalo_v[...] = jnp.zeros_like(m.ahalo_v)
    for s in range(samples):
        for side in range(2):
            m.table_v[s * two_halo + side * halo : s * two_halo + (side + 1) * halo, :] = m.halo_v[
                side, s * halo : (s + 1) * halo, :
            ]

    send_half = m.half_v[width : 2 * width, :]
    recv_half = m.half_v[2 * width : 3 * width, :]
    bias_edge, gain_edge, shift_edge = vec_ref[0:1, :] * 0.5, vec_ref[1:2, :], vec_ref[2:3, :]
    bias_node, gain_node, shift_node = vec_ref[3:4, :] * 0.5, vec_ref[4:5, :], vec_ref[5:6, :]

    for s in range(samples):
        node = node_ref[s * nodes : (s + 1) * nodes, :]
        high, low = split(dot_nn(node, send_half))
        m.pown_v[s * 2 * nodes : (s * 2 + 1) * nodes, :] = high
        m.pown_v[(s * 2 + 1) * nodes : (s * 2 + 2) * nodes, :] = low
        high, low = split(dot_nn(node, recv_half) + bias_edge)
        out_high, out_low = split(dot_nn(m.table_v[s * two_halo : (s + 1) * two_halo, :], send_half))
        zero = jnp.zeros((2 * LANES - 2 * z.fwd_nodes - 2 * two_halo, width), BF16)
        for c in range(z.fwd_chunks):
            own = slice(c * z.fwd_nodes, (c + 1) * z.fwd_nodes)
            base = (s * z.fwd_chunks + c) * 2 * LANES
            m.psel_v[base : base + 2 * LANES, :] = jnp.concatenate(
                [high[own], low[own], out_high, out_low, zero], 0
            )

    per = z.fwd_chunks
    last = samples * per - 1

    def join_edges(i, slot):
        s, c = i // per, i % per
        local = aligned(c, z.fwd_rows)
        own = m.own_v[local, :]
        left = jnp.concatenate([m.edge_v[aligned(i, z.fwd_rows), :], own, own, m.sel_v[local, :]], 1)
        right = jnp.concatenate(
            [m.half_v[0:width, :], m.pown_v[aligned(s, 2 * nodes), :], m.psel_v[aligned(i, 2 * LANES), :]], 0
        )
        m.pre_v[slot] = dot_nn(left, right)

    def activate(i, slot):
        rows = aligned(i, z.fwd_rows)
        act, slope = act_and_slope(m.pre_v[slot])
        act = act.astype(BF16)
        m.act_v[rows, :] = act
        m.slope_v[rows, :] = slope
        m.raw_v[slot] = dot_nn(act, weight_ref[3 * width : 4 * width, :])

    def update_edges(i, slot):
        rows, local = aligned(i, z.fwd_rows), aligned(i % per, z.fwd_rows)
        centre, inv = centred(m.raw_v[slot])
        live = m.live_v[local, :]
        inv = inv * live
        m.inv_v[rows, :] = inv
        normed = centre * both(inv)
        m.norm_v[rows, :] = normed.astype(BF16)
        update = normed * gain_edge + both(live) * shift_edge
        m.edge_out_v[rows, :] = (m.edge_v[rows, :].astype(F32) + update).astype(BF16)
        m.upd_v[slot] = update.astype(BF16)

    def gather_updates(i, slot):
        gathered = dot_nn(m.rep_t[0 : z.fwd_nodes, 0 : z.fwd_rows], m.upd_v[slot])
        m.gath_v[aligned(i, z.fwd_nodes), :] = gathered.astype(BF16)

    def edge_in(s):
        return sample_copy(edge_ref, m.edge_v, m.edge_sem, s)

    edge_in(0).wait()
    join_edges(0, 0)

    def forward(s, carry):
        pl.when(s < samples - 1)(lambda: edge_in(s + 1).wait())
        for c in range(per):
            i = s * per + c
            join_edges(jnp.minimum(i + 1, last), (c + 1) % 2)
            gather_updates(jnp.maximum(i - 2, 0), c % 2)
            activate(i, c % 2)
            update_edges(jnp.maximum(i - 1, 0), (c + 1) % 2)
        pl.when(s > 0)(lambda: sample_copy(m.edge_out_v, eout_ref, m.eout_sem, s - 1).start())
        return carry

    lax.fori_loop(0, samples, forward, 0)
    gather_updates(last - 1, 0)
    update_edges(last, 1)
    gather_updates(last, 1)
    sample_copy(m.edge_out_v, eout_ref, m.eout_sem, samples - 1).start()

    def node_part(i, carry):
        rows = aligned(i, 2 * nodes)
        node, gath = node_ref[rows, :], m.gath_v[rows, :]
        joined = jnp.concatenate([node, gath], 1)
        act, slope = act_and_slope(dot_nn(joined, m.half_v[4 * width : 6 * width, :]) + bias_node)
        act = act.astype(BF16)
        centre, inv = centred(dot_nn(act, weight_ref[6 * width : 7 * width, :]))
        normed = centre * inv
        nout_ref[rows, :] = (node.astype(F32) + normed * gain_node + shift_node).astype(BF16)
        back = m.ncot_v[rows, :].astype(F32)
        back_normed = back * normed
        scaled, scaled_normed = back * gain_node, back_normed * gain_node
        d_out = (inv * (scaled - row_mean(scaled) - normed * row_mean(scaled_normed))).astype(BF16)
        m.gmat_v[6 * width : 7 * width, :] += dot_tn(act, d_out)
        m.vsum_v[32:40, :] += fold_rows(back_normed)
        m.vsum_v[40:48, :] += fold_rows(back)
        d_pre = dot_nt(d_out, m.half_v[6 * width : 7 * width, :]) * slope
        d_pre = d_pre.astype(BF16)
        m.vsum_v[24:32, :] += fold_rows(d_pre.astype(F32))
        m.gmat_v[4 * width : 6 * width, :] += dot_tn(joined, d_pre)
        d_joined = dot_nt(d_pre, weight_ref[4 * width : 6 * width, :])
        m.total_v[rows, :] = back + d_joined[:, :width]
        high, low = split(d_joined[:, width:])
        for k in range(2):
            for c in range(z.bwd_chunks):
                own = slice(k * nodes + c * z.bwd_nodes, k * nodes + (c + 1) * z.bwd_nodes)
                m.drep_v[aligned((i * 2 + k) * z.bwd_chunks + c, 2 * LANES), :] = jnp.concatenate(
                    [high[own], low[own]], 0
                )
        return carry

    lax.fori_loop(0, samples // 2, node_part, 0)

    halves = z.bwd_rows // z.fwd_rows
    pairs = samples * z.bwd_chunks

    def spread_back(i, slot):
        half = slice((slot % halves) * z.fwd_rows, (slot % halves + 1) * z.fwd_rows)
        m.pre_v[slot] = dot_nn(m.rep_v[half, :], m.drep_v[aligned(i // halves, 2 * LANES), :])

    def norm_back(i, slot, pair):
        rows, local = aligned(i, z.fwd_rows), aligned(i % per, z.fwd_rows)
        d_update = (m.cot_v[rows, :].astype(F32) + m.pre_v[slot]) * both(m.live_v[local, :])
        normed = m.norm_v[rows, :].astype(F32)
        d_normed = d_update * normed
        m.vsum_v[8:16, :] += fold_rows(d_normed)
        m.vsum_v[16:24, :] += fold_rows(d_update)
        scaled, scaled_normed = d_update * gain_edge, d_normed * gain_edge
        d_out = both(m.inv_v[rows, :]) * (scaled - row_mean(scaled) - normed * row_mean(scaled_normed))
        m.dout_v[pair, slot * z.fwd_rows : (slot + 1) * z.fwd_rows, :] = d_out.astype(BF16)

    def activate_back(i, slot, pair):
        part = slice(slot * z.fwd_rows, (slot + 1) * z.fwd_rows)
        d_act = dot_nt(m.dout_v[pair, part, :], m.half_v[3 * width : 4 * width, :])
        m.dpre_v[pair, part, :] = (d_act * m.slope_v[aligned(i, z.fwd_rows), :]).astype(BF16)

    def weights_back(p, pair):
        s, c = p // z.bwd_chunks, p % z.bwd_chunks
        rows, local = aligned(p, z.bwd_rows), aligned(c, z.bwd_rows)
        d_out, d_pre = m.dout_v[pair], m.dpre_v[pair]
        m.gmat_v[3 * width : 4 * width, :] += dot_tn(m.act_v[rows, :], d_out)
        m.gmat_v[0:width, :] += dot_tn(m.edge_v[rows, :], d_pre)
        m.recv_v[aligned(p, z.bwd_nodes), :] = dot_nn(m.rep_t[...], d_pre)
        m.aown_v[aligned(s, nodes), :] += dot_nn(m.own_t[:, local], d_pre)
        m.ahalo_v[aligned(s, two_halo), :] += dot_nn(m.halo_t[:, local], d_pre)
        m.edge_out_v[rows, :] = (m.cot_v[rows, :].astype(F32) + dot_nt(d_pre, weight_ref[0:width, :])).astype(BF16)

    for s in range(samples):
        sample_copy(m.edge_out_v, eout_ref, m.eout_sem, s).wait()
    m.dout_v[1] = jnp.zeros_like(m.dout_v[1])
    m.dpre_v[1] = jnp.zeros_like(m.dpre_v[1])
    spread_back(0, 0)

    def backward(s, carry):
        sample_copy(cot_ref, m.cot_v, m.cot_sem, s).wait()
        for k in range(z.bwd_chunks):
            p = s * z.bwd_chunks + k
            i = p * halves
            spread_back(i + 1, 1)
            activate_back(jnp.maximum(i - 1, 0), 1, 1 - k)
            norm_back(i, 0, k)
            weights_back(jnp.maximum(p - 1, 0), 1 - k)
            spread_back(jnp.minimum(i + 2, last), 0)
            activate_back(i, 0, k)
            norm_back(i + 1, 1, k)
        pl.when(s > 0)(lambda: sample_copy(m.edge_out_v, egrad_ref, m.egrad_sem, s - 1).start())
        return carry

    lax.fori_loop(0, samples, backward, 0)
    activate_back(last, 1, 1)
    weights_back(pairs - 1, 1)
    sample_copy(m.edge_out_v, egrad_ref, m.egrad_sem, samples - 1).start()

    send_full = weight_ref[width : 2 * width, :]
    recv_full = weight_ref[2 * width : 3 * width, :]
    table = m.table_v[...]
    out_high, out_low = split(m.ahalo_v[...])
    grad_send = dot_tn(table, out_high) + dot_tn(table, out_low)
    grad_recv = jnp.zeros((width, width), F32)
    for s in range(samples):
        rows = slice(s * nodes, (s + 1) * nodes)
        recv_high, recv_low = split(m.recv_v[rows, :])
        own_high, own_low = split(m.aown_v[rows, :])
        node = node_ref[rows, :]
        grad_recv += dot_tn(node, recv_high) + dot_tn(node, recv_low)
        grad_send += dot_tn(node, own_high) + dot_tn(node, own_low)
    m.gmat_v[width : 2 * width, :] = grad_send
    m.gmat_v[2 * width : 3 * width, :] = grad_recv
    reduce = Reduce(cube, 0, 7 * width, m.gmat_v, m.gout_v, spare[:7])
    vectors = VectorSum(cube, *spare[7:])
    reduce.begin()
    border = (dot_nt(out_high, send_full) + dot_nt(out_low, send_full)).astype(BF16)
    for s in range(samples):
        for side in range(2):
            m.border_v[side, s * halo : (s + 1) * halo, :] = border[
                s * two_halo + side * halo : s * two_halo + (side + 1) * halo, :
            ]
    start_sides(m.border_v, m.ret_v, m.ret_sem)
    for s in range(samples):
        m.vsum_v[0:8, :] += fold_rows(m.recv_v[s * nodes : (s + 1) * nodes, :])
    vectors.begin(
        jnp.concatenate(
            [jnp.sum(m.vsum_v[k * 8 : (k + 1) * 8, :], 0, keepdims=True) for k in range(6)]
            + [jnp.zeros((2, width), F32)],
            0,
        )
    )
    reduce.spread()
    vectors.spread()
    for moment in moments:
        moment.forward()
    for s in range(samples):
        rows = slice(s * nodes, (s + 1) * nodes)
        recv_high, recv_low = split(m.recv_v[rows, :])
        own_high, own_low = split(m.aown_v[rows, :])
        m.total_v[rows, :] += (
            dot_nt(recv_high, recv_full) + dot_nt(recv_low, recv_full)
            + dot_nt(own_high, send_full) + dot_nt(own_low, send_full)
        )
    reduce.meet()
    vectors.meet()
    finish_sides(m.border_v, m.ret_v, m.ret_sem)
    low, high = (list_matrix(list_ref, side, nodes) for side in range(2))
    for s in range(samples):
        rows, part = slice(s * nodes, (s + 1) * nodes), slice(s * halo, (s + 1) * halo)
        ngrad_ref[rows, :] = (
            m.total_v[rows, :] + dot_nn(low, m.ret_v[0, part, :]) + dot_nn(high, m.ret_v[1, part, :])
        ).astype(BF16)
    reduce.settle()
    gvec_ref[...] = vectors.settle()
    for moment in moments:
        moment.finish()
    moments_out = [
        pltpu.make_async_copy(m.first_v, first_ref, m.local_sem.at[4]),
        pltpu.make_async_copy(m.second_v, second_ref, m.local_sem.at[5]),
    ]
    for copy in moments_out:
        copy.start()
    for s in range(samples):
        sample_copy(m.edge_out_v, egrad_ref, m.egrad_sem, s).wait()
    for copy in moments_out + [rows_out]:
        copy.wait()
    reduce.forward()
    reduce.end()
    vectors.end()
    grad_out = pltpu.make_async_copy(m.gout_v, grad_ref, m.local_sem.at[6])
    grad_out.start()
    grad_out.wait()


def round_call(z, count, edge, cot, node, ncot, five, senders, send_rows, kern, kfirst, ksecond, vectors):
    shard, width = kern.shape
    scratch = main_scratch(z, shard)
    cube = Cube(count)
    spare = Reduce.scratch(cube, 7 * width, width) + VectorSum.scratch(cube, (8, width))
    rows, per_node = z.samples * z.edges, z.samples * z.nodes
    whole = pl.BlockSpec(memory_space=pltpu.VMEM)
    anywhere = pl.BlockSpec(memory_space=pl.ANY)
    total = jax.ShapeDtypeStruct((7 * width, width), BF16)
    return pl.pallas_call(
        partial(round_kernel, z, tuple(scratch), count),
        out_shape=(
            jax.ShapeDtypeStruct((rows, width), BF16),
            jax.ShapeDtypeStruct((rows, width), BF16),
            jax.ShapeDtypeStruct((per_node, width), BF16),
            jax.ShapeDtypeStruct((per_node, width), BF16),
            total,
            jax.ShapeDtypeStruct((8, width), F32),
            total, total, total,
        ),
        in_specs=[anywhere, anywhere, whole, anywhere, whole, whole, whole, whole, anywhere, anywhere, whole],
        out_specs=(anywhere, anywhere, whole, whole, anywhere, whole, anywhere, anywhere, anywhere),
        scratch_shapes=list(scratch.values()) + spare,
        compiler_params=pltpu.CompilerParams(
            collective_id=0, has_side_effects=True, vmem_limit_bytes=VMEM_LIMIT
        ),
        name="edge_node_round",
    )(edge, cot, node, ncot, five, senders, send_rows, kern, kfirst, ksecond, vectors)


def dot_exact(left, right, dims):
    return lax.dot_general(left, right, (dims, ((), ())), precision=HIGH, preferred_element_type=F32)


BLOCK = 32
COUNT = 4
HALF = LANES // BLOCK


def wide_left(value):
    high, low = split(value)
    return jnp.concatenate([high, high, low], 1)


def wide_right(value):
    high, low = split(value)
    return jnp.concatenate([high, low, high], 1)


def dot_three(left, right):
    return dot_nt(wide_left(left), wide_right(right))


def factor_block(packed):
    sub = iota((8, LANES), 0)
    lane = iota((8, LANES), 1)
    tiles = BLOCK // 8
    group = lane & (LANES - BLOCK)
    parts = [packed[8 * r : 8 * r + 8, :] for r in range(tiles)]
    columns = [
        [jnp.take_along_axis(parts[r], group + l, axis=1) if r >= l // 8 else None for r in range(tiles)]
        for l in range(BLOCK)
    ]
    inverse = [jnp.where((lane & (BLOCK - 1)) == sub + 8 * r, 1.0, 0.0) for r in range(tiles)]

    def line(tile, s):
        return jnp.broadcast_to(tile[s : s + 1, :], (8, LANES))

    for j in range(BLOCK):
        rj, sj = j // 8, j % 8
        scale = lax.rsqrt(line(columns[j][rj], sj))
        below = [None if r < rj else columns[j][r] * scale for r in range(tiles)]
        below[rj] = jnp.where(sub > sj, below[rj], 0.0)
        for l in range(j + 1, BLOCK):
            weight = line(below[l // 8], l % 8)
            for r in range(l // 8, tiles):
                columns[l][r] = columns[l][r] - below[r] * weight
        row = line(inverse[rj], sj) * scale
        inverse[rj] = jnp.where(sub == sj, row, inverse[rj] - below[rj] * row)
        for r in range(rj + 1, tiles):
            inverse[r] = inverse[r] - below[r] * row
    return jnp.concatenate(inverse, 0)


def turned_blocks(k, width):
    return [h * HALF + (g - k) % HALF for h in range(width // LANES) for g in range(HALF)]


def pick_rows(value, blocks):
    return jnp.concatenate([value[i * BLOCK : (i + 1) * BLOCK, :] for i in blocks], 0)


def orthogonalize(work_v, bases_out, width, beside):
    blocks = width // BLOCK
    group = iota((BLOCK, LANES), 1) // BLOCK
    square = iota((LANES, LANES), 0) // BLOCK == iota((LANES, LANES), 1) // BLOCK

    def placed(values, b):
        return [jnp.where(group == (b + k) % COUNT, values[k], jnp.zeros_like(values[k])) for k in range(COUNT)]

    def lanes_of(b):
        return slice(b // HALF * LANES, (b // HALF + 1) * LANES)

    def rows_of(b):
        return slice(b * BLOCK, (b + 1) * BLOCK)

    packed = sum(placed([work_v[k, rows_of(0), lanes_of(0)] for k in range(COUNT)], 0))
    for b in range(blocks):
        beside(b)
        lanes, after = lanes_of(b), (b + 1) * BLOCK
        high, low = split(factor_block(packed).astype(F32))
        high, low = placed([high] * COUNT, b), placed([low] * COUNT, b)
        if b < blocks - 1:
            spread_high, spread_low = jnp.concatenate(high, 0), jnp.concatenate(low, 0)
            spread = jnp.concatenate([spread_high, spread_low, spread_high], 1)
            ahead = jnp.concatenate([work_v[k, rows_of(b + 1), lanes] for k in range(COUNT)], 0)
            turned = jnp.where(square, dot_nt(wide_left(ahead), spread), 0.0)
            order = [(g - b - 1) % COUNT for g in range(COUNT)]
            update = dot_nt(wide_left(turned), pick_rows(wide_right(turned), order))
            current = placed([work_v[k, rows_of(b + 1), lanes_of(b + 1)] for k in range(COUNT)], b + 1)
            packed = sum(current) - sum(update[rows_of(k), :] for k in range(COUNT))
        start = after // LANES * LANES
        for k in range(COUNT):
            four_high = jnp.concatenate([high[k]] * HALF, 0)
            four_low = jnp.concatenate([low[k]] * HALF, 0)
            below = wide_left(work_v[k, after:, lanes])
            turned = dot_nt(below, jnp.concatenate([four_high, four_low, four_high], 1))
            mine = iota((width, LANES), 1) // BLOCK == b % HALF
            bases_out[k, :, lanes] = jnp.where(mine, turned[width - after :, :], bases_out[k, :, lanes])
            if b == blocks - 1:
                continue
            turned_high, turned_low = split(turned)
            part = iota(turned.shape, 1) // BLOCK
            zero = jnp.zeros_like(turned_high)
            left = jnp.where(part == 2, turned_low, jnp.where(part == 3, zero, turned_high))
            right = jnp.where(part == 1, turned_low, jnp.where(part == 3, zero, turned_high))
            right = jnp.concatenate(
                [
                    right[(i - b - 1) * BLOCK : (i - b) * BLOCK, :] if i > b else zero[0:BLOCK, :]
                    for i in turned_blocks(k, width)[start // BLOCK :]
                ],
                0,
            )
            work_v[k, after:, start:] -= dot_nt(left, right)


def matrix_bounds(width):
    return [0, 3 * width, 4 * width, 6 * width, 7 * width]


def new_statistics(grad_ref, stat_ref, k):
    width = stat_ref.shape[-1]
    bounds = matrix_bounds(width)
    rows = grad_ref[bounds[k] : bounds[k + 1], :]
    return BETA_TWO * stat_ref[k] + (1.0 - BETA_TWO) * dot_tn(rows, rows)


def matrix_of(row, width):
    return sum((row >= bound).astype(jnp.int32) for bound in matrix_bounds(width)[1:-1])


def prepare_bases(stat_ref, bases_ref, work_v, width):
    for k in range(COUNT):
        order = turned_blocks(k, width)
        stat = stat_ref[k]
        flipped = bases_ref[k].T
        proj_rows = dot_three(flipped, stat)
        work_v[k, 0:width, :] = dot_three(proj_rows, pick_rows(proj_rows, order))
        work_v[k, width:, :] = dot_three(stat, pick_rows(flipped, order))


def adam_step(first, second, rotated):
    first = BETA_ONE * first + (1.0 - BETA_ONE) * rotated
    second = BETA_TWO * second + (1.0 - BETA_TWO) * rotated * rotated
    step = first / (1.0 - BETA_ONE**STEP) / (jnp.sqrt(second / (1.0 - BETA_TWO**STEP)) + ADAM_EPS)
    return first, second, step


def turn(rows, basis):
    high, low = split(basis)
    return dot_nn(rows, high) + dot_nn(rows, low)


def decayed(kern, turned):
    return kern - RATE_MATRIX * (turned + DECAY_RATE * kern)


def update_kernel(
    grad_ref, stat_ref, bases_ref, kern_ref, kfirst_ref, ksecond_ref, rows_ref, first_ref, second_ref,
    gvec_ref, vec_ref, vfirst_ref, vsecond_ref, eout_ref, egrad_ref, nout_ref, ngrad_ref,
    eout_out, egrad_out, nout_out, ngrad_out, kern_out, kfirst_out, ksecond_out, vec_out, vfirst_out, vsecond_out,
    stat_out, bases_out, half_out,
    grad_v, stat_v, bases_v, kern_v, kfirst_v, ksecond_v, rows_v, first_v, second_v,
    work_v, kern_new, kfirst_new, ksecond_new, stat_new, bases_new, half_v, eout_v, egrad_v, nout_v, ngrad_v, in_sem, out_sem, pass_sem,
):
    shard, width = kern_v.shape
    copies = [
        pltpu.make_async_copy(source, target, in_sem.at[i])
        for i, (source, target) in enumerate(
            [
                (bases_ref, bases_v), (stat_ref, stat_v), (grad_ref, grad_v), (kern_ref, kern_v), (kfirst_ref, kfirst_v),
                (ksecond_ref, ksecond_v), (rows_ref, rows_v), (first_ref, first_v), (second_ref, second_v),
            ]
        )
    ]
    passed = [
        (pltpu.make_async_copy(source, held, pass_sem.at[0, i]), pltpu.make_async_copy(held, target, pass_sem.at[1, i]))
        for i, (source, held, target) in enumerate(
            [
                (eout_ref, eout_v, eout_out), (egrad_ref, egrad_v, egrad_out),
                (nout_ref, nout_v, nout_out), (ngrad_ref, ngrad_v, ngrad_out),
            ]
        )
    ]
    outs = [
        pltpu.make_async_copy(source, target, out_sem.at[i])
        for i, (source, target) in enumerate(
            [
                (stat_new, stat_out), (kern_new, kern_out), (kfirst_new, kfirst_out), (ksecond_new, ksecond_out),
                (half_v, half_out), (bases_new, bases_out),
            ]
        )
    ]
    for copy in copies:
        copy.start()
    bases_new[...] = jnp.zeros_like(bases_new)
    for copy in copies[:3]:
        copy.wait()
    for k in range(COUNT):
        stat_new[k] = new_statistics(grad_v, stat_v, k)
    outs[0].start()
    for copy in copies[3:]:
        copy.wait()
    for copy, _ in passed:
        copy.start()
    prepare_bases(stat_new, bases_v, work_v, width)

    def own_rows():
        first_row = lax.axis_index("fs") * shard
        grad = grad_v[pl.ds(pl.multiple_of(first_row, 64), shard), :]
        one = matrix_of(first_row, width)
        two = matrix_of(first_row + shard - 1, width)
        in_two = matrix_of(first_row + iota((shard, width), 0), width) != one
        basis_one, basis_two = bases_v[one], bases_v[two]
        rotated = jnp.where(in_two, turn(grad, basis_two), turn(grad, basis_one))
        kfirst_new[...], ksecond_new[...], step = adam_step(kfirst_v[...], ksecond_v[...], rotated)
        turned = jnp.where(in_two, dot_three(step, basis_two), dot_three(step, basis_one))
        kern_new[...] = decayed(kern_v[...], turned)

    def all_rows(k):
        bounds = matrix_bounds(width)
        rows = slice(bounds[k], bounds[k + 1])
        rotated = turn(grad_v[rows, :], bases_v[k])
        _, _, step = adam_step(first_v[rows, :].astype(F32), second_v[rows, :].astype(F32), rotated)
        turned = dot_nt(step.astype(BF16), bases_v[k].astype(BF16))
        half_v[rows, :] = decayed(rows_v[rows, :].astype(F32), turned).astype(BF16)

    def vector_rows():
        first, second, step = adam_step(vfirst_ref[...], vsecond_ref[...], gvec_ref[0:6, :])
        vfirst_out[...], vsecond_out[...] = first, second
        vec_out[...] = vec_ref[...] - RATE_VECTOR * step

    def beside(b):
        if b < COUNT:
            all_rows(b)
        elif b == COUNT:
            own_rows()
        elif b == COUNT + 1:
            vector_rows()
            for arrived, leaving in passed:
                arrived.wait()
                leaving.start()
            for copy in outs[1:5]:
                copy.start()

    orthogonalize(work_v, bases_new, width, beside)
    outs[5].start()
    for copy in outs + [leaving for _, leaving in passed]:
        copy.wait()


def update_call(grad, stat, bases, kern, kfirst, ksecond, rows, first, second, gvec, vec, vfirst, vsecond, *through):
    shard, width = kern.shape
    whole, anywhere = pl.BlockSpec(memory_space=pltpu.VMEM), pl.BlockSpec(memory_space=pl.ANY)

    def like(array):
        return jax.ShapeDtypeStruct(array.shape, array.dtype)

    def held(array):
        return pltpu.VMEM(array.shape, array.dtype)

    loaded = (grad, stat, bases, kern, kfirst, ksecond, rows, first, second)
    return pl.pallas_call(
        update_kernel,
        out_shape=tuple(map(like, through))
        + (like(kern), like(kern), like(kern), like(vec), like(vec), like(vec), like(stat), like(stat), like(grad)),
        in_specs=[anywhere] * 9 + [whole] * 4 + [anywhere] * 4,
        out_specs=(anywhere,) * 7 + (whole,) * 3 + (anywhere,) * 3,
        scratch_shapes=[held(array) for array in loaded]
        + [pltpu.VMEM((COUNT, 2 * width, width), F32)]
        + [held(array) for array in (kern, kern, kern, stat, stat, grad) + through]
        + [pltpu.SemaphoreType.DMA((9,)), pltpu.SemaphoreType.DMA((6,)), pltpu.SemaphoreType.DMA((2, 4))],
        compiler_params=pltpu.CompilerParams(vmem_limit_bytes=VMEM_LIMIT),
        name="update",
    )(*loaded, gvec, vec, vfirst, vsecond, *through)


def on_device(
    edge_latent, node_latent, edge_cot, node_cot, five_flag, senders, send_rows, kernels, kernel_first, kernel_second,
    vectors, vector_first, vector_second, statistics, bases,
):
    samples, nodes, width = node_latent.shape
    slots = senders.shape[0] // nodes
    z = Sizes(samples, nodes, slots, send_rows.shape[1], width)
    edge_out, edge_grad, node_out, node_grad, grad, gvec, rows, first, second = round_call(
        z,
        lax.axis_size("nodes"),
        edge_latent.reshape(-1, width),
        edge_cot.reshape(-1, width),
        node_latent.reshape(-1, width),
        node_cot.reshape(-1, width),
        five_flag.reshape(1, -1),
        senders.reshape(1, -1),
        send_rows,
        kernels,
        kernel_first,
        kernel_second,
        vectors,
    )
    edge_out, edge_grad, node_out, node_grad, *rest = update_call(
        grad, statistics, bases, kernels, kernel_first, kernel_second, rows, first, second, gvec,
        vectors, vector_first, vector_second, edge_out, edge_grad, node_out, node_grad,
    )
    return (
        edge_out.reshape(edge_latent.shape),
        node_out.reshape(node_latent.shape),
        edge_grad.reshape(edge_latent.shape),
        node_grad.reshape(node_latent.shape),
        *rest,
    )


def solution(mesh):
    in_specs = (
        P("fs", "nodes", None),
        P("fs", "nodes", None),
        P("fs", "nodes", None),
        P("fs", "nodes", None),
        P("nodes"),
        P("nodes"),
        P("nodes", None),
        P("fs", None),
        P("fs", None),
        P("fs", None),
        P(),
        P(),
        P(),
        P(),
        P(),
    )
    out_specs = (
        P("fs", "nodes", None),
        P("fs", "nodes", None),
        P("fs", "nodes", None),
        P("fs", "nodes", None),
        P("fs", None),
        P("fs", None),
        P("fs", None),
        P(),
        P(),
        P(),
        P(),
        P(),
        P(),
    )
    return jax.shard_map(
        on_device, mesh=mesh, in_specs=in_specs, out_specs=out_specs, check_vma=False
    )
```

time: 240 us -> 83.1 us (0.35)
  waiting for transfers between devices: 76.4 us -> 0 us
  blocking collectives: 61.8 us -> 0 us
  Pallas kernels: 62.1 us -> 80.7 us
  between operations: 14.2 us -> 0.83 us
  starting transfers between devices: 12 us -> 0 us
  local copies, waits for them, and re-layouts: 8.23 us -> 1.29 us
  other arithmetic: 5.07 us -> 0 us
    psum x1 -> x0, waiting for transfers between devices: 76.4 us -> none  [on_device(): grad = lax.psum(grad, ('nodes', 'fs'))]
    psum x1 -> x0, blocking collectives: 42.6 us -> none  [on_device(): gvec = lax.psum(gvec, ('nodes', 'fs'))]
    all_gather x2 -> x0, blocking collectives: 19.2 us -> none  [the longest x1 9.79 us: on_device(): weights = lax.all_gather(kernels.astype(BF16), 'fs', axis=0, tiled=True)]
    pallas_call x2, Pallas kernels: 62.1 us -> 80.7 us  [the longest x1 59.1 us: round_call(): pl.pallas_call(partial(round_kernel, z, tuple(scratch), count), out_shape...]
    ppermute x4 -> x0, starting transfers between devices: 12 us -> none  [the longest x2 9.39 us: exchange(): lax.ppermute(high_part, 'nodes', up)]
    reshape x2 -> x0, local copies, waits for them, and re-layouts: 2.68 us -> none  [the longest x1 1.92 us: on_device(): node_total = node_total.reshape(samples, nodes, width)]
    scatter-add x2 -> x0, other arithmetic: 2.41 us -> none  [the longest x1 1.3 us: on_device(): node_total = node_total.at[:, send_rows[1]].add(above.astype(F32))]
  transfers between devices with their start and end apart: 5 -> 0, of which waited for: 1 -> 0; matrix products, arithmetic and copies ran while one was open for 4% -> 0% of each run, Pallas kernels for 0% -> 0%
where the time goes in v4:
time: 83.1 us; the launch traced here: 82.8 us
  Pallas kernels  80.7 us (97%)
  local copies, waits for them, and re-layouts  1.29 us (2%)
    pallas_call x1, Pallas kernels, round_call(): pl.pallas_call(partial(round_kernel, z, tuple(scratch), count), out_shape...  59.1 us
    pallas_call x1, Pallas kernels, update_call(): pl.pallas_call(update_kernel, out_shape=tuple(map(like, through)) + (like...  21.6 us

profile of v4, /device:TPU:0, one launch (start us, length us, event | category | flops | bytes accessed | tf_op | source)
XLA Modules:
  0.0 82.8 jit_solution(17466183462930936711)
XLA Ops:
  0.6 1.3 %reshape.61.send_ref = s32[1,1536]{1,0:T(1,128)} reshape(s32[1536]{0:T(1024)} %param.20) | data formatting | bytes 12288 | tf_op jit(solution)/shard_map/reshape | solution.py:1088
  1.9 59.1 %edge_node_round.1 = (bf16[6144,256]{1,0:T(8,128)(2,1)}, bf16[6144,256]{1,0:T(8,128)(2,1)}, bf16[1024,256]{1,0:T(8,128)(2,1)}, bf16[1024,256]{1,0:T(8,128)(2,1)}...) custom-call(bf16[6144,256]{1,0:T(8,128)(2,1)} %bitcast.9, ...), custom_call_target="tpu_custom_call" | custom-call | tf_op jit(solution)/shard_map/edge_node_round/pallas_call | solution.py:775
  61.0 21.6 %update.1 = (bf16[6144,256]{1,0:T(8,128)(2,1)}, bf16[6144,256]{1,0:T(8,128)(2,1)}, bf16[1024,256]{1,0:T(8,128)(2,1)}, bf16[1024,256]{1,0:T(8,128)(2,1)}, f32[448...) custom-call(bf16[1792,256]{1,0:T(8,128)(2,1)} %get-tuple-element.35., ...), custom_call_target="tpu_custom_call" | custom-call | tf_op jit(solution)/shard_map/update/pallas_call | solution.py:1058

commit v5 on v4

v5 whole, which is shorter than its diff:
```python
from functools import partial

import jax
import jax.numpy as jnp
from jax import lax
from jax.experimental import pallas as pl
from jax.experimental.pallas import tpu as pltpu
from jax.sharding import PartitionSpec as P

STEP = 5

NORM_EPS = 1e-05
BETA_ONE = 0.5
BETA_TWO = 0.5
RATE_MATRIX = 0.05
RATE_VECTOR = 0.2
DECAY_RATE = 0.01
ADAM_EPS = 1e-08
TINY = 1e-37
HIGH = lax.Precision.HIGHEST
F32 = jnp.float32
BF16 = jnp.bfloat16
LANES = 128
VMEM_LIMIT = 61 * 1024 * 1024


def dot_nn(left, right):
    return lax.dot_general(left, right, (((1,), (0,)), ((), ())), preferred_element_type=F32)


def dot_nt(left, right):
    return lax.dot_general(left, right, (((1,), (1,)), ((), ())), preferred_element_type=F32)


def dot_tn(left, right):
    return lax.dot_general(left, right, (((0,), (0,)), ((), ())), preferred_element_type=F32)


def split(value):
    high = value.astype(BF16)
    return high, (value - high.astype(F32)).astype(BF16)


def iota(shape, dim):
    return lax.broadcasted_iota(jnp.int32, shape, dim)


def ones_where(mask):
    return jnp.where(mask, 1.0, 0.0).astype(BF16)


def fold_rows(value):
    rows, width = value.shape
    return jnp.sum(value.reshape(rows // 8, 8, width), 0)


def aligned(index, step):
    return pl.ds(pl.multiple_of(index * step, step), step)


class Sizes:
    def __init__(self, samples, nodes, slots, halo, width):
        self.samples, self.nodes, self.slots = samples, nodes, slots
        self.halo, self.width = halo, width
        self.edges = nodes * slots
        self.fwd_nodes, self.bwd_nodes = 64, 128
        self.fwd_rows = self.fwd_nodes * slots
        self.bwd_rows = self.bwd_nodes * slots
        self.fwd_chunks = nodes // self.fwd_nodes
        self.bwd_chunks = nodes // self.bwd_nodes


def main_scratch(z):
    rows, width = z.samples * z.edges, z.width
    per_node = z.samples * z.nodes
    per_halo = z.samples * 2 * z.halo
    return dict(
        edge_v=pltpu.VMEM((rows, width), BF16),
        cot_v=pltpu.VMEM((rows, width), BF16),
        edge_out_v=pltpu.VMEM((rows, width), BF16),
        act_v=pltpu.VMEM((rows, width), BF16),
        slope_v=pltpu.VMEM((rows, width), F32),
        norm_v=pltpu.VMEM((rows, width), BF16),
        inv_v=pltpu.VMEM((rows, LANES), F32),
        own_v=pltpu.VMEM((z.edges, z.nodes), BF16),
        scat_v=pltpu.VMEM((z.bwd_chunks, z.nodes + 2 * z.halo + LANES, z.bwd_rows), BF16),
        sel_v=pltpu.VMEM((z.edges, 2 * LANES), BF16),
        rep_v=pltpu.VMEM((z.bwd_rows, 2 * LANES), BF16),
        live_v=pltpu.VMEM((z.edges, LANES), F32),
        half_v=pltpu.VMEM((7 * width, width), BF16),
        pown_v=pltpu.VMEM((per_node, width), BF16),
        psel_v=pltpu.VMEM((z.samples * z.fwd_chunks * 2 * LANES, width), BF16),
        gath_v=pltpu.VMEM((per_node, width), BF16),
        drep_v=pltpu.VMEM((z.samples * z.bwd_chunks * 2 * LANES, width), BF16),
        recv_v=pltpu.VMEM((per_node, width), F32),
        aown_v=pltpu.VMEM((per_node, width), F32),
        ahalo_v=pltpu.VMEM((per_halo, width), F32),
        table_v=pltpu.VMEM((per_halo, width), BF16),
        gmat_v=pltpu.VMEM((7 * width, width), F32),
        vsum_v=pltpu.VMEM((6 * 8, width), F32),
        pre_v=pltpu.VMEM((2, z.fwd_rows, width), F32),
        raw_v=pltpu.VMEM((2, z.fwd_rows, width), F32),
        upd_v=pltpu.VMEM((2, z.fwd_rows, width), BF16),
        dout_v=pltpu.VMEM((2, z.bwd_rows, width), BF16),
        dpre_v=pltpu.VMEM((2, z.bwd_rows, width), BF16),
        dall_v=pltpu.VMEM((rows, width), BF16),
        ncot_v=pltpu.VMEM((per_node, width), BF16),
        total_v=pltpu.VMEM((per_node, width), F32),
        rows_v=pltpu.VMEM((7 * width, width), BF16),
        first_v=pltpu.VMEM((7 * width, width), BF16),
        second_v=pltpu.VMEM((7 * width, width), BF16),
        list_v=pltpu.VMEM((2, z.samples * z.halo, width), BF16),
        halo_v=pltpu.VMEM((2, z.samples * z.halo, width), BF16),
        border_v=pltpu.VMEM((2, z.samples * z.halo, width), BF16),
        ret_v=pltpu.VMEM((2, z.samples * z.halo, width), BF16),
        gout_v=pltpu.VMEM((7 * width, width), BF16),
        edge_sem=pltpu.SemaphoreType.DMA((z.samples,)),
        cot_sem=pltpu.SemaphoreType.DMA((z.samples,)),
        eout_sem=pltpu.SemaphoreType.DMA((z.samples,)),
        egrad_sem=pltpu.SemaphoreType.DMA((z.samples,)),
        stat_v=pltpu.VMEM((PAIR, width, width), F32),
        bases_v=pltpu.VMEM((PAIR, width, width), F32),
        node_v=pltpu.VMEM((per_node, width), BF16),
        nout_v=pltpu.VMEM((per_node, width), BF16),
        ngrad_v=pltpu.VMEM((per_node, width), BF16),
        snew_v=pltpu.VMEM((PAIR, width, width), F32),
        work_v=pltpu.VMEM((PAIR, 2 * width, width), F32),
        hnew_v=pltpu.VMEM((3 * width, width), BF16),
        local_sem=pltpu.SemaphoreType.DMA((7,)),
        out_sem=pltpu.SemaphoreType.DMA((10,)),
        rows_sem=pltpu.SemaphoreType.DMA((2, 12)),
        first_sem=pltpu.SemaphoreType.DMA((2, 3)),
        second_sem=pltpu.SemaphoreType.DMA((2, 3)),
        halo_sem=pltpu.SemaphoreType.DMA((2, 2)),
        ret_sem=pltpu.SemaphoreType.DMA((2, 2)),
    )


def build_selectors(z, m, five_ref, send_ref):
    halo, nodes, slots = z.halo, z.nodes, z.slots
    lane = iota((LANES, LANES), 1)
    row = iota((LANES, LANES), 0)
    for g in range(z.edges // LANES):
        rows = slice(g * LANES, (g + 1) * LANES)
        line = jnp.broadcast_to(send_ref[g : g + 1, :].astype(F32), (LANES, LANES))
        column = line.T.astype(jnp.int32)
        for h in range(nodes // LANES):
            m.own_v[rows, h * LANES : (h + 1) * LANES] = ones_where(column == lane + (halo + h * LANES))
        place = jnp.where(column < halo, column, jnp.where(column >= halo + nodes, column - nodes, -1))
        in_halo = (place == (lane & (2 * halo - 1))) & (lane < 4 * halo)
        first = slots * (lane & (z.fwd_nodes - 1))
        local = row + (g * LANES) % z.fwd_rows
        m.sel_v[rows, 0:LANES] = ones_where((first <= local) & (local < first + slots))
        m.sel_v[rows, LANES : 2 * LANES] = ones_where(in_halo)
    place = iota((nodes + 2 * halo, z.bwd_rows), 0)
    place = jnp.where(place < nodes, place + halo, jnp.where(place < nodes + halo, place - nodes, place))
    first = slots * iota((LANES, z.bwd_rows), 0)
    local = iota((LANES, z.bwd_rows), 1)
    rep_t = ones_where((first <= local) & (local < first + slots))
    for c in range(z.bwd_chunks):
        lines = range(c * z.bwd_rows // LANES, (c + 1) * z.bwd_rows // LANES)
        senders = jnp.concatenate([send_ref[g : g + 1, :] for g in lines], 1)
        senders = jnp.broadcast_to(senders, place.shape)
        m.scat_v[c, 0 : nodes + 2 * halo, :] = ones_where(senders == place)
        m.scat_v[c, nodes + 2 * halo :, :] = rep_t
    first = slots * (iota((z.bwd_rows, 2 * LANES), 1) & (LANES - 1))
    local = iota((z.bwd_rows, 2 * LANES), 0)
    rep = ones_where((first <= local) & (local < first + slots))
    m.rep_v[...] = rep
    local = iota((z.bwd_rows, LANES), 0).astype(F32)
    slot = local - slots * jnp.floor((local + 0.5) * (1.0 / slots))
    for h in range(nodes // LANES):
        five = jnp.broadcast_to(five_ref[:, h * LANES : (h + 1) * LANES].astype(F32), (LANES, LANES)).T
        spread = dot_nn(rep[:, :LANES], five.astype(BF16))
        m.live_v[h * z.bwd_rows : (h + 1) * z.bwd_rows, :] = jnp.where(slot < slots - spread, 1.0, 0.0)


def both(column):
    return jnp.concatenate([column, column], 1)


def row_mean(value):
    return jnp.sum(value, -1, keepdims=True) * (1.0 / value.shape[-1])


def centred(value):
    centre = value - row_mean(value)
    return centre, lax.rsqrt(row_mean(centre * centre) + NORM_EPS)


def act_and_slope(half):
    turn = jnp.tanh(half)
    above = 1.0 + turn
    act = half * above
    return act, above + act * (1.0 - turn)


MESH = pl.DeviceIdType.MESH


def greet(partners):
    barrier = pltpu.get_barrier_semaphore()
    count = 0
    for device, exists in partners:
        if exists is None:
            pl.semaphore_signal(barrier, inc=1, device_id=device, device_id_type=MESH)
            count = count + 1
        else:
            pl.when(exists)(partial(pl.semaphore_signal, barrier, inc=1, device_id=device, device_id_type=MESH))
            count = count + exists.astype(jnp.int32)
    return lambda: pl.semaphore_wait(barrier, count)


def send(source, target, sems, slot, device):
    return pltpu.make_async_remote_copy(
        src_ref=source, dst_ref=target, send_sem=sems.at[0, slot], recv_sem=sems.at[1, slot],
        device_id=device, device_id_type=MESH,
    )


class Gather:
    def __init__(self, rows_v, sems, shard, fs, node):
        self.rows_v, self.sems, self.shard, self.fs = rows_v, sems, shard, fs
        self.parts = sems.shape[1] // 3
        self.next, self.far = (fs ^ 1, node), (fs ^ 2, node)

    def piece(self, owner, part):
        size = self.shard // self.parts
        return self.rows_v.at[pl.ds(pl.multiple_of(owner * self.shard + part * size, 16), size)]

    def copy(self, owner, part, slot, device):
        return send(self.piece(owner, part), self.piece(owner, part), self.sems, slot * self.parts + part, device)

    def start(self):
        for part in range(self.parts):
            self.copy(self.fs, part, 0, self.far).start()
        for part in range(self.parts):
            self.copy(self.fs, part, 1, self.next).start()

    def forward(self):
        for part in range(self.parts):
            self.copy(self.fs, part, 0, self.far).wait_recv()
            self.copy(self.fs ^ 2, part, 2, self.next).start()

    def finish(self):
        for part in range(self.parts):
            self.copy(self.fs, part, 0, self.far).wait_send()
            self.copy(self.fs, part, 1, self.next).wait()
            self.copy(self.fs ^ 2, part, 2, self.next).wait()


def list_matrix(send_ref, side, nodes):
    halo = send_ref.shape[1]
    listed = jnp.broadcast_to(send_ref[side : side + 1, :], (nodes, halo))
    return ones_where(listed == iota((nodes, halo), 0))


def sides(node, count):
    return ((node - 1, node > 0), (node + 1, node < count - 1))


class Cube:
    def __init__(self, count, fs=None, node=None):
        bits = count.bit_length() - 1
        self.node_bits = min(2, bits)
        self.size = 2 << self.node_bits
        self.extra = list(range(self.node_bits, bits))
        self.fs, self.node = fs, node
        if fs is not None:
            self.me = (fs >> 1) + 2 * (node & ((1 << self.node_bits) - 1))
        self.far_first = sorted(range(1, self.size), key=lambda r: (-r.bit_count(), -r))

    def device(self, r):
        return self.fs ^ (2 * (r & 1)), self.node ^ (r >> 1)

    def over(self, bit):
        return self.fs, self.node ^ (1 << bit)


def tree_sum(parts):
    while len(parts) > 1:
        parts = [left + right for left, right in zip(parts[::2], parts[1::2], strict=True)]
    return parts[0]


class Reduce:
    def __init__(self, cube, first, rows, sum_v, out_v, buffers):
        self.cube, self.sum_v, self.out_v = cube, sum_v, out_v
        self.give_v, self.land_v, self.near_v, self.cube_v, self.acc_v, self.extra_v, self.sems = buffers
        self.half = rows // 2
        self.size = self.half // cube.size
        core = cube.fs & 1
        self.keep, self.give = first + core * self.half, first + (1 - core) * self.half
        self.twin = (cube.fs ^ 1, cube.node)
        self.order = cube.far_first + [0]
        self.started = []

    @staticmethod
    def scratch(cube, rows, width):
        half, extra = rows // 2, max(2 * len(cube.extra), 1)
        size = half // cube.size
        return [
            pltpu.VMEM((half, width), BF16),
            pltpu.VMEM((half, width), BF16),
            pltpu.VMEM((half, width), BF16),
            pltpu.VMEM((cube.size, size, width), BF16),
            pltpu.VMEM((size, width), F32),
            pltpu.VMEM((extra, size, width), BF16),
            pltpu.SemaphoreType.DMA((2, 4 * cube.size + extra)),
        ]

    def rows(self, r, base=0):
        return pl.ds(pl.multiple_of(base + (self.cube.me ^ r) * self.size, 16), self.size)

    def launch(self, source, target, slot, device):
        copy = send(source, target, self.sems, slot, device)
        copy.start()
        self.started.append(copy)
        return copy

    def begin(self):
        self.core = {}
        for r in self.order:
            part = self.give_v.at[self.rows(r)]
            part[...] = self.sum_v[self.rows(r, self.give), :].astype(BF16)
            self.core[r] = self.launch(part, self.land_v.at[self.rows(r)], r, self.twin)

    def spread(self):
        self.near = {}
        for r in self.order:
            self.core[r].wait_recv()
            total = self.sum_v[self.rows(r, self.keep), :] + self.land_v[self.rows(r), :].astype(F32)
            if r:
                part = self.near_v.at[self.rows(r)]
                part[...] = total.astype(BF16)
                self.near[r] = self.launch(part, self.cube_v.at[r], self.cube.size + r, self.cube.device(r))
            else:
                self.acc_v[...] = total

    def meet(self):
        total = self.acc_v[...]
        for r in reversed(self.cube.far_first):
            self.near[r].wait_recv()
            total = total + self.cube_v[r].astype(F32)
        self.far = None
        if self.cube.extra:
            self.exchange(total, 0)
        else:
            self.acc_v[...] = total

    def exchange(self, total, e):
        self.extra_v[2 * e] = total.astype(BF16)
        self.far = self.launch(
            self.extra_v.at[2 * e], self.extra_v.at[2 * e + 1], 4 * self.cube.size + e, self.cube.over(self.cube.extra[e])
        )

    def settle(self):
        total = self.acc_v[...]
        for e in range(len(self.cube.extra)):
            self.far.wait_recv()
            total = self.extra_v[2 * e].astype(F32) + self.extra_v[2 * e + 1].astype(F32)
            if e + 1 < len(self.cube.extra):
                self.exchange(total, e + 1)
        own = self.out_v.at[self.rows(0, self.keep)]
        own[...] = total.astype(BF16)
        size = self.cube.size
        self.back = {r: self.launch(own, own, 2 * size + r, self.cube.device(r)) for r in self.cube.far_first}
        self.last = [self.launch(own, own, 3 * size, self.twin)]

    def forward(self):
        for r in reversed(self.cube.far_first):
            self.back[r].wait_recv()
            part = self.out_v.at[self.rows(r, self.keep)]
            self.last.append(self.launch(part, part, 3 * self.cube.size + r, self.twin))

    def arrive(self):
        for copy in self.last:
            copy.wait_recv()

    def end(self):
        for copy in self.started:
            copy.wait_send()


class VectorSum:
    def __init__(self, cube, send_v, land_v, sems):
        self.cube, self.send_v, self.land_v, self.sems = cube, send_v, land_v, sems
        self.started = []

    @staticmethod
    def scratch(cube, shape):
        extra = len(cube.extra)
        return [
            pltpu.VMEM((2 + extra,) + shape, F32),
            pltpu.VMEM((cube.size + extra,) + shape, F32),
            pltpu.SemaphoreType.DMA((2, cube.size + extra)),
        ]

    def launch(self, source, slot, device):
        copy = send(self.send_v.at[source], self.land_v.at[slot], self.sems, slot, device)
        copy.start()
        self.started.append(copy)
        return copy

    def begin(self, value):
        self.send_v[0] = value
        self.core = self.launch(0, 0, (self.cube.fs ^ 1, self.cube.node))

    def spread(self):
        self.core.wait_recv()
        self.send_v[1] = self.send_v[0] + self.land_v[0]
        self.near = [self.launch(1, r, self.cube.device(r)) for r in range(1, self.cube.size)]

    def meet(self):
        for copy in self.near:
            copy.wait_recv()
        self.total = tree_sum([self.send_v[1]] + [self.land_v[r] for r in range(1, self.cube.size)])
        self.far = self.exchange(0) if self.cube.extra else None

    def exchange(self, e):
        self.send_v[2 + e] = self.total
        return self.launch(2 + e, self.cube.size + e, self.cube.over(self.cube.extra[e]))

    def settle(self):
        for e in range(len(self.cube.extra)):
            self.far.wait_recv()
            self.total = self.total + self.land_v[self.cube.size + e]
            if e + 1 < len(self.cube.extra):
                self.far = self.exchange(e + 1)
        return self.total

    def end(self):
        for copy in self.started:
            copy.wait_send()


BLOCK = 32
COUNT = 4
PAIR = 2
AHEAD = 4
HALF = LANES // BLOCK


def wide_left(value):
    high, low = split(value)
    return jnp.concatenate([high, high, low], 1)


def wide_right(value):
    high, low = split(value)
    return jnp.concatenate([high, low, high], 1)


def dot_three(left, right):
    return dot_nt(wide_left(left), wide_right(right))


def factor_block(packed):
    sub = iota((8, LANES), 0)
    lane = iota((8, LANES), 1)
    tiles = BLOCK // 8
    group = lane & (LANES - BLOCK)
    plain = [packed[8 * r : 8 * r + 8, :] for r in range(tiles)]
    columns = {}

    def take_columns(panel):
        for l in range(8 * panel, 8 * panel + 8):
            columns[l] = [None] * panel + [jnp.take_along_axis(part, group + l, axis=1) for part in plain[panel:]]

    take_columns(0)
    inverse = [jnp.where((lane & (BLOCK - 1)) == sub + 8 * r, 1.0, 0.0) for r in range(tiles)]

    def line(tile, s):
        return jnp.broadcast_to(tile[s : s + 1, :], (8, LANES))

    for j in range(BLOCK):
        rj, sj = j // 8, j % 8
        scale = lax.rsqrt(line(columns[j][rj], sj))
        below = [None if r < rj else columns[j][r] * scale for r in range(tiles)]
        below[rj] = jnp.where(sub > sj, below[rj], 0.0)
        for l in [l for l in columns if l > j]:
            weight = line(below[l // 8], l % 8)
            for r in range(l // 8, tiles):
                columns[l][r] = columns[l][r] - below[r] * weight
        if j < BLOCK - 8 - AHEAD:
            row = line(plain[rj], sj) * scale
            for r in range(rj, tiles):
                plain[r] = plain[r] - below[r] * row
        if j % 8 == 7 - AHEAD and j < BLOCK - 8:
            take_columns(rj + 1)
        row = line(inverse[rj], sj) * scale
        inverse[rj] = jnp.where(sub == sj, row, inverse[rj] - below[rj] * row)
        for r in range(rj + 1, tiles):
            inverse[r] = inverse[r] - below[r] * row
    return jnp.concatenate(inverse, 0)


def turned_blocks(k, width):
    return [h * HALF + (g - k) % HALF for h in range(width // LANES) for g in range(HALF)]


def pick_rows(value, blocks):
    return jnp.concatenate([value[i * BLOCK : (i + 1) * BLOCK, :] for i in blocks], 0)


def orthogonalize(work_v, bases_out, width, beside):
    blocks = width // BLOCK
    group = iota((BLOCK, LANES), 1) // BLOCK
    square = iota((LANES, LANES), 0) // BLOCK == iota((LANES, LANES), 1) // BLOCK

    def placed(values, b):
        return [jnp.where(group == (b + k) % COUNT, values[k], jnp.zeros_like(values[k])) for k in range(COUNT)]

    def lanes_of(b):
        return slice(b // HALF * LANES, (b // HALF + 1) * LANES)

    def rows_of(b):
        return slice(b * BLOCK, (b + 1) * BLOCK)

    packed = sum(placed([work_v[k, rows_of(0), lanes_of(0)] for k in range(COUNT)], 0))
    for b in range(blocks):
        beside(b)
        lanes, after = lanes_of(b), (b + 1) * BLOCK
        high, low = split(factor_block(packed).astype(F32))
        high, low = placed([high] * COUNT, b), placed([low] * COUNT, b)
        if b < blocks - 1:
            spread_high, spread_low = jnp.concatenate(high, 0), jnp.concatenate(low, 0)
            spread = jnp.concatenate([spread_high, spread_low, spread_high], 1)
            ahead = jnp.concatenate([work_v[k, rows_of(b + 1), lanes] for k in range(COUNT)], 0)
            turned = jnp.where(square, dot_nt(wide_left(ahead), spread), 0.0)
            order = [(g - b - 1) % COUNT for g in range(COUNT)]
            update = dot_nt(wide_left(turned), pick_rows(wide_right(turned), order))
            current = placed([work_v[k, rows_of(b + 1), lanes_of(b + 1)] for k in range(COUNT)], b + 1)
            packed = sum(current) - sum(update[rows_of(k), :] for k in range(COUNT))
        start = after // LANES * LANES
        for k in range(COUNT):
            four_high = jnp.concatenate([high[k]] * HALF, 0)
            four_low = jnp.concatenate([low[k]] * HALF, 0)
            below = wide_left(work_v[k, after:, lanes])
            turned = dot_nt(below, jnp.concatenate([four_high, four_low, four_high], 1))
            mine = iota((width, LANES), 1) // BLOCK == b % HALF
            bases_out[k, :, lanes] = jnp.where(mine, turned[width - after :, :], bases_out[k, :, lanes])
            if b == blocks - 1:
                continue
            turned_high, turned_low = split(turned)
            part = iota(turned.shape, 1) // BLOCK
            zero = jnp.zeros_like(turned_high)
            left = jnp.where(part == 2, turned_low, jnp.where(part == 3, zero, turned_high))
            right = jnp.where(part == 1, turned_low, jnp.where(part == 3, zero, turned_high))
            right = jnp.concatenate(
                [
                    right[(i - b - 1) * BLOCK : (i - b) * BLOCK, :] if i > b else zero[0:BLOCK, :]
                    for i in turned_blocks(k, width)[start // BLOCK :]
                ],
                0,
            )
            work_v[k, after:, start:] -= dot_nt(left, right)


def matrix_bounds(width):
    return [0, 3 * width, 4 * width, 6 * width, 7 * width]


def new_statistics(rows, stat):
    return BETA_TWO * stat + (1.0 - BETA_TWO) * dot_tn(rows, rows)


def matrix_of(row, width):
    return sum((row >= bound).astype(jnp.int32) for bound in matrix_bounds(width)[1:-1])


def prepare_bases(stat, basis, k):
    width = stat.shape[-1]
    order = turned_blocks(k, width)
    flipped = basis.T
    proj_rows = dot_three(flipped, stat)
    gram = dot_three(proj_rows, pick_rows(proj_rows, order))
    return gram, dot_three(stat, pick_rows(flipped, order))


def adam_step(first, second, rotated):
    first = BETA_ONE * first + (1.0 - BETA_ONE) * rotated
    second = BETA_TWO * second + (1.0 - BETA_TWO) * rotated * rotated
    square = second * (1.0 / (1.0 - BETA_TWO**STEP))
    root = square * lax.rsqrt(jnp.maximum(square, TINY))
    return first, second, first * (1.0 / (1.0 - BETA_ONE**STEP)) * (1.0 / (root + ADAM_EPS))


def turn(rows, basis):
    high, low = split(basis)
    return dot_nn(rows, high) + dot_nn(rows, low)


def decayed(kern, turned):
    return kern - RATE_MATRIX * (turned + DECAY_RATE * kern)


def rounded_rows(grad, basis, kern, first, second):
    _, _, step = adam_step(first.astype(F32), second.astype(F32), turn(grad, basis))
    return decayed(kern.astype(F32), dot_nt(step.astype(BF16), basis.astype(BF16))).astype(BF16)


def round_kernel(
    z, names, count, edge_ref, cot_ref, node_hbm, ncot_ref, five_ref, send_ref, list_ref, kern_ref, kfirst_ref, ksecond_ref,
    vec_ref, stat_ref, bases_ref, eout_ref, egrad_ref, nout_hbm, ngrad_hbm, grad_ref, gvec_ref, rows_ref, first_ref, second_ref,
    stat_hbm, work_hbm, half_hbm, *scratch,
):
    m = type("Held", (), {})()
    for name, ref in zip(names, scratch[: len(names)], strict=True):
        setattr(m, name, ref)
    spare = scratch[len(names) :]
    fs, node_id = lax.axis_index("fs"), lax.axis_index("nodes")
    cube = Cube(count, fs, node_id)
    around = sides(node_id, count)
    shard = kern_ref.shape[0]
    width, nodes, edges, samples, halo = z.width, z.nodes, z.edges, z.samples, z.halo
    two_halo = 2 * halo

    def sample_copy(source, target, sem, s):
        rows = aligned(s, edges)
        return pltpu.make_async_copy(source.at[rows], target.at[rows], sem.at[s])

    weight_ref = m.rows_v
    mine = pl.ds(pl.multiple_of(fs * shard, 16), shard)
    staged = [pl.ds(i * shard, shard) for i in range(3)]
    locals_in = [
        pltpu.make_async_copy(source, target, m.local_sem.at[i])
        for i, (source, target) in enumerate(
            [
                (kern_ref, m.slope_v.at[staged[0]]), (node_hbm, m.node_v), (kfirst_ref, m.slope_v.at[staged[1]]),
                (ksecond_ref, m.slope_v.at[staged[2]]), (ncot_ref, m.ncot_v),
                (stat_ref.at[pl.ds(PAIR, PAIR)], m.stat_v), (bases_ref.at[pl.ds(PAIR, PAIR)], m.bases_v),
            ]
        )
    ]
    node_ref, nout_ref, ngrad_ref = m.node_v, m.nout_v, m.ngrad_v
    stat_out, work_out, half_out = m.snew_v, m.work_v, m.hnew_v

    def start_out(i, source, target):
        copy = pltpu.make_async_copy(source, target, m.out_sem.at[i])
        copy.start()
        outs.append(copy)

    outs = []
    gather = Gather(weight_ref, m.rows_sem, shard, fs, node_id)
    moments = [Gather(m.first_v, m.first_sem, shard, fs, node_id), Gather(m.second_v, m.second_sem, shard, fs, node_id)]
    for copy in locals_in[:2]:
        copy.start()
    m.halo_v[...] = jnp.zeros_like(m.halo_v)
    m.ret_v[...] = jnp.zeros_like(m.ret_v)
    all_in = greet(
        [(gather.next, None)]
        + [(cube.device(r), None) for r in range(1, cube.size)]
        + [(cube.over(bit), None) for bit in cube.extra]
        + [((fs, other), exists) for other, exists in around]
    )
    locals_in[0].wait()
    weight_ref[mine, :] = m.slope_v[staged[0], :].astype(BF16)
    all_in()
    gather.start()
    for copy in locals_in[2:]:
        copy.start()
    for s in range(samples):
        sample_copy(edge_ref, m.edge_v, m.edge_sem, s).start()
    for s in range(samples):
        sample_copy(cot_ref, m.cot_v, m.cot_sem, s).start()

    def to_side(source, target, sems, side, other):
        return send(source.at[side], target.at[1 - side], sems, side, (fs, other))

    def start_sides(source, target, sems):
        for side, (other, exists) in enumerate(around):
            pl.when(exists)(lambda side=side, other=other: to_side(source, target, sems, side, other).start())

    def finish_sides(source, target, sems):
        for side, (other, exists) in enumerate(around):
            def settle(side=side, other=other):
                to_side(source, target, sems, side, other).wait_send()
                to_side(source, target, sems, 1 - side, other).wait_recv()
            pl.when(exists)(settle)

    locals_in[1].wait()
    for side in range(2):
        chosen = list_matrix(list_ref, side, nodes)
        for s in range(samples):
            m.list_v[side, s * halo : (s + 1) * halo, :] = dot_tn(
                chosen, node_ref[s * nodes : (s + 1) * nodes, :]
            ).astype(BF16)
    start_sides(m.list_v, m.halo_v, m.halo_sem)
    build_selectors(z, m, five_ref, send_ref)
    gather.forward()
    gather.finish()
    finish_sides(m.list_v, m.halo_v, m.halo_sem)
    start_out(0, weight_ref, rows_ref)
    for copy in locals_in[2:]:
        copy.wait()
    for k, (moment, held) in enumerate(zip(moments, (m.first_v, m.second_v), strict=True)):
        held[mine, :] = m.slope_v[staged[k + 1], :].astype(BF16)
        moment.start()
    m.half_v[...] = weight_ref[...] * jnp.asarray(0.5, BF16)
    m.gmat_v[...] = jnp.zeros_like(m.gmat_v)
    m.vsum_v[...] = jnp.zeros_like(m.vsum_v)
    m.aown_v[...] = jnp.zeros_like(m.aown_v)
    m.ahalo_v[...] = jnp.zeros_like(m.ahalo_v)
    for s in range(samples):
        for side in range(2):
            m.table_v[s * two_halo + side * halo : s * two_halo + (side + 1) * halo, :] = m.halo_v[
                side, s * halo : (s + 1) * halo, :
            ]

    send_half = m.half_v[width : 2 * width, :]
    recv_half = m.half_v[2 * width : 3 * width, :]
    bias_edge, gain_edge, shift_edge = vec_ref[0:1, :] * 0.5, vec_ref[1:2, :], vec_ref[2:3, :]
    bias_node, gain_node, shift_node = vec_ref[3:4, :] * 0.5, vec_ref[4:5, :], vec_ref[5:6, :]

    for s in range(samples):
        node = node_ref[s * nodes : (s + 1) * nodes, :]
        m.pown_v[s * nodes : (s + 1) * nodes, :] = dot_nn(node, send_half).astype(BF16)
        high, low = split(dot_nn(node, recv_half) + bias_edge)
        out_high, out_low = split(dot_nn(m.table_v[s * two_halo : (s + 1) * two_halo, :], send_half))
        zero = jnp.zeros((2 * LANES - 2 * z.fwd_nodes - 2 * two_halo, width), BF16)
        for c in range(z.fwd_chunks):
            own = slice(c * z.fwd_nodes, (c + 1) * z.fwd_nodes)
            base = (s * z.fwd_chunks + c) * 2 * LANES
            m.psel_v[base : base + 2 * LANES, :] = jnp.concatenate(
                [high[own], low[own], out_high, out_low, zero], 0
            )

    per = z.fwd_chunks
    last = samples * per - 1

    def join_edges(i, slot):
        s, c = i // per, i % per
        local = aligned(c, z.fwd_rows)
        left = jnp.concatenate([m.edge_v[aligned(i, z.fwd_rows), :], m.own_v[local, :], m.sel_v[local, :]], 1)
        right = jnp.concatenate(
            [m.half_v[0:width, :], m.pown_v[aligned(s, nodes), :], m.psel_v[aligned(i, 2 * LANES), :]], 0
        )
        m.pre_v[slot] = dot_nn(left, right)

    def activate(i, slot):
        rows = aligned(i, z.fwd_rows)
        act, slope = act_and_slope(m.pre_v[slot])
        act = act.astype(BF16)
        m.act_v[rows, :] = act
        m.slope_v[rows, :] = slope
        m.raw_v[slot] = dot_nn(act, weight_ref[3 * width : 4 * width, :])

    def update_edges(i, slot):
        rows, local = aligned(i, z.fwd_rows), aligned(i % per, z.fwd_rows)
        centre, inv = centred(m.raw_v[slot])
        live = m.live_v[local, :]
        inv = inv * live
        m.inv_v[rows, :] = inv
        normed = centre * both(inv)
        m.norm_v[rows, :] = normed.astype(BF16)
        update = normed * gain_edge + both(live) * shift_edge
        m.edge_out_v[rows, :] = (m.edge_v[rows, :].astype(F32) + update).astype(BF16)
        m.upd_v[slot] = update.astype(BF16)

    def gather_updates(i, slot):
        take = slice(nodes + two_halo, nodes + two_halo + z.fwd_nodes)
        gathered = dot_nn(m.scat_v[0, take, 0 : z.fwd_rows], m.upd_v[slot])
        m.gath_v[aligned(i, z.fwd_nodes), :] = gathered.astype(BF16)

    def edge_in(s):
        return sample_copy(edge_ref, m.edge_v, m.edge_sem, s)

    edge_in(0).wait()
    join_edges(0, 0)

    def forward(s, carry):
        pl.when(s < samples - 1)(lambda: edge_in(s + 1).wait())
        for c in range(per):
            i = s * per + c
            join_edges(jnp.minimum(i + 1, last), (c + 1) % 2)
            gather_updates(jnp.maximum(i - 2, 0), c % 2)
            activate(i, c % 2)
            update_edges(jnp.maximum(i - 1, 0), (c + 1) % 2)
        pl.when(s > 0)(lambda: sample_copy(m.edge_out_v, eout_ref, m.eout_sem, s - 1).start())
        return carry

    lax.fori_loop(0, samples, forward, 0)
    gather_updates(last - 1, 0)
    update_edges(last, 1)
    gather_updates(last, 1)
    sample_copy(m.edge_out_v, eout_ref, m.eout_sem, samples - 1).start()

    def node_part(i, carry):
        rows = aligned(i, 2 * nodes)
        node, gath = node_ref[rows, :], m.gath_v[rows, :]
        joined = jnp.concatenate([node, gath], 1)
        act, slope = act_and_slope(dot_nn(joined, m.half_v[4 * width : 6 * width, :]) + bias_node)
        act = act.astype(BF16)
        centre, inv = centred(dot_nn(act, weight_ref[6 * width : 7 * width, :]))
        normed = centre * inv
        nout_ref[rows, :] = (node.astype(F32) + normed * gain_node + shift_node).astype(BF16)
        back = m.ncot_v[rows, :].astype(F32)
        back_normed = back * normed
        scaled, scaled_normed = back * gain_node, back_normed * gain_node
        d_out = (inv * (scaled - row_mean(scaled) - normed * row_mean(scaled_normed))).astype(BF16)
        m.gmat_v[6 * width : 7 * width, :] += dot_tn(act, d_out)
        m.vsum_v[32:40, :] += fold_rows(back_normed)
        m.vsum_v[40:48, :] += fold_rows(back)
        d_pre = dot_nt(d_out, m.half_v[6 * width : 7 * width, :]) * slope
        d_pre = d_pre.astype(BF16)
        m.vsum_v[24:32, :] += fold_rows(d_pre.astype(F32))
        m.gmat_v[4 * width : 6 * width, :] += dot_tn(joined, d_pre)
        d_joined = dot_nt(d_pre, weight_ref[4 * width : 6 * width, :])
        m.total_v[rows, :] = back + d_joined[:, :width]
        high, low = split(d_joined[:, width:])
        for k in range(2):
            for c in range(z.bwd_chunks):
                own = slice(k * nodes + c * z.bwd_nodes, k * nodes + (c + 1) * z.bwd_nodes)
                m.drep_v[aligned((i * 2 + k) * z.bwd_chunks + c, 2 * LANES), :] = jnp.concatenate(
                    [high[own], low[own]], 0
                )
        return carry

    lax.fori_loop(0, samples // 2, node_part, 0)

    halves = z.bwd_rows // z.fwd_rows
    pairs = samples * z.bwd_chunks

    def spread_back(i, slot):
        half = slice((slot % halves) * z.fwd_rows, (slot % halves + 1) * z.fwd_rows)
        m.pre_v[slot] = dot_nn(m.rep_v[half, :], m.drep_v[aligned(i // halves, 2 * LANES), :])

    def norm_back(i, slot, pair):
        rows, local = aligned(i, z.fwd_rows), aligned(i % per, z.fwd_rows)
        d_update = (m.cot_v[rows, :].astype(F32) + m.pre_v[slot]) * both(m.live_v[local, :])
        normed = m.norm_v[rows, :].astype(F32)
        d_normed = d_update * normed
        m.vsum_v[8:16, :] += fold_rows(d_normed)
        m.vsum_v[16:24, :] += fold_rows(d_update)
        scaled, scaled_normed = d_update * gain_edge, d_normed * gain_edge
        d_out = both(m.inv_v[rows, :]) * (scaled - row_mean(scaled) - normed * row_mean(scaled_normed))
        m.dout_v[pair, slot * z.fwd_rows : (slot + 1) * z.fwd_rows, :] = d_out.astype(BF16)

    def activate_back(i, slot, pair):
        part = slice(slot * z.fwd_rows, (slot + 1) * z.fwd_rows)
        d_act = dot_nt(m.dout_v[pair, part, :], m.half_v[3 * width : 4 * width, :])
        d_pre = (d_act * m.slope_v[aligned(i, z.fwd_rows), :]).astype(BF16)
        m.dpre_v[pair, part, :] = d_pre
        m.dall_v[aligned(i, z.fwd_rows), :] = d_pre

    def weights_back(p, pair):
        s, c = p // z.bwd_chunks, p % z.bwd_chunks
        rows = aligned(p, z.bwd_rows)
        d_out, d_pre = m.dout_v[pair], m.dpre_v[pair]
        m.gmat_v[3 * width : 4 * width, :] += dot_tn(m.act_v[rows, :], d_out)
        m.gmat_v[0:width, :] += dot_tn(m.edge_v[rows, :], d_pre)
        sums = dot_nn(m.scat_v[c], d_pre)
        m.aown_v[aligned(s, nodes), :] += sums[0:nodes, :]
        m.ahalo_v[aligned(s, two_halo), :] += sums[nodes : nodes + two_halo, :]
        m.recv_v[aligned(p, z.bwd_nodes), :] = sums[nodes + two_halo :, :]

    m.dout_v[1] = jnp.zeros_like(m.dout_v[1])
    m.dpre_v[1] = jnp.zeros_like(m.dpre_v[1])
    spread_back(0, 0)

    def backward(s, carry):
        sample_copy(cot_ref, m.cot_v, m.cot_sem, s).wait()
        for k in range(z.bwd_chunks):
            p = s * z.bwd_chunks + k
            i = p * halves
            spread_back(i + 1, 1)
            activate_back(jnp.maximum(i - 1, 0), 1, 1 - k)
            norm_back(i, 0, k)
            weights_back(jnp.maximum(p - 1, 0), 1 - k)
            spread_back(jnp.minimum(i + 2, last), 0)
            activate_back(i, 0, k)
            norm_back(i + 1, 1, k)
        return carry

    nodes_sum = Reduce(cube, 4 * width, 3 * width, m.gmat_v, m.gout_v, spare[7:14])
    nodes_sum.begin()
    start_out(1, nout_ref, nout_hbm)
    lax.fori_loop(0, 1, backward, 0)
    nodes_sum.spread()
    lax.fori_loop(1, samples, backward, 0)
    activate_back(last, 1, 1)
    weights_back(pairs - 1, 1)

    def edge_gradient(s, carry):
        for c in range(per):
            rows = aligned(s * per + c, z.fwd_rows)
            d_edge = dot_nt(m.dall_v[rows, :], weight_ref[0:width, :])
            m.edge_out_v[rows, :] = (m.cot_v[rows, :].astype(F32) + d_edge).astype(BF16)
        sample_copy(m.edge_out_v, egrad_ref, m.egrad_sem, s).start()
        return carry

    send_full = weight_ref[width : 2 * width, :]
    recv_full = weight_ref[2 * width : 3 * width, :]
    table = m.table_v[...]
    out_high, out_low = split(m.ahalo_v[...])
    nodes_all = node_ref[...]
    grad_send = dot_tn(table, out_high) + dot_tn(nodes_all, m.aown_v[...].astype(BF16))
    grad_recv = dot_tn(nodes_all, m.recv_v[...].astype(BF16))
    m.gmat_v[width : 2 * width, :] = grad_send
    m.gmat_v[2 * width : 3 * width, :] = grad_recv
    reduce = Reduce(cube, 0, 4 * width, m.gmat_v, m.gout_v, spare[:7])
    vectors = VectorSum(cube, *spare[14:])
    reduce.begin()
    nodes_sum.meet()
    border = (dot_nt(out_high, send_full) + dot_nt(out_low, send_full)).astype(BF16)
    for s in range(samples):
        for side in range(2):
            m.border_v[side, s * halo : (s + 1) * halo, :] = border[
                s * two_halo + side * halo : s * two_halo + (side + 1) * halo, :
            ]
    start_sides(m.border_v, m.ret_v, m.ret_sem)
    for s in range(samples):
        m.vsum_v[0:8, :] += fold_rows(m.recv_v[s * nodes : (s + 1) * nodes, :])
    vectors.begin(
        jnp.concatenate(
            [jnp.sum(m.vsum_v[k * 8 : (k + 1) * 8, :], 0, keepdims=True) for k in range(6)]
            + [jnp.zeros((2, width), F32)],
            0,
        )
    )
    reduce.spread()
    vectors.spread()
    for moment in moments:
        moment.forward()
    for s in range(samples):
        sample_copy(m.edge_out_v, eout_ref, m.eout_sem, s).wait()
    lax.fori_loop(0, samples, edge_gradient, 0)
    nodes_sum.settle()
    for s in range(samples):
        rows = slice(s * nodes, (s + 1) * nodes)
        recv_high, recv_low = split(m.recv_v[rows, :])
        own_high, own_low = split(m.aown_v[rows, :])
        m.total_v[rows, :] += (
            dot_nt(recv_high, recv_full) + dot_nt(recv_low, recv_full)
            + dot_nt(own_high, send_full) + dot_nt(own_low, send_full)
        )
    reduce.meet()
    vectors.meet()
    nodes_sum.forward()
    finish_sides(m.border_v, m.ret_v, m.ret_sem)
    low, high = (list_matrix(list_ref, side, nodes) for side in range(2))
    for s in range(samples):
        rows, part = slice(s * nodes, (s + 1) * nodes), slice(s * halo, (s + 1) * halo)
        ngrad_ref[rows, :] = (
            m.total_v[rows, :] + dot_nn(low, m.ret_v[0, part, :]) + dot_nn(high, m.ret_v[1, part, :])
        ).astype(BF16)
    start_out(2, ngrad_ref, ngrad_hbm)
    reduce.settle()
    gvec_ref[...] = vectors.settle()
    nodes_sum.arrive()
    bounds = matrix_bounds(width)
    for k in range(PAIR):
        stat_out[k] = new_statistics(m.gout_v[bounds[PAIR + k] : bounds[PAIR + k + 1], :], m.stat_v[k])
    start_out(5, m.gout_v.at[pl.ds(4 * width, 3 * width)], grad_ref.at[pl.ds(4 * width, 3 * width)])
    start_out(6, stat_out, stat_hbm)
    for k in range(PAIR):
        work_out[k, 0:width, :], work_out[k, width:, :] = prepare_bases(stat_out[k], m.bases_v[k], PAIR + k)
    start_out(7, work_out, work_hbm)
    for moment in moments:
        moment.finish()
    start_out(3, m.first_v.at[pl.ds(0, 4 * width)], first_ref)
    start_out(4, m.second_v.at[pl.ds(0, 4 * width)], second_ref)
    for k in range(PAIR):
        low, high = bounds[PAIR + k], bounds[PAIR + k + 1]
        half_out[low - 4 * width : high - 4 * width, :] = rounded_rows(
            m.gout_v[low:high, :], m.bases_v[k], weight_ref[low:high, :], m.first_v[low:high, :], m.second_v[low:high, :]
        )
    start_out(8, half_out, half_hbm)
    for s in range(samples):
        sample_copy(m.edge_out_v, egrad_ref, m.egrad_sem, s).wait()
    for copy in outs:
        copy.wait()
    reduce.forward()
    reduce.arrive()
    grad_out = pltpu.make_async_copy(m.gout_v.at[pl.ds(0, 4 * width)], grad_ref.at[pl.ds(0, 4 * width)], m.out_sem.at[9])
    grad_out.start()
    reduce.end()
    nodes_sum.end()
    vectors.end()
    grad_out.wait()


def round_call(z, count, edge, cot, node, ncot, five, senders, send_rows, kern, kfirst, ksecond, vectors, stat, bases):
    shard, width = kern.shape
    scratch = main_scratch(z)
    cube = Cube(count)
    spare = Reduce.scratch(cube, 4 * width, width) + Reduce.scratch(cube, 3 * width, width) + VectorSum.scratch(cube, (8, width))
    rows, per_node = z.samples * z.edges, z.samples * z.nodes
    whole = pl.BlockSpec(memory_space=pltpu.VMEM)
    anywhere = pl.BlockSpec(memory_space=pl.ANY)
    total = jax.ShapeDtypeStruct((7 * width, width), BF16)
    moments = jax.ShapeDtypeStruct((4 * width, width), BF16)
    return pl.pallas_call(
        partial(round_kernel, z, tuple(scratch), count),
        out_shape=(
            jax.ShapeDtypeStruct((rows, width), BF16),
            jax.ShapeDtypeStruct((rows, width), BF16),
            jax.ShapeDtypeStruct((per_node, width), BF16),
            jax.ShapeDtypeStruct((per_node, width), BF16),
            total,
            jax.ShapeDtypeStruct((8, width), F32),
            total, moments, moments,
            jax.ShapeDtypeStruct((PAIR, width, width), F32),
            jax.ShapeDtypeStruct((PAIR, 2 * width, width), F32),
            jax.ShapeDtypeStruct((3 * width, width), BF16),
        ),
        in_specs=[anywhere] * 4 + [whole] * 3 + [anywhere] * 3 + [whole] + [anywhere] * 2,
        out_specs=(anywhere,) * 5 + (whole,) + (anywhere,) * 6,
        scratch_shapes=list(scratch.values()) + spare,
        compiler_params=pltpu.CompilerParams(
            collective_id=0, has_side_effects=True, vmem_limit_bytes=VMEM_LIMIT
        ),
        name="edge_node_round",
    )(edge, cot, node, ncot, five, senders, send_rows, kern, kfirst, ksecond, vectors, stat, bases)


def update_kernel(
    grad_ref, stat_ref, bases_ref, kern_ref, kfirst_ref, ksecond_ref, rows_ref, first_ref, second_ref,
    gvec_ref, vec_ref, vfirst_ref, vsecond_ref, work_ref, eout_ref, egrad_ref, nout_ref, ngrad_ref, spair_ref, hpair_ref,
    eout_out, egrad_out, nout_out, ngrad_out, kern_out, kfirst_out, ksecond_out, vec_out, vfirst_out, vsecond_out,
    stat_out, bases_out, half_out,
    grad_v, stat_v, bases_v, kern_v, kfirst_v, ksecond_v, rows_v, first_v, second_v,
    work_v, kern_new, kfirst_new, ksecond_new, stat_new, bases_new, half_v, eout_v, egrad_v, nout_v, ngrad_v, spair_v, hpair_v, in_sem, out_sem, pass_sem,
):
    shard, width = kern_v.shape
    copies = [
        pltpu.make_async_copy(source, target, in_sem.at[i])
        for i, (source, target) in enumerate(
            [
                (bases_ref, bases_v), (stat_ref.at[pl.ds(0, PAIR)], stat_v), (grad_ref, grad_v),
                (work_ref, work_v.at[pl.ds(PAIR, PAIR)]), (kern_ref, kern_v), (kfirst_ref, kfirst_v),
                (ksecond_ref, ksecond_v), (rows_ref, rows_v), (first_ref, first_v), (second_ref, second_v),
            ]
        )
    ]
    passed = [
        (pltpu.make_async_copy(source, held, pass_sem.at[0, i]), pltpu.make_async_copy(held, target, pass_sem.at[1, i]))
        for i, (source, held, target) in enumerate(
            [
                (eout_ref, eout_v, eout_out), (egrad_ref, egrad_v, egrad_out),
                (nout_ref, nout_v, nout_out), (ngrad_ref, ngrad_v, ngrad_out),
                (spair_ref, spair_v, stat_out.at[pl.ds(PAIR, PAIR)]),
                (hpair_ref, hpair_v, half_out.at[pl.ds(4 * width, 3 * width)]),
            ]
        )
    ]
    outs = [
        pltpu.make_async_copy(source, target, out_sem.at[i])
        for i, (source, target) in enumerate(
            [
                (stat_new, stat_out.at[pl.ds(0, PAIR)]), (kern_new, kern_out), (kfirst_new, kfirst_out), (ksecond_new, ksecond_out),
                (half_v, half_out.at[pl.ds(0, 4 * width)]), (bases_new, bases_out),
            ]
        )
    ]
    for copy in copies:
        copy.start()
    bases_new[...] = jnp.zeros_like(bases_new)
    for copy in copies[:3]:
        copy.wait()
    bounds = matrix_bounds(width)
    for k in range(PAIR):
        stat_new[k] = new_statistics(grad_v[bounds[k] : bounds[k + 1], :], stat_v[k])
    outs[0].start()
    for copy in copies[3:]:
        copy.wait()
    for copy, _ in passed:
        copy.start()
    for k in range(PAIR):
        work_v[k, 0:width, :], work_v[k, width:, :] = prepare_bases(stat_new[k], bases_v[k], k)

    def own_rows():
        first_row = lax.axis_index("fs") * shard
        grad = grad_v[pl.ds(pl.multiple_of(first_row, 64), shard), :]
        one = matrix_of(first_row, width)
        two = matrix_of(first_row + shard - 1, width)
        in_two = matrix_of(first_row + iota((shard, width), 0), width) != one
        basis_one, basis_two = bases_v[one], bases_v[two]
        rotated = jnp.where(in_two, turn(grad, basis_two), turn(grad, basis_one))
        kfirst_new[...], ksecond_new[...], step = adam_step(kfirst_v[...], ksecond_v[...], rotated)
        turned = jnp.where(in_two, dot_three(step, basis_two), dot_three(step, basis_one))
        kern_new[...] = decayed(kern_v[...], turned)

    def all_rows(k):
        rows = slice(bounds[k], bounds[k + 1])
        half_v[rows, :] = rounded_rows(grad_v[rows, :], bases_v[k], rows_v[rows, :], first_v[rows, :], second_v[rows, :])

    def vector_rows():
        first, second, step = adam_step(vfirst_ref[...], vsecond_ref[...], gvec_ref[0:6, :])
        vfirst_out[...], vsecond_out[...] = first, second
        vec_out[...] = vec_ref[...] - RATE_VECTOR * step

    def beside(b):
        if b < PAIR:
            all_rows(b)
        elif b == PAIR:
            own_rows()
        elif b == PAIR + 2:
            vector_rows()
            for arrived, leaving in passed:
                arrived.wait()
                leaving.start()
            for copy in outs[1:5]:
                copy.start()

    orthogonalize(work_v, bases_new, width, beside)
    outs[5].start()
    for copy in outs + [leaving for _, leaving in passed]:
        copy.wait()


def update_call(grad, stat, bases, kern, kfirst, ksecond, rows, first, second, gvec, vec, vfirst, vsecond, work, *through):
    shard, width = kern.shape
    whole, anywhere = pl.BlockSpec(memory_space=pltpu.VMEM), pl.BlockSpec(memory_space=pl.ANY)

    def like(array):
        return jax.ShapeDtypeStruct(array.shape, array.dtype)

    def held(array):
        return pltpu.VMEM(array.shape, array.dtype)

    pair = jax.ShapeDtypeStruct((PAIR,) + stat.shape[1:], F32)
    four = jax.ShapeDtypeStruct((4 * width, width), BF16)
    loaded = (grad, stat, bases, kern, kfirst, ksecond, rows, first, second)
    return pl.pallas_call(
        update_kernel,
        out_shape=tuple(map(like, through[:4]))
        + (like(kern), like(kern), like(kern), like(vec), like(vec), like(vec), like(stat), like(stat), like(grad)),
        in_specs=[anywhere] * 9 + [whole] * 4 + [anywhere] * 7,
        out_specs=(anywhere,) * 7 + (whole,) * 3 + (anywhere,) * 3,
        scratch_shapes=[held(array) for array in (grad, pair, *loaded[2:])]
        + [pltpu.VMEM((COUNT, 2 * width, width), F32)]
        + [held(array) for array in (kern, kern, kern, pair, stat, four, *through)]
        + [pltpu.SemaphoreType.DMA((10,)), pltpu.SemaphoreType.DMA((6,)), pltpu.SemaphoreType.DMA((2, 6))],
        compiler_params=pltpu.CompilerParams(vmem_limit_bytes=VMEM_LIMIT),
        name="update",
    )(*loaded, gvec, vec, vfirst, vsecond, work, *through)


def on_device(
    edge_latent, node_latent, edge_cot, node_cot, five_flag, senders, send_rows, kernels, kernel_first, kernel_second,
    vectors, vector_first, vector_second, statistics, bases,
):
    samples, nodes, width = node_latent.shape
    slots = senders.shape[0] // nodes
    z = Sizes(samples, nodes, slots, send_rows.shape[1], width)
    edge_out, edge_grad, node_out, node_grad, grad, gvec, rows, first, second, stat_pair, work, half_pair = round_call(
        z,
        lax.axis_size("nodes"),
        edge_latent.reshape(-1, width),
        edge_cot.reshape(-1, width),
        node_latent.reshape(-1, width),
        node_cot.reshape(-1, width),
        five_flag.reshape(1, -1),
        senders.reshape(-1, LANES),
        send_rows,
        kernels,
        kernel_first,
        kernel_second,
        vectors,
        statistics,
        bases,
    )
    edge_out, edge_grad, node_out, node_grad, *rest = update_call(
        grad, statistics, bases, kernels, kernel_first, kernel_second, rows, first, second, gvec,
        vectors, vector_first, vector_second, work, edge_out, edge_grad, node_out, node_grad, stat_pair, half_pair,
    )
    return (
        edge_out.reshape(edge_latent.shape),
        node_out.reshape(node_latent.shape),
        edge_grad.reshape(edge_latent.shape),
        node_grad.reshape(node_latent.shape),
        *rest,
    )


def solution(mesh):
    in_specs = (
        P("fs", "nodes", None),
        P("fs", "nodes", None),
        P("fs", "nodes", None),
        P("fs", "nodes", None),
        P("nodes"),
        P("nodes"),
        P("nodes", None),
        P("fs", None),
        P("fs", None),
        P("fs", None),
        P(),
        P(),
        P(),
        P(),
        P(),
    )
    out_specs = (
        P("fs", "nodes", None),
        P("fs", "nodes", None),
        P("fs", "nodes", None),
        P("fs", "nodes", None),
        P("fs", None),
        P("fs", None),
        P("fs", None),
        P(),
        P(),
        P(),
        P(),
        P(),
        P(),
    )
    return jax.shard_map(
        on_device, mesh=mesh, in_specs=in_specs, out_specs=out_specs, check_vma=False
    )
```

time: 83.1 us -> 72.3 us (0.87)
  Pallas kernels: 80.7 us -> 70.5 us
  local copies, waits for them, and re-layouts: 1.29 us -> 0 us
    pallas_call x1, Pallas kernels: 59.1 us -> 51.9 us  [round_call(): pl.pallas_call(partial(round_kernel, z, tuple(scratch), count), out_shape...]
    pallas_call x1, Pallas kernels: 21.6 us -> 18.6 us  [update_call(): pl.pallas_call(update_kernel, out_shape=tuple(map(like, through[:4])) + (...]
    reshape x1 -> x0, local copies, waits for them, and re-layouts: 1.29 us -> none  [on_device(): senders.reshape(1, -1)]
where the time goes in v5:
time: 72.3 us; the launch traced here: 71.3 us
  Pallas kernels  70.5 us (98%)
  between operations  0.84 us (1%)
    pallas_call x1, Pallas kernels, round_call(): pl.pallas_call(partial(round_kernel, z, tuple(scratch), count), out_shape...  51.9 us
    pallas_call x1, Pallas kernels, update_call(): pl.pallas_call(update_kernel, out_shape=tuple(map(like, through[:4])) + (...  18.6 us

profile of v5, /device:TPU:0, one launch (start us, length us, event | category | flops | bytes accessed | tf_op | source)
XLA Modules:
  0.0 71.3 jit_solution(2666280623145644390)
XLA Ops:
  0.6 51.9 %edge_node_round.1 = (bf16[6144,256]{1,0:T(8,128)(2,1)}, bf16[6144,256]{1,0:T(8,128)(2,1)}, bf16[1024,256]{1,0:T(8,128)(2,1)}, bf16[1024,256]{1,0:T(8,128)(2,1)}...) custom-call(bf16[6144,256]{1,0:T(8,128)(2,1)} %bitcast.10, ...), custom_call_target="tpu_custom_call" | custom-call | tf_op jit(solution)/shard_map/edge_node_round/pallas_call | solution.py:994
  52.5 18.6 %update.1 = (bf16[6144,256]{1,0:T(8,128)(2,1)}, bf16[6144,256]{1,0:T(8,128)(2,1)}, bf16[1024,256]{1,0:T(8,128)(2,1)}, bf16[1024,256]{1,0:T(8,128)(2,1)}, f32[448...) custom-call(bf16[1792,256]{1,0:T(8,128)(2,1)} %get-tuple-element.38., ...), custom_call_target="tpu_custom_call" | custom-call | tf_op jit(solution)/shard_map/update/pallas_call | solution.py:1126

commit v6 on v5

--- a/solution.py
+++ b/solution.py
@@ -126,8 +126,13 @@
         snew_v=pltpu.VMEM((PAIR, width, width), F32),
         work_v=pltpu.VMEM((PAIR, 2 * width, width), F32),
         hnew_v=pltpu.VMEM((3 * width, width), BF16),
-        local_sem=pltpu.SemaphoreType.DMA((7,)),
-        out_sem=pltpu.SemaphoreType.DMA((10,)),
+        list_ids=pltpu.VMEM((2, z.halo), jnp.int32),
+        five_v=pltpu.VMEM((1, z.nodes), jnp.int32),
+        send_ids=pltpu.VMEM((z.edges // LANES, LANES), jnp.int32),
+        vec_v=pltpu.VMEM((6, width), F32),
+        gvec_v=pltpu.VMEM((8, width), F32),
+        local_sem=pltpu.SemaphoreType.DMA((11,)),
+        out_sem=pltpu.SemaphoreType.DMA((11,)),
         rows_sem=pltpu.SemaphoreType.DMA((2, 12)),
         first_sem=pltpu.SemaphoreType.DMA((2, 3)),
         second_sem=pltpu.SemaphoreType.DMA((2, 3)),
@@ -521,7 +526,9 @@
     for b in range(blocks):
         beside(b)
         lanes, after = lanes_of(b), (b + 1) * BLOCK
-        high, low = split(factor_block(packed).astype(F32))
+        high, low = split(factor_block(packed))
+        whole_high = high.astype(F32)
+        next_high, next_low = pltpu.roll(whole_high, BLOCK, 1), pltpu.roll(low.astype(F32), 2 * BLOCK, 1)
         high, low = placed([high] * COUNT, b), placed([low] * COUNT, b)
         if b < blocks - 1:
             spread_high, spread_low = jnp.concatenate(high, 0), jnp.concatenate(low, 0)
@@ -534,10 +541,18 @@
             packed = sum(current) - sum(update[rows_of(k), :] for k in range(COUNT))
         start = after // LANES * LANES
         for k in range(COUNT):
-            four_high = jnp.concatenate([high[k]] * HALF, 0)
-            four_low = jnp.concatenate([low[k]] * HALF, 0)
-            below = wide_left(work_v[k, after:, lanes])
-            turned = dot_nt(below, jnp.concatenate([four_high, four_low, four_high], 1))
+            below = work_v[k, after:, lanes]
+            place = (iota(below.shape, 1) // BLOCK - b - k) & (HALF - 1)
+            below = jnp.where(
+                place == 1, pltpu.roll(below, BLOCK, 1), jnp.where(place == 2, pltpu.roll(below, 2 * BLOCK, 1), below)
+            )
+            below_high, below_low = split(below)
+            below = jnp.where(place == 1, below_low, below_high)
+            place = (group - b - k) & (HALF - 1)
+            factor = jnp.where(
+                place == 0, whole_high, jnp.where(place == 1, next_high, jnp.where(place == 2, next_low, 0.0))
+            ).astype(BF16)
+            turned = dot_nt(below, jnp.concatenate([factor] * HALF, 0))
             mine = iota((width, LANES), 1) // BLOCK == b % HALF
             bases_out[k, :, lanes] = jnp.where(mine, turned[width - after :, :], bases_out[k, :, lanes])
             if b == blocks - 1:
@@ -601,8 +616,8 @@
 
 
 def round_kernel(
-    z, names, count, edge_ref, cot_ref, node_hbm, ncot_ref, five_ref, send_ref, list_ref, kern_ref, kfirst_ref, ksecond_ref,
-    vec_ref, stat_ref, bases_ref, eout_ref, egrad_ref, nout_hbm, ngrad_hbm, grad_ref, gvec_ref, rows_ref, first_ref, second_ref,
+    z, names, count, edge_ref, cot_ref, node_hbm, ncot_ref, five_hbm, send_hbm, list_hbm, kern_ref, kfirst_ref, ksecond_ref,
+    vec_hbm, stat_ref, bases_ref, eout_ref, egrad_ref, nout_hbm, ngrad_hbm, grad_ref, gvec_hbm, rows_ref, first_ref, second_ref,
     stat_hbm, work_hbm, half_hbm, *scratch,
 ):
     m = type("Held", (), {})()
@@ -627,13 +642,15 @@
         pltpu.make_async_copy(source, target, m.local_sem.at[i])
         for i, (source, target) in enumerate(
             [
-                (kern_ref, m.slope_v.at[staged[0]]), (node_hbm, m.node_v), (kfirst_ref, m.slope_v.at[staged[1]]),
+                (kern_ref, m.slope_v.at[staged[0]]), (node_hbm, m.node_v), (list_hbm, m.list_ids), (five_hbm, m.five_v),
+                (send_hbm, m.send_ids), (vec_hbm, m.vec_v), (kfirst_ref, m.slope_v.at[staged[1]]),
                 (ksecond_ref, m.slope_v.at[staged[2]]), (ncot_ref, m.ncot_v),
                 (stat_ref.at[pl.ds(PAIR, PAIR)], m.stat_v), (bases_ref.at[pl.ds(PAIR, PAIR)], m.bases_v),
             ]
         )
     ]
     node_ref, nout_ref, ngrad_ref = m.node_v, m.nout_v, m.ngrad_v
+    list_ref, five_ref, send_ref, vec_ref = m.list_ids, m.five_v, m.send_ids, m.vec_v
     stat_out, work_out, half_out = m.snew_v, m.work_v, m.hnew_v
 
     def start_out(i, source, target):
@@ -644,7 +661,7 @@
     outs = []
     gather = Gather(weight_ref, m.rows_sem, shard, fs, node_id)
     moments = [Gather(m.first_v, m.first_sem, shard, fs, node_id), Gather(m.second_v, m.second_sem, shard, fs, node_id)]
-    for copy in locals_in[:2]:
+    for copy in locals_in[:6]:
         copy.start()
     m.halo_v[...] = jnp.zeros_like(m.halo_v)
     m.ret_v[...] = jnp.zeros_like(m.ret_v)
@@ -658,7 +675,7 @@
     weight_ref[mine, :] = m.slope_v[staged[0], :].astype(BF16)
     all_in()
     gather.start()
-    for copy in locals_in[2:]:
+    for copy in locals_in[6:]:
         copy.start()
     for s in range(samples):
         sample_copy(edge_ref, m.edge_v, m.edge_sem, s).start()
@@ -679,7 +696,8 @@
                 to_side(source, target, sems, 1 - side, other).wait_recv()
             pl.when(exists)(settle)
 
-    locals_in[1].wait()
+    for copy in locals_in[1:6]:
+        copy.wait()
     for side in range(2):
         chosen = list_matrix(list_ref, side, nodes)
         for s in range(samples):
@@ -692,7 +710,7 @@
     gather.finish()
     finish_sides(m.list_v, m.halo_v, m.halo_sem)
     start_out(0, weight_ref, rows_ref)
-    for copy in locals_in[2:]:
+    for copy in locals_in[6:]:
         copy.wait()
     for k, (moment, held) in enumerate(zip(moments, (m.first_v, m.second_v), strict=True)):
         held[mine, :] = m.slope_v[staged[k + 1], :].astype(BF16)
@@ -849,8 +867,9 @@
         rows = aligned(p, z.bwd_rows)
         d_out, d_pre = m.dout_v[pair], m.dpre_v[pair]
         m.gmat_v[3 * width : 4 * width, :] += dot_tn(m.act_v[rows, :], d_out)
-        m.gmat_v[0:width, :] += dot_tn(m.edge_v[rows, :], d_pre)
-        sums = dot_nn(m.scat_v[c], d_pre)
+        sums = dot_nn(jnp.concatenate([m.edge_v[rows, :].T, m.scat_v[c]], 0), d_pre)
+        m.gmat_v[0:width, :] += sums[0:width, :]
+        sums = sums[width:, :]
         m.aown_v[aligned(s, nodes), :] += sums[0:nodes, :]
         m.ahalo_v[aligned(s, two_halo), :] += sums[nodes : nodes + two_halo, :]
         m.recv_v[aligned(p, z.bwd_nodes), :] = sums[nodes + two_halo :, :]
@@ -947,7 +966,8 @@
         ).astype(BF16)
     start_out(2, ngrad_ref, ngrad_hbm)
     reduce.settle()
-    gvec_ref[...] = vectors.settle()
+    m.gvec_v[...] = vectors.settle()
+    start_out(10, m.gvec_v, gvec_hbm)
     nodes_sum.arrive()
     bounds = matrix_bounds(width)
     for k in range(PAIR):
@@ -987,7 +1007,6 @@
     cube = Cube(count)
     spare = Reduce.scratch(cube, 4 * width, width) + Reduce.scratch(cube, 3 * width, width) + VectorSum.scratch(cube, (8, width))
     rows, per_node = z.samples * z.edges, z.samples * z.nodes
-    whole = pl.BlockSpec(memory_space=pltpu.VMEM)
     anywhere = pl.BlockSpec(memory_space=pl.ANY)
     total = jax.ShapeDtypeStruct((7 * width, width), BF16)
     moments = jax.ShapeDtypeStruct((4 * width, width), BF16)
@@ -1005,8 +1024,8 @@
             jax.ShapeDtypeStruct((PAIR, 2 * width, width), F32),
             jax.ShapeDtypeStruct((3 * width, width), BF16),
         ),
-        in_specs=[anywhere] * 4 + [whole] * 3 + [anywhere] * 3 + [whole] + [anywhere] * 2,
-        out_specs=(anywhere,) * 5 + (whole,) + (anywhere,) * 6,
+        in_specs=[anywhere] * 13,
+        out_specs=(anywhere,) * 12,
         scratch_shapes=list(scratch.values()) + spare,
         compiler_params=pltpu.CompilerParams(
             collective_id=0, has_side_effects=True, vmem_limit_bytes=VMEM_LIMIT
@@ -1017,11 +1036,12 @@
 
 def update_kernel(
     grad_ref, stat_ref, bases_ref, kern_ref, kfirst_ref, ksecond_ref, rows_ref, first_ref, second_ref,
-    gvec_ref, vec_ref, vfirst_ref, vsecond_ref, work_ref, eout_ref, egrad_ref, nout_ref, ngrad_ref, spair_ref, hpair_ref,
-    eout_out, egrad_out, nout_out, ngrad_out, kern_out, kfirst_out, ksecond_out, vec_out, vfirst_out, vsecond_out,
+    gvec_hbm, vec_hbm, vfirst_hbm, vsecond_hbm, work_ref, eout_ref, egrad_ref, nout_ref, ngrad_ref, spair_ref, hpair_ref,
+    eout_out, egrad_out, nout_out, ngrad_out, kern_out, kfirst_out, ksecond_out, vec_hout, vfirst_hout, vsecond_hout,
     stat_out, bases_out, half_out,
     grad_v, stat_v, bases_v, kern_v, kfirst_v, ksecond_v, rows_v, first_v, second_v,
-    work_v, kern_new, kfirst_new, ksecond_new, stat_new, bases_new, half_v, eout_v, egrad_v, nout_v, ngrad_v, spair_v, hpair_v, in_sem, out_sem, pass_sem,
+    work_v, kern_new, kfirst_new, ksecond_new, stat_new, bases_new, half_v, eout_v, egrad_v, nout_v, ngrad_v, spair_v, hpair_v, gvec_ref, vec_ref, vfirst_ref, vsecond_ref,
+    vec_out, vfirst_out, vsecond_out, in_sem, out_sem, pass_sem,
 ):
     shard, width = kern_v.shape
     copies = [
@@ -1031,6 +1051,7 @@
                 (bases_ref, bases_v), (stat_ref.at[pl.ds(0, PAIR)], stat_v), (grad_ref, grad_v),
                 (work_ref, work_v.at[pl.ds(PAIR, PAIR)]), (kern_ref, kern_v), (kfirst_ref, kfirst_v),
                 (ksecond_ref, ksecond_v), (rows_ref, rows_v), (first_ref, first_v), (second_ref, second_v),
+                (gvec_hbm, gvec_ref), (vec_hbm, vec_ref), (vfirst_hbm, vfirst_ref), (vsecond_hbm, vsecond_ref),
             ]
         )
     ]
@@ -1050,7 +1071,8 @@
         for i, (source, target) in enumerate(
             [
                 (stat_new, stat_out.at[pl.ds(0, PAIR)]), (kern_new, kern_out), (kfirst_new, kfirst_out), (ksecond_new, ksecond_out),
-                (half_v, half_out.at[pl.ds(0, 4 * width)]), (bases_new, bases_out),
+                (half_v, half_out.at[pl.ds(0, 4 * width)]), (vec_out, vec_hout), (vfirst_out, vfirst_hout),
+                (vsecond_out, vsecond_hout), (bases_new, bases_out),
             ]
         )
     ]
@@ -1101,18 +1123,18 @@
             for arrived, leaving in passed:
                 arrived.wait()
                 leaving.start()
-            for copy in outs[1:5]:
+            for copy in outs[1:8]:
                 copy.start()
 
     orthogonalize(work_v, bases_new, width, beside)
-    outs[5].start()
+    outs[8].start()
     for copy in outs + [leaving for _, leaving in passed]:
         copy.wait()
 
 
 def update_call(grad, stat, bases, kern, kfirst, ksecond, rows, first, second, gvec, vec, vfirst, vsecond, work, *through):
     shard, width = kern.shape
-    whole, anywhere = pl.BlockSpec(memory_space=pltpu.VMEM), pl.BlockSpec(memory_space=pl.ANY)
+    anywhere = pl.BlockSpec(memory_space=pl.ANY)
 
     def like(array):
         return jax.ShapeDtypeStruct(array.shape, array.dtype)
@@ -1127,12 +1149,12 @@
         update_kernel,
         out_shape=tuple(map(like, through[:4]))
         + (like(kern), like(kern), like(kern), like(vec), like(vec), like(vec), like(stat), like(stat), like(grad)),
-        in_specs=[anywhere] * 9 + [whole] * 4 + [anywhere] * 7,
-        out_specs=(anywhere,) * 7 + (whole,) * 3 + (anywhere,) * 3,
+        in_specs=[anywhere] * 20,
+        out_specs=(anywhere,) * 13,
         scratch_shapes=[held(array) for array in (grad, pair, *loaded[2:])]
         + [pltpu.VMEM((COUNT, 2 * width, width), F32)]
-        + [held(array) for array in (kern, kern, kern, pair, stat, four, *through)]
-        + [pltpu.SemaphoreType.DMA((10,)), pltpu.SemaphoreType.DMA((6,)), pltpu.SemaphoreType.DMA((2, 6))],
+        + [held(array) for array in (kern, kern, kern, pair, stat, four, *through, gvec, vec, vec, vec, vec, vec, vec)]
+        + [pltpu.SemaphoreType.DMA((14,)), pltpu.SemaphoreType.DMA((9,)), pltpu.SemaphoreType.DMA((2, 6))],
         compiler_params=pltpu.CompilerParams(vmem_limit_bytes=VMEM_LIMIT),
         name="update",
     )(*loaded, gvec, vec, vfirst, vsecond, work, *through)

time: 72.3 us -> 68.1 us (0.942)
  Pallas kernels: 70.5 us -> 66.5 us
    pallas_call x1, Pallas kernels: 18.6 us -> 16.3 us  [update_call(): pl.pallas_call(update_kernel, out_shape=tuple(map(like, through[:4])) + (...]
    pallas_call x1, Pallas kernels: 51.9 us -> 50.1 us  [round_call(): pl.pallas_call(partial(round_kernel, z, tuple(scratch), count), out_shape...]
where the time goes in v6:
time: 68.1 us; the launch traced here: 67.3 us
  Pallas kernels  66.5 us (98%)
  between operations  0.82 us (1%)
    pallas_call x1, Pallas kernels, round_call(): pl.pallas_call(partial(round_kernel, z, tuple(scratch), count), out_shape...  50.1 us
    pallas_call x1, Pallas kernels, update_call(): pl.pallas_call(update_kernel, out_shape=tuple(map(like, through[:4])) + (...  16.3 us

profile of v6, /device:TPU:0, one launch (start us, length us, event | category | flops | bytes accessed | tf_op | source)
XLA Modules:
  0.0 67.3 jit_solution(16647204022544900255)
XLA Ops:
  0.6 50.1 %edge_node_round.1 = (bf16[6144,256]{1,0:T(8,128)(2,1)}, bf16[6144,256]{1,0:T(8,128)(2,1)}, bf16[1024,256]{1,0:T(8,128)(2,1)}, bf16[1024,256]{1,0:T(8,128)(2,1)}...) custom-call(bf16[6144,256]{1,0:T(8,128)(2,1)} %bitcast.10, ...), custom_call_target="tpu_custom_call" | custom-call | tf_op jit(solution)/shard_map/edge_node_round/pallas_call | solution.py:1013
  50.8 16.3 %update.1 = (bf16[6144,256]{1,0:T(8,128)(2,1)}, bf16[6144,256]{1,0:T(8,128)(2,1)}, bf16[1024,256]{1,0:T(8,128)(2,1)}, bf16[1024,256]{1,0:T(8,128)(2,1)}, f32[448...) custom-call(bf16[1792,256]{1,0:T(8,128)(2,1)} %get-tuple-element.38., ...), custom_call_target="tpu_custom_call" | custom-call | tf_op jit(solution)/shard_map/update/pallas_call | solution.py:1148

commit v7 on v6

--- a/solution.py
+++ b/solution.py
@@ -898,6 +898,7 @@
     lax.fori_loop(0, 1, backward, 0)
     nodes_sum.spread()
     lax.fori_loop(1, samples, backward, 0)
+    nodes_sum.meet()
     activate_back(last, 1, 1)
     weights_back(pairs - 1, 1)
 
@@ -921,7 +922,6 @@
     reduce = Reduce(cube, 0, 4 * width, m.gmat_v, m.gout_v, spare[:7])
     vectors = VectorSum(cube, *spare[14:])
     reduce.begin()
-    nodes_sum.meet()
     border = (dot_nt(out_high, send_full) + dot_nt(out_low, send_full)).astype(BF16)
     for s in range(samples):
         for side in range(2):
@@ -942,10 +942,10 @@
     vectors.spread()
     for moment in moments:
         moment.forward()
+    nodes_sum.settle()
     for s in range(samples):
         sample_copy(m.edge_out_v, eout_ref, m.eout_sem, s).wait()
     lax.fori_loop(0, samples, edge_gradient, 0)
-    nodes_sum.settle()
     for s in range(samples):
         rows = slice(s * nodes, (s + 1) * nodes)
         recv_high, recv_low = split(m.recv_v[rows, :])
@@ -1085,12 +1085,12 @@
     for k in range(PAIR):
         stat_new[k] = new_statistics(grad_v[bounds[k] : bounds[k + 1], :], stat_v[k])
     outs[0].start()
+    for k in range(PAIR):
+        work_v[k, 0:width, :], work_v[k, width:, :] = prepare_bases(stat_new[k], bases_v[k], k)
     for copy in copies[3:]:
         copy.wait()
     for copy, _ in passed:
         copy.start()
-    for k in range(PAIR):
-        work_v[k, 0:width, :], work_v[k, width:, :] = prepare_bases(stat_new[k], bases_v[k], k)
 
     def own_rows():
         first_row = lax.axis_index("fs") * shard

time: 68.1 us -> 66.9 us (0.982)
  Pallas kernels: 66.5 us -> 65.3 us
    pallas_call x1, Pallas kernels: 16.3 us -> 15.4 us  [update_call(): pl.pallas_call(update_kernel, out_shape=tuple(map(like, through[:4])) + (...]
where the time goes in v7:
time: 66.9 us; the launch traced here: 66.1 us
  Pallas kernels  65.3 us (98%)
  between operations  0.82 us (1%)
    pallas_call x1, Pallas kernels, round_call(): pl.pallas_call(partial(round_kernel, z, tuple(scratch), count), out_shape...  49.9 us
    pallas_call x1, Pallas kernels, update_call(): pl.pallas_call(update_kernel, out_shape=tuple(map(like, through[:4])) + (...  15.4 us

profile of v7, /device:TPU:0, one launch (start us, length us, event | category | flops | bytes accessed | tf_op | source)
XLA Modules:
  0.0 66.1 jit_solution(3066486478005680326)
XLA Ops:
  0.6 49.9 %edge_node_round.1 = (bf16[6144,256]{1,0:T(8,128)(2,1)}, bf16[6144,256]{1,0:T(8,128)(2,1)}, bf16[1024,256]{1,0:T(8,128)(2,1)}, bf16[1024,256]{1,0:T(8,128)(2,1)}...) custom-call(bf16[6144,256]{1,0:T(8,128)(2,1)} %bitcast.10, ...), custom_call_target="tpu_custom_call" | custom-call | tf_op jit(solution)/shard_map/edge_node_round/pallas_call | solution.py:1013
  50.5 15.4 %update.1 = (bf16[6144,256]{1,0:T(8,128)(2,1)}, bf16[6144,256]{1,0:T(8,128)(2,1)}, bf16[1024,256]{1,0:T(8,128)(2,1)}, bf16[1024,256]{1,0:T(8,128)(2,1)}, f32[448...) custom-call(bf16[1792,256]{1,0:T(8,128)(2,1)} %get-tuple-element.38., ...), custom_call_target="tpu_custom_call" | custom-call | tf_op jit(solution)/shard_map/update/pallas_call | solution.py:1148

commit v8 on v7

--- a/solution.py
+++ b/solution.py
@@ -560,8 +560,11 @@
             turned_high, turned_low = split(turned)
             part = iota(turned.shape, 1) // BLOCK
             zero = jnp.zeros_like(turned_high)
-            left = jnp.where(part == 2, turned_low, jnp.where(part == 3, zero, turned_high))
-            right = jnp.where(part == 1, turned_low, jnp.where(part == 3, zero, turned_high))
+            left = jnp.where(part == 2, turned_low, turned_high)
+            rest = width - after
+            right = jnp.where(
+                part[0:rest] == 1, turned_low[0:rest], jnp.where(part[0:rest] == 3, zero[0:rest], turned_high[0:rest])
+            )
             right = jnp.concatenate(
                 [
                     right[(i - b - 1) * BLOCK : (i - b) * BLOCK, :] if i > b else zero[0:BLOCK, :]
@@ -584,10 +587,9 @@
     return sum((row >= bound).astype(jnp.int32) for bound in matrix_bounds(width)[1:-1])
 
 
-def prepare_bases(stat, basis, k):
+def prepare_bases(stat, flipped, k):
     width = stat.shape[-1]
     order = turned_blocks(k, width)
-    flipped = basis.T
     proj_rows = dot_three(flipped, stat)
     gram = dot_three(proj_rows, pick_rows(proj_rows, order))
     return gram, dot_three(stat, pick_rows(flipped, order))
@@ -706,6 +708,12 @@
             ).astype(BF16)
     start_sides(m.list_v, m.halo_v, m.halo_sem)
     build_selectors(z, m, five_ref, send_ref)
+    m.gmat_v[...] = jnp.zeros_like(m.gmat_v)
+    m.vsum_v[...] = jnp.zeros_like(m.vsum_v)
+    m.aown_v[...] = jnp.zeros_like(m.aown_v)
+    m.ahalo_v[...] = jnp.zeros_like(m.ahalo_v)
+    m.dout_v[1] = jnp.zeros_like(m.dout_v[1])
+    m.dpre_v[1] = jnp.zeros_like(m.dpre_v[1])
     gather.forward()
     gather.finish()
     finish_sides(m.list_v, m.halo_v, m.halo_sem)
@@ -716,10 +724,6 @@
         held[mine, :] = m.slope_v[staged[k + 1], :].astype(BF16)
         moment.start()
     m.half_v[...] = weight_ref[...] * jnp.asarray(0.5, BF16)
-    m.gmat_v[...] = jnp.zeros_like(m.gmat_v)
-    m.vsum_v[...] = jnp.zeros_like(m.vsum_v)
-    m.aown_v[...] = jnp.zeros_like(m.aown_v)
-    m.ahalo_v[...] = jnp.zeros_like(m.ahalo_v)
     for s in range(samples):
         for side in range(2):
             m.table_v[s * two_halo + side * halo : s * two_halo + (side + 1) * halo, :] = m.halo_v[
@@ -874,8 +878,6 @@
         m.ahalo_v[aligned(s, two_halo), :] += sums[nodes : nodes + two_halo, :]
         m.recv_v[aligned(p, z.bwd_nodes), :] = sums[nodes + two_halo :, :]
 
-    m.dout_v[1] = jnp.zeros_like(m.dout_v[1])
-    m.dpre_v[1] = jnp.zeros_like(m.dpre_v[1])
     spread_back(0, 0)
 
     def backward(s, carry):
@@ -975,7 +977,7 @@
     start_out(5, m.gout_v.at[pl.ds(4 * width, 3 * width)], grad_ref.at[pl.ds(4 * width, 3 * width)])
     start_out(6, stat_out, stat_hbm)
     for k in range(PAIR):
-        work_out[k, 0:width, :], work_out[k, width:, :] = prepare_bases(stat_out[k], m.bases_v[k], PAIR + k)
+        work_out[k, 0:width, :], work_out[k, width:, :] = prepare_bases(stat_out[k], m.bases_v[k].T, PAIR + k)
     start_out(7, work_out, work_hbm)
     for moment in moments:
         moment.finish()
@@ -1072,21 +1074,24 @@
             [
                 (stat_new, stat_out.at[pl.ds(0, PAIR)]), (kern_new, kern_out), (kfirst_new, kfirst_out), (ksecond_new, ksecond_out),
                 (half_v, half_out.at[pl.ds(0, 4 * width)]), (vec_out, vec_hout), (vfirst_out, vfirst_hout),
-                (vsecond_out, vsecond_hout), (bases_new, bases_out),
+                (vsecond_out, vsecond_hout), (bases_new.at[:, :, pl.ds(0, LANES)], bases_out.at[:, :, pl.ds(0, LANES)]),
+                (bases_new.at[:, :, pl.ds(LANES, width - LANES)], bases_out.at[:, :, pl.ds(LANES, width - LANES)]),
             ]
         )
     ]
     for copy in copies:
         copy.start()
     bases_new[...] = jnp.zeros_like(bases_new)
-    for copy in copies[:3]:
+    copies[0].wait()
+    flipped = [bases_v[k].T for k in range(PAIR)]
+    for copy in copies[1:3]:
         copy.wait()
     bounds = matrix_bounds(width)
     for k in range(PAIR):
         stat_new[k] = new_statistics(grad_v[bounds[k] : bounds[k + 1], :], stat_v[k])
     outs[0].start()
     for k in range(PAIR):
-        work_v[k, 0:width, :], work_v[k, width:, :] = prepare_bases(stat_new[k], bases_v[k], k)
+        work_v[k, 0:width, :], work_v[k, width:, :] = prepare_bases(stat_new[k], flipped[k], k)
     for copy in copies[3:]:
         copy.wait()
     for copy, _ in passed:
@@ -1114,20 +1119,23 @@
         vec_out[...] = vec_ref[...] - RATE_VECTOR * step
 
     def beside(b):
-        if b < PAIR:
-            all_rows(b)
-        elif b == PAIR:
+        if b == 0:
+            all_rows(0)
+        if b == 1:
+            all_rows(1)
+        if b == 4:
             own_rows()
-        elif b == PAIR + 2:
+        if b == 3:
             vector_rows()
             for arrived, leaving in passed:
                 arrived.wait()
                 leaving.start()
-            for copy in outs[1:8]:
+        if b == 5:
+            for copy in outs[1:9]:
                 copy.start()
 
     orthogonalize(work_v, bases_new, width, beside)
-    outs[8].start()
+    outs[9].start()
     for copy in outs + [leaving for _, leaving in passed]:
         copy.wait()
 
@@ -1154,7 +1162,7 @@
         scratch_shapes=[held(array) for array in (grad, pair, *loaded[2:])]
         + [pltpu.VMEM((COUNT, 2 * width, width), F32)]
         + [held(array) for array in (kern, kern, kern, pair, stat, four, *through, gvec, vec, vec, vec, vec, vec, vec)]
-        + [pltpu.SemaphoreType.DMA((14,)), pltpu.SemaphoreType.DMA((9,)), pltpu.SemaphoreType.DMA((2, 6))],
+        + [pltpu.SemaphoreType.DMA((14,)), pltpu.SemaphoreType.DMA((10,)), pltpu.SemaphoreType.DMA((2, 6))],
         compiler_params=pltpu.CompilerParams(vmem_limit_bytes=VMEM_LIMIT),
         name="update",
     )(*loaded, gvec, vec, vfirst, vsecond, work, *through)

time: 66.9 us -> 65.4 us (0.978)
  Pallas kernels: 65.3 us -> 63.8 us
    pallas_call x1, Pallas kernels: 15.4 us -> 14.1 us  [update_call(): pl.pallas_call(update_kernel, out_shape=tuple(map(like, through[:4])) + (...]
where the time goes in v8:
time: 65.4 us; the launch traced here: 64.6 us
  Pallas kernels  63.8 us (98%)
  between operations  0.82 us (1%)
    pallas_call x1, Pallas kernels, round_call(): pl.pallas_call(partial(round_kernel, z, tuple(scratch), count), out_shape...  49.7 us
    pallas_call x1, Pallas kernels, update_call(): pl.pallas_call(update_kernel, out_shape=tuple(map(like, through[:4])) + (...  14.1 us

profile of v8, /device:TPU:0, one launch (start us, length us, event | category | flops | bytes accessed | tf_op | source)
XLA Modules:
  0.0 64.6 jit_solution(5562054063492680167)
XLA Ops:
  0.6 49.7 %edge_node_round.1 = (bf16[6144,256]{1,0:T(8,128)(2,1)}, bf16[6144,256]{1,0:T(8,128)(2,1)}, bf16[1024,256]{1,0:T(8,128)(2,1)}, bf16[1024,256]{1,0:T(8,128)(2,1)}...) custom-call(bf16[6144,256]{1,0:T(8,128)(2,1)} %bitcast.10, ...), custom_call_target="tpu_custom_call" | custom-call | tf_op jit(solution)/shard_map/edge_node_round/pallas_call | solution.py:1015
  50.3 14.1 %update.1 = (bf16[6144,256]{1,0:T(8,128)(2,1)}, bf16[6144,256]{1,0:T(8,128)(2,1)}, bf16[1024,256]{1,0:T(8,128)(2,1)}, bf16[1024,256]{1,0:T(8,128)(2,1)}, f32[448...) custom-call(bf16[1792,256]{1,0:T(8,128)(2,1)} %get-tuple-element.38., ...), custom_call_target="tpu_custom_call" | custom-call | tf_op jit(solution)/shard_map/update/pallas_call | solution.py:1156
